TPU v7x, 32 devices: a whole 2x2x4 slice. The times are simulated.
32 devices in a mesh: fsdp: 8 (over y, x, core), dp: 4 (over z).
Axes of the slice: x: 2, y: 2, z: 4, core: 2. Of those that a mesh axis runs over, the one named last changes fastest.
Arguments:
- enc_input: bfloat16 [32768, 1024], P(('fsdp', 'dp')), may hold values from -6 to 6
- dec_input: bfloat16 [8192, 1024], P(('fsdp', 'dp')), may hold values from -6 to 6
- enc_cot: bfloat16 [32768, 1024], P(('fsdp', 'dp')), may hold values from -6 to 6
- dec_cot: bfloat16 [8192, 1024], P(('fsdp', 'dp')), may hold values from -6 to 6
- enc_qkv: bfloat16 [1024, 3072], P('fsdp'), may hold values from -0.1875 to 0.1875
- enc_attn_out: bfloat16 [1024, 1024], P('fsdp'), may hold values from -0.75 to 0.75
- enc_ffn_in: bfloat16 [1024, 4096], P('fsdp'), may hold values from -0.1875 to 0.1875
- enc_ffn_out: bfloat16 [4096, 1024], P('fsdp'), may hold values from -0.09375 to 0.09375
- dec_self_qkv: bfloat16 [1024, 3072], P('fsdp'), may hold values from -0.1875 to 0.1875
- dec_self_out: bfloat16 [1024, 1024], P('fsdp'), may hold values from -0.75 to 0.75
- dec_cross_q: bfloat16 [1024, 1024], P('fsdp'), may hold values from -0.1875 to 0.1875
- dec_cross_kv: bfloat16 [1024, 2048], P('fsdp'), may hold values from -0.1875 to 0.1875
- dec_cross_out: bfloat16 [1024, 1024], P('fsdp'), may hold values from -0.75 to 0.75
- dec_ffn_in: bfloat16 [1024, 4096], P('fsdp'), may hold values from -0.1875 to 0.1875
- dec_ffn_out: bfloat16 [4096, 1024], P('fsdp'), may hold values from -0.09375 to 0.09375
- norm_gains: float32 [5, 1024], replicated, may hold values from 0.25 to 1.75
- enc_down: float32 [1024, 512], replicated, may hold values from -0.1875 to 0.1875
- enc_up: float32 [512, 1024], replicated, may hold values from -0.0625 to 0.0625
- dec_down: float32 [1024, 512], replicated, may hold values from -0.1875 to 0.1875
- dec_up: float32 [512, 1024], replicated, may hold values from -0.0625 to 0.0625
- enc_lengths: int32 [32], P(('fsdp', 'dp')), may hold values from 256 to 1024, as said below
- dec_lengths: int32 [32], P(('fsdp', 'dp')), may hold values from 64 to 256, as said below
Outputs:
- enc_out: bfloat16 [32768, 1024], P(('fsdp', 'dp'))
- dec_out: bfloat16 [8192, 1024], P(('fsdp', 'dp'))
- enc_input_grad: float32 [32768, 1024], P(('fsdp', 'dp'))
- dec_input_grad: float32 [8192, 1024], P(('fsdp', 'dp'))
- enc_down_grad: float32 [1024, 512], replicated
- enc_up_grad: float32 [512, 1024], replicated
- dec_down_grad: float32 [1024, 512], replicated
- dec_up_grad: float32 [512, 1024], replicated
- rms: float32 [7], replicated
Inputs may be any that keep to these rules, and one draw needn't show every extreme that they name: `enc_lengths`: one sequence of every draw has all 1024 encoder positions valid. `dec_lengths`: one sequence of every draw has all 256 decoder positions valid.
All inputs are finite; a program needn't handle non-finite values.
Results may differ from a plain program's by a relative error of at most 0.015.
Values may be sent and summed in bfloat16 or wider, within the bound.
A program may use at most 320 MiB of HBM per device.

v0:
```python
import math

import jax
import jax.numpy as jnp
from jax import lax
from jax.sharding import PartitionSpec as P

HEAD = 64


EPSILON = 1e-05


def product(former, latter):
    return jnp.dot(former, latter, preferred_element_type=jnp.float32)


def times_trans(former, latter):
    return lax.dot_general(
        former, latter, (((1,), (1,)), ((), ())), preferred_element_type=jnp.float32
    )


def trans_times(former, latter):
    return lax.dot_general(
        former, latter, (((0,), (0,)), ((), ())), preferred_element_type=jnp.float32
    )


def gelu_exact(entries):
    return 0.5 * entries * (1.0 + lax.erf(entries * (1.0 / math.sqrt(2.0))))


def silu_smooth(entries):
    return entries * jax.nn.sigmoid(entries)


def local_grad(function, entries, upstream):
    return jax.vjp(function, entries)[1](upstream)[0]


def normalize(entries, gain_row):
    centered = entries - jnp.mean(entries, axis=-1, keepdims=True)
    spread = jnp.mean(centered * centered, axis=-1, keepdims=True)
    return centered * lax.rsqrt(spread + EPSILON) * gain_row


def norm_grad(entries, gain_row, upstream):
    return local_grad(lambda within: normalize(within, gain_row), entries, upstream)


def masked_square(entries, row_mask):
    return jnp.sum(jnp.sum(entries * entries, axis=1) * row_mask)


def masked_scores(query_block, key_heads, offset, key_limit, causal):
    factor = 1.0 / math.sqrt(key_heads.shape[-1])
    scores = (
        jnp.einsum("qhd,khd->hqk", query_block, key_heads, preferred_element_type=jnp.float32)
        * factor
    )
    columns = lax.broadcasted_iota(jnp.int32, (query_block.shape[0], key_heads.shape[0]), 1)
    allowed = columns < key_limit
    if causal:
        row_index = lax.broadcasted_iota(jnp.int32, columns.shape, 0) + offset
        allowed = allowed & (columns <= row_index)
    return jnp.where(allowed[None], scores, -1000000000.0)


def attend_forward(queries, key_rows, value_rows, key_limit, causal):
    length = queries.shape[0]
    block_rows = min(512, length)
    block_count = length // block_rows
    query_heads = queries.reshape(block_count, block_rows, -1, HEAD)
    key_heads = key_rows.reshape(key_rows.shape[0], -1, HEAD)
    value_heads = value_rows.reshape(value_rows.shape[0], -1, HEAD)

    def one_block(packed):
        query_block, offset = packed
        scores = masked_scores(query_block, key_heads, offset, key_limit, causal)
        highest = jnp.max(scores, axis=-1, keepdims=True)
        weights = jnp.exp(scores - highest)
        totals = jnp.sum(weights, axis=-1, keepdims=True)
        probs_low = (weights / totals).astype(jnp.bfloat16)
        mixture = jnp.einsum(
            "hqk,khd->qhd", probs_low, value_heads, preferred_element_type=jnp.float32
        )
        return (mixture, highest + jnp.log(totals))

    offsets = jnp.arange(block_count, dtype=jnp.int32) * block_rows
    mixture, logsum = lax.map(one_block, (query_heads, offsets))
    return (mixture.reshape(length, -1), logsum)


def attend_backward(queries, key_rows, value_rows, logsum, upstream, key_limit, causal):
    length = queries.shape[0]
    block_rows = min(512, length)
    block_count = length // block_rows
    factor = 1.0 / math.sqrt(HEAD)
    query_heads = queries.reshape(block_count, block_rows, -1, HEAD)
    upstream_heads = upstream.reshape(block_count, block_rows, -1, HEAD)
    key_heads = key_rows.reshape(key_rows.shape[0], -1, HEAD)
    value_heads = value_rows.reshape(value_rows.shape[0], -1, HEAD)

    def one_block(totals_in, packed):
        key_total, value_total = totals_in
        query_block, upstream_block, logsum_block, offset = packed
        scores = masked_scores(query_block, key_heads, offset, key_limit, causal)
        probs = jnp.exp(scores - logsum_block)
        probs_grad = jnp.einsum(
            "qhd,khd->hqk", upstream_block, value_heads, preferred_element_type=jnp.float32
        )
        row_inner = jnp.sum(probs * probs_grad, axis=-1, keepdims=True)
        scores_grad = (probs * (probs_grad - row_inner)).astype(jnp.bfloat16)
        query_grad = (
            jnp.einsum("hqk,khd->qhd", scores_grad, key_heads, preferred_element_type=jnp.float32)
            * factor
        )
        key_total = (
            key_total
            + jnp.einsum(
                "hqk,qhd->khd", scores_grad, query_block, preferred_element_type=jnp.float32
            )
            * factor
        )
        value_total = value_total + jnp.einsum(
            "hqk,qhd->khd",
            probs.astype(jnp.bfloat16),
            upstream_block,
            preferred_element_type=jnp.float32,
        )
        return ((key_total, value_total), query_grad)

    offsets = jnp.arange(block_count, dtype=jnp.int32) * block_rows
    zeroed = jnp.zeros(key_heads.shape, jnp.float32)
    (key_total, value_total), query_grad = lax.scan(
        one_block, (zeroed, zeroed), (query_heads, upstream_heads, logsum, offsets)
    )
    key_count = key_rows.shape[0]
    return (
        query_grad.reshape(length, -1),
        key_total.reshape(key_count, -1),
        value_total.reshape(key_count, -1),
    )


def branch_forward(hidden, w_in, w_back, down_low, up_low):
    hidden_low = hidden.astype(jnp.bfloat16)
    pre_ffn = product(hidden_low, w_in)
    act_ffn = gelu_exact(pre_ffn).astype(jnp.bfloat16)
    ffn_result = product(act_ffn, w_back)
    pre_adapter = product(hidden_low, down_low)
    act_adapter = silu_smooth(pre_adapter).astype(jnp.bfloat16)
    adapted = product(act_adapter, up_low)
    return (ffn_result + 4.0 * adapted, (hidden_low, pre_ffn, pre_adapter, act_adapter))


def branch_backward(upstream, saved, w_in, w_back, down_low, up_low):
    hidden_low, pre_ffn, pre_adapter, act_adapter = saved
    grad_ffn = upstream.astype(jnp.bfloat16)
    grad_adapted = (4.0 * upstream).astype(jnp.bfloat16)
    grad_act = times_trans(grad_ffn, w_back)
    grad_pre = local_grad(gelu_exact, pre_ffn, grad_act).astype(jnp.bfloat16)
    grad_hidden = times_trans(grad_pre, w_in)
    up_grad = trans_times(act_adapter, grad_adapted)
    grad_act_ad = times_trans(grad_adapted, up_low)
    grad_pre_ad = local_grad(silu_smooth, pre_adapter, grad_act_ad).astype(jnp.bfloat16)
    down_grad = trans_times(hidden_low, grad_pre_ad)
    grad_hidden = grad_hidden + times_trans(grad_pre_ad, down_low)
    return (grad_hidden, down_grad, up_grad)


def encoder_forward(enc_rows, weights, gains, down_low, up_low, key_limit):
    w_qkv, w_out, w_in, w_back = weights
    qkv_low = product(enc_rows, w_qkv).astype(jnp.bfloat16)
    queries, key_rows, value_rows = jnp.split(qkv_low, 3, axis=1)
    mixture, logsum = attend_forward(queries, key_rows, value_rows, key_limit, False)
    attended = product(mixture.astype(jnp.bfloat16), w_out)
    resid_one = enc_rows.astype(jnp.float32) + attended
    hidden = normalize(resid_one, gains[0])
    branch, branch_saved = branch_forward(hidden, w_in, w_back, down_low, up_low)
    resid_two = hidden + branch
    output = normalize(resid_two, gains[1])
    row_mask = (jnp.arange(enc_rows.shape[0], dtype=jnp.int32) < key_limit).astype(jnp.float32)
    squares = jnp.stack(
        [
            masked_square(attended, row_mask),
            masked_square(branch, row_mask),
            masked_square(output, row_mask),
        ]
    )
    saved = (queries, key_rows, value_rows, logsum, resid_one, resid_two, branch_saved)
    return (output, squares, saved)


def encoder_backward(upstream, saved, weights, gains, down_low, up_low, key_limit):
    w_qkv, w_out, w_in, w_back = weights
    queries, key_rows, value_rows, logsum, resid_one, resid_two, branch_saved = saved
    grad_two = norm_grad(resid_two, gains[1], upstream)
    branch_grad, down_grad, up_grad = branch_backward(
        grad_two, branch_saved, w_in, w_back, down_low, up_low
    )
    grad_one = norm_grad(resid_one, gains[0], grad_two + branch_grad)
    mixture_grad = times_trans(grad_one.astype(jnp.bfloat16), w_out).astype(jnp.bfloat16)
    query_grad, key_grad, value_grad = attend_backward(
        queries, key_rows, value_rows, logsum, mixture_grad, key_limit, False
    )
    qkv_grad = jnp.concatenate([query_grad, key_grad, value_grad], axis=1).astype(jnp.bfloat16)
    return (grad_one + times_trans(qkv_grad, w_qkv), down_grad, up_grad)


def decoder_forward(dec_rows, enc_low, weights, gains, down_low, up_low, enc_limit, dec_limit):
    w_sqkv, w_so, w_cq, w_ckv, w_co, w_in, w_back = weights
    qkv_low = product(dec_rows, w_sqkv).astype(jnp.bfloat16)
    queries, key_rows, value_rows = jnp.split(qkv_low, 3, axis=1)
    mixture, logsum = attend_forward(queries, key_rows, value_rows, dec_limit, True)
    attended = product(mixture.astype(jnp.bfloat16), w_so)
    resid_self = dec_rows.astype(jnp.float32) + attended
    hidden = normalize(resid_self, gains[2])
    cross_q = product(hidden.astype(jnp.bfloat16), w_cq).astype(jnp.bfloat16)
    cross_kv = product(enc_low, w_ckv).astype(jnp.bfloat16)
    cross_k, cross_v = jnp.split(cross_kv, 2, axis=1)
    cross_mix, cross_logsum = attend_forward(cross_q, cross_k, cross_v, enc_limit, False)
    crossed = product(cross_mix.astype(jnp.bfloat16), w_co)
    resid_cross = hidden + crossed
    hidden_c = normalize(resid_cross, gains[3])
    branch, branch_saved = branch_forward(hidden_c, w_in, w_back, down_low, up_low)
    resid_two = hidden_c + branch
    output = normalize(resid_two, gains[4])
    row_mask = (jnp.arange(dec_rows.shape[0], dtype=jnp.int32) < dec_limit).astype(jnp.float32)
    squares = jnp.stack(
        [
            masked_square(attended, row_mask),
            masked_square(crossed, row_mask),
            masked_square(branch, row_mask),
            masked_square(output, row_mask),
        ]
    )
    saved = (
        queries,
        key_rows,
        value_rows,
        logsum,
        resid_self,
        cross_q,
        cross_k,
        cross_v,
        cross_logsum,
        resid_cross,
        resid_two,
        branch_saved,
    )
    return (output, squares, saved)


def decoder_backward(upstream, saved, weights, gains, down_low, up_low, enc_limit, dec_limit):
    w_sqkv, w_so, w_cq, w_ckv, w_co, w_in, w_back = weights
    (
        queries,
        key_rows,
        value_rows,
        logsum,
        resid_self,
        cross_q,
        cross_k,
        cross_v,
        cross_logsum,
        resid_cross,
        resid_two,
        branch_saved,
    ) = saved
    grad_two = norm_grad(resid_two, gains[4], upstream)
    branch_grad, down_grad, up_grad = branch_backward(
        grad_two, branch_saved, w_in, w_back, down_low, up_low
    )
    grad_cross = norm_grad(resid_cross, gains[3], grad_two + branch_grad)
    cross_mix_grad = times_trans(grad_cross.astype(jnp.bfloat16), w_co).astype(jnp.bfloat16)
    cq_grad, ck_grad, cv_grad = attend_backward(
        cross_q, cross_k, cross_v, cross_logsum, cross_mix_grad, enc_limit, False
    )
    grad_hidden = grad_cross + times_trans(cq_grad.astype(jnp.bfloat16), w_cq)
    enc_grad = times_trans(jnp.concatenate([ck_grad, cv_grad], axis=1).astype(jnp.bfloat16), w_ckv)
    grad_self = norm_grad(resid_self, gains[2], grad_hidden)
    mixture_grad = times_trans(grad_self.astype(jnp.bfloat16), w_so).astype(jnp.bfloat16)
    query_grad, key_grad, value_grad = attend_backward(
        queries, key_rows, value_rows, logsum, mixture_grad, dec_limit, True
    )
    qkv_grad = jnp.concatenate([query_grad, key_grad, value_grad], axis=1).astype(jnp.bfloat16)
    return (grad_self + times_trans(qkv_grad, w_sqkv), enc_grad, down_grad, up_grad)


def shards(
    enc_input,
    dec_input,
    enc_cot,
    dec_cot,
    enc_qkv,
    enc_attn_out,
    enc_ffn_in,
    enc_ffn_out,
    dec_self_qkv,
    dec_self_out,
    dec_cross_q,
    dec_cross_kv,
    dec_cross_out,
    dec_ffn_in,
    dec_ffn_out,
    norm_gains,
    enc_down,
    enc_up,
    dec_down,
    dec_up,
    enc_lengths,
    dec_lengths,
):
    enc_weights = (
        lax.all_gather(enc_qkv, "fsdp", axis=0, tiled=True),
        lax.all_gather(enc_attn_out, "fsdp", axis=0, tiled=True),
        lax.all_gather(enc_ffn_in, "fsdp", axis=0, tiled=True),
        lax.all_gather(enc_ffn_out, "fsdp", axis=0, tiled=True),
    )
    dec_weights = (
        lax.all_gather(dec_self_qkv, "fsdp", axis=0, tiled=True),
        lax.all_gather(dec_self_out, "fsdp", axis=0, tiled=True),
        lax.all_gather(dec_cross_q, "fsdp", axis=0, tiled=True),
        lax.all_gather(dec_cross_kv, "fsdp", axis=0, tiled=True),
        lax.all_gather(dec_cross_out, "fsdp", axis=0, tiled=True),
        lax.all_gather(dec_ffn_in, "fsdp", axis=0, tiled=True),
        lax.all_gather(dec_ffn_out, "fsdp", axis=0, tiled=True),
    )
    enc_down_low = enc_down.astype(jnp.bfloat16)
    enc_up_low = enc_up.astype(jnp.bfloat16)
    dec_down_low = dec_down.astype(jnp.bfloat16)
    dec_up_low = dec_up.astype(jnp.bfloat16)
    width = enc_input.shape[1]
    enc_results, dec_results, enc_saves, cross_grads, dec_in_grads = ([], [], [], [], [])
    seq_index = 0
    enc_limit = enc_lengths[seq_index]
    dec_limit = dec_lengths[seq_index]
    enc_result, enc_squares, enc_saved = encoder_forward(
        enc_input, enc_weights, norm_gains, enc_down_low, enc_up_low, enc_limit
    )
    enc_low = enc_result.astype(jnp.bfloat16)
    dec_result, dec_squares, dec_saved = decoder_forward(
        dec_input, enc_low, dec_weights, norm_gains, dec_down_low, dec_up_low, enc_limit, dec_limit
    )
    dec_upstream = dec_cot.astype(jnp.float32)
    dec_grad, enc_grad, down_grad, up_grad = decoder_backward(
        dec_upstream,
        dec_saved,
        dec_weights,
        norm_gains,
        dec_down_low,
        dec_up_low,
        enc_limit,
        dec_limit,
    )
    dec_down_grad = down_grad
    dec_up_grad = up_grad
    squares_total = jnp.concatenate([enc_squares, dec_squares])
    enc_results.append(enc_low)
    dec_results.append(dec_result.astype(jnp.bfloat16))
    enc_saves.append(enc_saved)
    cross_grads.append(enc_grad)
    dec_in_grads.append(dec_grad)
    counts = jnp.stack([jnp.sum(enc_lengths), jnp.sum(dec_lengths)]).astype(jnp.float32)
    statistics = jnp.concatenate([squares_total, counts])
    enc_back_weights = (
        lax.all_gather(enc_qkv, "fsdp", axis=0, tiled=True),
        lax.all_gather(enc_attn_out, "fsdp", axis=0, tiled=True),
        lax.all_gather(enc_ffn_in, "fsdp", axis=0, tiled=True),
        lax.all_gather(enc_ffn_out, "fsdp", axis=0, tiled=True),
    )
    seq_index = 0
    enc_upstream = enc_cot.astype(jnp.float32) + cross_grads[seq_index]
    enc_grad, down_grad, up_grad = encoder_backward(
        enc_upstream,
        enc_saves[seq_index],
        enc_back_weights,
        norm_gains,
        enc_down_low,
        enc_up_low,
        enc_lengths[seq_index],
    )
    enc_down_grad = down_grad
    enc_up_grad = up_grad
    enc_down_grad, enc_up_grad, dec_down_grad, dec_up_grad, statistics = lax.psum(
        (enc_down_grad, enc_up_grad, dec_down_grad, dec_up_grad, statistics), ("fsdp", "dp")
    )
    denominators = jnp.concatenate(
        [jnp.broadcast_to(statistics[7], (3,)), jnp.broadcast_to(statistics[8], (4,))]
    )
    rms = jnp.sqrt(statistics[:7] / (denominators * width))
    return (
        enc_results[0],
        dec_results[0],
        enc_grad,
        dec_in_grads[0],
        enc_down_grad,
        enc_up_grad,
        dec_down_grad,
        dec_up_grad,
        rms,
    )


def solution(mesh):
    placed = (
        P(("fsdp", "dp"), None),
        P(("fsdp", "dp"), None),
        P(("fsdp", "dp"), None),
        P(("fsdp", "dp"), None),
        P("fsdp", None),
        P("fsdp", None),
        P("fsdp", None),
        P("fsdp", None),
        P("fsdp", None),
        P("fsdp", None),
        P("fsdp", None),
        P("fsdp", None),
        P("fsdp", None),
        P("fsdp", None),
        P("fsdp", None),
        P(),
        P(),
        P(),
        P(),
        P(),
        P(("fsdp", "dp")),
        P(("fsdp", "dp")),
    )
    return jax.shard_map(
        shards,
        mesh=mesh,
        in_specs=placed,
        out_specs=(
            P(("fsdp", "dp"), None),
            P(("fsdp", "dp"), None),
            P(("fsdp", "dp"), None),
            P(("fsdp", "dp"), None),
            P(),
            P(),
            P(),
            P(),
            P(),
        ),
        check_vma=False,
    )
```

profile of v0, /device:TPU:0, one launch (start us, length us, event | category | flops | bytes accessed | tf_op | source)
XLA Modules:
  0.0 1110.6 jit_solution(6382028194719073615)
XLA Ops:
  16.2 4.0 copy.63
  24.6 33.5 %all-gather.20.cloned.1.call-done = bf16[1024,3072]{1,0:T(8,128)(2,1)} async-done(((bf16[128,3072]{1,0:T(8,128)(2,1)}), bf16[1024,3072]{1,0:T(8,128)(2,1)}) %all-gather.20.cloned.1.call-update) | async-done | bytes 6291472 | tf_op jit(solution)/shard_map/all_gather | solution.py:323
  58.2 4.6 convolution_convert_fusion.1
  68.0 19.9 %all-gather.22.cloned.1.call-done = bf16[1024,1024]{1,0:T(8,128)(2,1)} async-done(((bf16[128,1024]{1,0:T(8,128)(2,1)}), bf16[1024,1024]{1,0:T(8,128)(2,1)}) %all-gather.22.cloned.1.call-update) | async-done | bytes 2097168 | tf_op jit(solution)/shard_map/all_gather | solution.py:324
  88.0 3.5 fusion.163
  92.4 25.4 %all-gather.26.cloned.1.call-done = bf16[1024,1024]{1,0:T(8,128)(2,1)} async-done(((bf16[128,1024]{1,0:T(8,128)(2,1)}), bf16[1024,1024]{1,0:T(8,128)(2,1)}) %all-gather.26.cloned.1.call-update) | async-done | bytes 2097168 | tf_op jit(solution)/shard_map/all_gather | solution.py:325
  117.8 3.2 convolution_convert_fusion.5
  123.0 42.1 %all-gather.12.cloned.1.call-done = bf16[1024,3072]{1,0:T(8,128)(2,1)} async-done(((bf16[128,3072]{1,0:T(8,128)(2,1)}), bf16[1024,3072]{1,0:T(8,128)(2,1)}) %all-gather.12.cloned.1.call-update) | async-done | bytes 6291472 | tf_op jit(solution)/shard_map/all_gather | solution.py:317
  165.1 9.6 convolution_convert_fusion
  174.8 2.9 fusion.167
  177.7 3.9 reshape.321
  181.7 5.5 copy.67
  190.0 14.2 %copy.66 = bf16[1024,1024]{0,1:T(8,128)(2,1)} copy(bf16[1024,1024]{1,0:T(8,128)(2,1)} %get-tuple-element.359) | data formatting | bytes 4194304 | tf_op jit(solution)/shard_map/split | solution.py:176
  205.7 93.5 %while.5 = (s32[]{:T(128)}, bf16[2,512,16,64]{1,3,2,0:T(8,128)(2,1)}, f32[2,16,512,1]{2,1,3,0:T(8,128)S(1)}, s32[]{:T(128)}, bf16[2,512,16,64]{1,3,2,0:T(8,128)(...) while((s32[]{:T(128)}, bf16[2,512,16,64]{1,3,2,0:T(8,128)(2,1)}, ...), condition=%wide.region_3.4_spmd, body=%wide.region_0.3_spmd.sunk | while | flops 2248139776 | bytes 116659320 | solution.py:91
  206.4 15.0 %fusion.265 = (f32[16,512]{1,0:T(8,128)S(1)}, f32[16,512,1024]{2,1,0:T(8,128)}) fusion(pred[1024]{0:T(1024)(128)(4,1)S(1)} %iota_compare_fusion.7, bf16[1024,16,64]{0,2,1:T(8,128)(2,1)S(1)} %get-tuple-element.532, bf16[2,512,16,64]{1,3,2,0:T(8,128)(2,1)} %get-tuple-element.531, s32[]{:T(128)} %get-tuple-element.519), kind=kOutput, calls=%fused_computation.3.clone.1 | convolution fusion | flops 1098899456 | bytes 36734464 | tf_op jit(solution)/shard_map/while/body/eval_jaxpr/qhd,khd->hqk/dot_general | solution.py:59
  221.4 15.7 %fusion.266 = f32[16,512]{1,0:T(8,128)S(1)} fusion(f32[16,512,1024]{2,1,0:T(8,128)} %get-tuple-element.497, f32[16,512]{1,0:T(8,128)S(1)} %get-tuple-element.498, pred[1024]{0:T(1024)(128)(4,1)S(1)} %iota_compare_fusion.7), kind=kLoop, calls=%fused_computation.4.clone.1 | loop fusion | flops 33546240 | bytes 33620992 | tf_op jit(solution)/shard_map/while/body/eval_jaxpr/reduce_sum | solution.py:83
  237.1 14.9 %bitcast_dynamic-update-slice_fusion.6 = bf16[2,512,16,64]{1,3,2,0:T(8,128)(2,1)} fusion(bf16[2,512,16,64]{1,3,2,0:T(8,128)(2,1)} %get-tuple-element.520, s32[]{:T(128)} %get-tuple-element.519, bf16[1024,16,64]{0,2,1:T(8,128)(2,1)S(1)} %copy-done.6, f32[16,512,1024]{2,1,0:T(8,128)} %get-tuple-element.497, f32[16,512]{1,0:T(8,128)S(1)} %fusion.266, ...), kind=kOutput, calls=%fused_computation.6.clone.1 | convolution fusion | flops 1115684864 | bytes 37815808 | tf_op jit(solution)/shard_map/while/body/eval_jaxpr/hqk,khd->qhd/dot_general | solution.py:85
  252.7 15.8 %fusion.265 = (f32[16,512]{1,0:T(8,128)S(1)}, f32[16,512,1024]{2,1,0:T(8,128)}) fusion(pred[1024]{0:T(1024)(128)(4,1)S(1)} %iota_compare_fusion.7, bf16[1024,16,64]{0,2,1:T(8,128)(2,1)S(1)} %get-tuple-element.532, bf16[2,512,16,64]{1,3,2,0:T(8,128)(2,1)} %get-tuple-element.531, s32[]{:T(128)} %get-tuple-element.519), kind=kOutput, calls=%fused_computation.3.clone.1 | convolution fusion | flops 1098899456 | bytes 36734464 | tf_op jit(solution)/shard_map/while/body/eval_jaxpr/qhd,khd->hqk/dot_general | solution.py:59
  268.5 15.9 %fusion.266 = f32[16,512]{1,0:T(8,128)S(1)} fusion(f32[16,512,1024]{2,1,0:T(8,128)} %get-tuple-element.497, f32[16,512]{1,0:T(8,128)S(1)} %get-tuple-element.498, pred[1024]{0:T(1024)(128)(4,1)S(1)} %iota_compare_fusion.7), kind=kLoop, calls=%fused_computation.4.clone.1 | loop fusion | flops 33546240 | bytes 33620992 | tf_op jit(solution)/shard_map/while/body/eval_jaxpr/reduce_sum | solution.py:83
  284.4 14.8 %bitcast_dynamic-update-slice_fusion.6 = bf16[2,512,16,64]{1,3,2,0:T(8,128)(2,1)} fusion(bf16[2,512,16,64]{1,3,2,0:T(8,128)(2,1)} %get-tuple-element.520, s32[]{:T(128)} %get-tuple-element.519, bf16[1024,16,64]{0,2,1:T(8,128)(2,1)S(1)} %copy-done.6, f32[16,512,1024]{2,1,0:T(8,128)} %get-tuple-element.497, f32[16,512]{1,0:T(8,128)S(1)} %fusion.266, ...), kind=kOutput, calls=%fused_computation.6.clone.1 | convolution fusion | flops 1115684864 | bytes 37815808 | tf_op jit(solution)/shard_map/while/body/eval_jaxpr/hqk,khd->qhd/dot_general | solution.py:85
  299.2 4.6 copy.68
  305.7 5.7 fusion.166
  317.2 15.0 %fusion.179 = f32[1024,4096]{1,0:T(8,128)} fusion(bf16[1024,1024]{0,1:T(8,128)(2,1)S(1)} %fusion.51, bf16[1024,4096]{1,0:T(8,128)(2,1)} %all-gather.16.cloned.1.call-done), kind=kOutput, calls=%fused_computation.281 | convolution fusion | flops 8589934592 | bytes 27262976 | tf_op jit(solution)/shard_map/dot_general | solution.py:15
  332.2 16.8 %fusion.35 = f32[1024,1024]{0,1:T(8,128)S(1)} fusion(bf16[4096,1024]{1,0:T(8,128)(2,1)} %all-gather.18.cloned.1.call-done, f32[1024,4096]{1,0:T(8,128)} %fusion.179), kind=kOutput, calls=%fused_computation.54 | convolution fusion | flops 8610906112 | bytes 29360128 | tf_op jit(solution)/shard_map/dot_general | solution.py:15
  354.1 7.8 convolution_convert_fusion.2
  367.4 4.6 copy.73
  374.6 3.8 fusion.31
  380.9 4.5 fusion.99
  389.1 42.8 %all-gather.30.cloned.1.call-done = bf16[1024,4096]{1,0:T(8,128)(2,1)} async-done(((bf16[128,4096]{1,0:T(8,128)(2,1)}), bf16[1024,4096]{1,0:T(8,128)(2,1)}) %all-gather.30.cloned.1.call-update) | async-done | bytes 8388624 | tf_op jit(solution)/shard_map/all_gather | solution.py:328
  431.9 7.9 fusion.177
  439.8 48.4 %all-gather.32.cloned.1.call-done = bf16[4096,1024]{1,0:T(8,128)(2,1)} async-done(((bf16[512,1024]{1,0:T(8,128)(2,1)}), bf16[4096,1024]{1,0:T(8,128)(2,1)}) %all-gather.32.cloned.1.call-update) | async-done | bytes 8388624 | tf_op jit(solution)/shard_map/all_gather | solution.py:329
  488.2 7.1 fusion.62
  498.7 13.5 %fusion.63 = f32[256,1024]{1,0:T(8,128)} fusion(bf16[1024,4096]{1,0:T(8,128)(2,1)} %all-gather.30.cloned.1.call-done, f32[256,4096]{1,0:T(8,128)} %fusion.177, bf16[4096,1024]{1,0:T(8,128)(2,1)} %all-gather.32.cloned.1.call-done, f32[256,1024]{1,0:T(8,128)S(1)} %get-tuple-element.344, f32[256]{0:T(256)S(1)} %negate_multiply_fusion.4), kind=kOutput, calls=%fused_computation.114 | convolution fusion | flops 4309123072 | bytes 23069696 | tf_op jit(solution)/shard_map/dot_general | solution.py:19
  519.9 14.6 %multiply_reduce_fusion.1 = (f32[16,256]{1,0:T(8,128)S(1)}, f32[16,256,1024]{2,1,0:T(8,128)}) fusion(f32[16,256,1024]{2,1,0:T(8,128)} %copy-done.4, f32[16,256]{1,0:T(8,128)S(1)} %log_add_fusion.1, bf16[256,16,64]{0,2,1:T(8,128)(2,1)} %bitcast.221, bf16[1024,16,64]{0,2,1:T(8,128)(2,1)} %bitcast.214), kind=kOutput, calls=%fused_computation.44 | convolution fusion | flops 549449728 | bytes 36208640 | tf_op jit(solution)/shard_map/while/body/eval_jaxpr/qhd,khd->hqk/dot_general | solution.py:110
  534.5 9.7 fusion.76
  548.2 8.2 multiply_convert_fusion.1
  562.9 7.4 multiply_reduce_fusion.2
  583.5 4.8 fusion.129
  590.1 4.4 concatenate.21
  594.6 3.9 copy.87
  598.5 39.3 %psum.39 = f32[9]{0:T(128)} all-reduce(f32[9]{0:T(128)S(1)} %concatenate.21), channel_id=1, replica_groups=mesh['fsdp'=8,'dp'=4] {'fsdp','dp'}, use_global_device_ids=true, to_apply=%region_51.52 | all-reduce | flops 9 | bytes 72 | tf_op jit(solution)/shard_map/psum | solution.py:387
  643.7 21.2 %add_convert_fusion.6.clone.4 = bf16[1024,4096]{1,0:T(8,128)(2,1)} fusion(f32[1024,4096]{1,0:T(8,128)} %fusion.179, bf16[4096,1024]{1,0:T(8,128)(2,1)} %all-gather.18.cloned.1.call-done, f32[1024,1024]{0,1:T(8,128)} %copy-done.37, f32[1024]{0:T(1024)S(1)} %negate_multiply_fusion.1), kind=kOutput, calls=%fused_computation.42.clone.clone.clone.clone.clone.clone.1 | convolution fusion | flops 8646557696 | bytes 37752832 | tf_op jit(solution)/shard_map/dot_general | solution.py:19
  665.0 14.5 %multiply_reduce_fusion.6 = (f32[1024]{0:T(1024)S(1)}, f32[1024,1024]{0,1:T(8,128)S(1)}) fusion(f32[1024,1024]{0,1:T(8,128)S(1)} %copy-done.15, f32[1024]{0:T(1024)S(1)} %copy-done.72, f32[1024]{0:T(1024)S(1)} %bitcast.257, f32[1024,1024]{0,1:T(8,128)S(1)} %copy-done.21, bf16[1024,4096]{1,0:T(8,128)(2,1)} %all-gather.16.cloned.1.call-done, ...), kind=kOutput, calls=%fused_computation.78 | convolution fusion | flops 8597273600 | bytes 33570816 | tf_op jit(solution)/shard_map/dot_general | solution.py:19
  685.1 4.0 reshape.320
  689.1 5.6 copy.80
  696.2 209.7 %while.6 = (s32[]{:T(128)}, f32[1024,16,64]{0,2,1:T(8,128)}, f32[1024,16,64]{0,2,1:T(8,128)}, bf16[2,512,16,64]{1,3,2,0:T(8,128)(2,1)}, bf16[2,512,16,64]{1,3,2,...) while((s32[]{:T(128)}, f32[1024,16,64]{0,2,1:T(8,128)}, ...), condition=%wide.region_29.30_spmd.clone, body=%wide.region_27.29_spmd.clone.sunk | while | flops 5500298240 | bytes 373528832 | solution.py:136
  696.6 14.6 %fusion.276 = f32[16,512,1024]{2,1,0:T(8,128)} fusion(bf16[1024,16,64]{0,2,1:T(8,128)(2,1)S(1)} %get-tuple-element.565, bf16[2,512,16,64]{1,3,2,0:T(8,128)(2,1)} %get-tuple-element.563, s32[]{:T(128)} %get-tuple-element.547), kind=kOutput, calls=%fused_computation.28.clone.1 | convolution fusion | flops 1073741824 | bytes 36700672 | tf_op jit(solution)/shard_map/while/body/eval_jaxpr/qhd,khd->hqk/dot_general | solution.py:59
  711.9 23.2 %multiply_reduce_fusion.21 = (f32[16,512]{1,0:T(8,128)S(1)}, f32[16,512,1024]{2,1,0:T(8,128)}) fusion(f32[16,512,1024]{2,1,0:T(8,128)} %fusion.276, f32[16,512]{1,0:T(8,128)S(1)} %dynamic-slice_bitcast_fusion.2, pred[1024]{0:T(1024)(128)(4,1)S(1)} %iota_compare_fusion.8, bf16[1024,16,64]{0,2,1:T(8,128)(2,1)S(1)} %copy-done.7, ...), kind=kOutput, calls=%fused_computation.16.clone.1 | convolution fusion | flops 1115676672 | bytes 70321152 | tf_op jit(solution)/shard_map/while/body/eval_jaxpr/qhd,khd->hqk/dot_general | solution.py:110
  735.1 27.8 %multiply_convert_fusion.23 = bf16[16,512,1024]{2,1,0:T(8,128)(2,1)} fusion(f32[16,512,1024]{2,1,0:T(8,128)} %get-tuple-element.509, f32[16,512,1024]{2,1,0:T(8,128)} %fusion.276, f32[16,512]{1,0:T(8,128)S(1)} %get-tuple-element.510, f32[16,512]{1,0:T(8,128)S(1)} %dynamic-slice_bitcast_fusion.2, pred[1024]{0:T(1024)(128)(4,1)S(1)} %iota_compare_fusion.8), kind=kLoop, calls=%fused_computation.15.clone.1 | loop fusion | flops 50331648 | bytes 83952640 | tf_op jit(solution)/shard_map/while/body/eval_jaxpr/convert_element_type | solution.py:114
  762.9 11.4 %bitcast_add_fusion.4 = f32[1024,16,64]{0,2,1:T(8,128)} fusion(f32[1024,16,64]{0,2,1:T(8,128)} %get-tuple-element.548, bf16[16,512,1024]{2,1,0:T(8,128)(2,1)} %multiply_convert_fusion.23, pred[]{:T(512)S(6)} %compare.4, bf16[2,512,16,64]{1,3,2,0:T(8,128)(2,1)} %get-tuple-element.563, s32[]{:T(128)} %get-tuple-element.547), kind=kOutput, calls=%fused_computation.22.clone.1 | convolution fusion | flops 1076887552 | bytes 26214912 | tf_op jit(solution)/shard_map/while/body/eval_jaxpr/hqk,qhd->khd/dot_general | solution.py:121
  775.1 7.8 bitcast_dynamic-update-slice_fusion.8
  782.9 17.1 %bitcast_add_fusion.5 = f32[1024,16,64]{0,2,1:T(8,128)} fusion(f32[1024,16,64]{0,2,1:T(8,128)} %get-tuple-element.549, f32[16,512,1024]{2,1,0:T(8,128)} %fusion.276, f32[16,512]{1,0:T(8,128)S(1)} %dynamic-slice_bitcast_fusion.2, pred[1024]{0:T(1024)(128)(4,1)S(1)} %iota_compare_fusion.8, pred[]{:T(512)S(6)} %compare.4, ...), kind=kOutput, calls=%fused_computation.21.clone.1 | convolution fusion | flops 1109393408 | bytes 43025920 | tf_op jit(solution)/shard_map/while/body/eval_jaxpr/hqk,qhd->khd/dot_general | solution.py:126
  800.0 14.6 %fusion.276 = f32[16,512,1024]{2,1,0:T(8,128)} fusion(bf16[1024,16,64]{0,2,1:T(8,128)(2,1)S(1)} %get-tuple-element.565, bf16[2,512,16,64]{1,3,2,0:T(8,128)(2,1)} %get-tuple-element.563, s32[]{:T(128)} %get-tuple-element.547), kind=kOutput, calls=%fused_computation.28.clone.1 | convolution fusion | flops 1073741824 | bytes 36700672 | tf_op jit(solution)/shard_map/while/body/eval_jaxpr/qhd,khd->hqk/dot_general | solution.py:59
  815.3 23.2 %multiply_reduce_fusion.21 = (f32[16,512]{1,0:T(8,128)S(1)}, f32[16,512,1024]{2,1,0:T(8,128)}) fusion(f32[16,512,1024]{2,1,0:T(8,128)} %fusion.276, f32[16,512]{1,0:T(8,128)S(1)} %dynamic-slice_bitcast_fusion.2, pred[1024]{0:T(1024)(128)(4,1)S(1)} %iota_compare_fusion.8, bf16[1024,16,64]{0,2,1:T(8,128)(2,1)S(1)} %copy-done.7, ...), kind=kOutput, calls=%fused_computation.16.clone.1 | convolution fusion | flops 1115676672 | bytes 70321152 | tf_op jit(solution)/shard_map/while/body/eval_jaxpr/qhd,khd->hqk/dot_general | solution.py:110
  838.5 27.8 %multiply_convert_fusion.23 = bf16[16,512,1024]{2,1,0:T(8,128)(2,1)} fusion(f32[16,512,1024]{2,1,0:T(8,128)} %get-tuple-element.509, f32[16,512,1024]{2,1,0:T(8,128)} %fusion.276, f32[16,512]{1,0:T(8,128)S(1)} %get-tuple-element.510, f32[16,512]{1,0:T(8,128)S(1)} %dynamic-slice_bitcast_fusion.2, pred[1024]{0:T(1024)(128)(4,1)S(1)} %iota_compare_fusion.8), kind=kLoop, calls=%fused_computation.15.clone.1 | loop fusion | flops 50331648 | bytes 83952640 | tf_op jit(solution)/shard_map/while/body/eval_jaxpr/convert_element_type | solution.py:114
  866.2 12.6 %bitcast_add_fusion.4 = f32[1024,16,64]{0,2,1:T(8,128)} fusion(f32[1024,16,64]{0,2,1:T(8,128)} %get-tuple-element.548, bf16[16,512,1024]{2,1,0:T(8,128)(2,1)} %multiply_convert_fusion.23, pred[]{:T(512)S(6)} %compare.4, bf16[2,512,16,64]{1,3,2,0:T(8,128)(2,1)} %get-tuple-element.563, s32[]{:T(128)} %get-tuple-element.547), kind=kOutput, calls=%fused_computation.22.clone.1 | convolution fusion | flops 1076887552 | bytes 26214912 | tf_op jit(solution)/shard_map/while/body/eval_jaxpr/hqk,qhd->khd/dot_general | solution.py:121
  879.7 7.8 bitcast_dynamic-update-slice_fusion.8
  887.5 18.3 %bitcast_add_fusion.5 = f32[1024,16,64]{0,2,1:T(8,128)} fusion(f32[1024,16,64]{0,2,1:T(8,128)} %get-tuple-element.549, f32[16,512,1024]{2,1,0:T(8,128)} %fusion.276, f32[16,512]{1,0:T(8,128)S(1)} %dynamic-slice_bitcast_fusion.2, pred[1024]{0:T(1024)(128)(4,1)S(1)} %iota_compare_fusion.8, pred[]{:T(512)S(6)} %compare.4, ...), kind=kOutput, calls=%fused_computation.21.clone.1 | convolution fusion | flops 1109393408 | bytes 43025920 | tf_op jit(solution)/shard_map/while/body/eval_jaxpr/hqk,qhd->khd/dot_general | solution.py:126
  905.9 3.9 copy.81
  916.2 12.3 %add_add_fusion.2 = f32[1024,1024]{0,1:T(8,128)} fusion(f32[1024,1024]{0,1:T(8,128)} %copy-done.42, f32[1024]{0:T(1024)S(1)} %copy-done.90, bf16[1024,3072]{1,0:T(8,128)(2,1)} %all-gather.12.cloned.1.call-done, bf16[1024,1024]{0,1:T(8,128)(2,1)} %bitcast.230, bf16[1024,1024]{0,1:T(8,128)(2,1)S(1)} %bitcast.229, bf16[1024,1024]{0,1:T(8,128)(2,1)} %bitcast.233), kind=kOutput, calls=%fused_computation.96 | convolution fusion | flops 6463422464 | bytes 20975616 | tf_op jit(solution)/shard_map/dot_general | solution.py:19
  928.6 5.5 copy.88
  936.6 3.5 multiply_reduce_fusion.5
  946.8 149.5 %all-reduce.4.cloned.1.call-done = (f32[1024,512]{1,0:T(8,128)}, f32[512,1024]{1,0:T(8,128)}, f32[1024,512]{1,0:T(8,128)}, f32[512,1024]{1,0:T(8,128)}) async-done(((f32[1024,512]{1,0:T(8,128)}, f32[512,1024]{1,0:T(8,128)}, f32[1024,512]{1,0:T(8,128)}, f32[512,1024]{1,0:T(8,128)}), (f32[1024,512]{1,0:T(8,128)}, f32[512,1024]{1,0:T(8,128)}, f32[1024,512]{1,0:T(8,128)}, ...) | async-done | bytes 8388624 | tf_op jit(solution)/shard_map/psum | solution.py:387
  1096.3 3.2 copy.130
  (366 shorter events, 124.5 us)
Async XLA Ops:
  7.2 8.4 copy-start.85
  7.2 51.0 %all-gather.20.cloned.1.call-start = ((), (), s32[]{:S(2)}) async-start(), calls=%async_computation.4 | async-start | bytes 7077888 | tf_op jit(solution)/shard_map/all_gather | solution.py:323
  7.9 80.1 %all-gather.22.cloned.1.call-start = ((), (), s32[]{:S(2)}) async-start(), calls=%async_computation.5 | async-start | bytes 2359296 | tf_op jit(solution)/shard_map/all_gather | solution.py:324
  8.7 109.1 %all-gather.26.cloned.1.call-start = ((), (), s32[]{:S(2)}) async-start(), calls=%async_computation.7 | async-start | bytes 2359296 | tf_op jit(solution)/shard_map/all_gather | solution.py:325
  9.4 155.7 %all-gather.12.cloned.1.call-start = ((), (), s32[]{:S(2)}) async-start(), calls=%async_computation | async-start | bytes 7077888 | tf_op jit(solution)/shard_map/all_gather | solution.py:317
  10.0 295.8 %all-gather.14.cloned.1.call-start = ((), (), s32[]{:S(2)}) async-start(), calls=%async_computation.1 | async-start | bytes 2359296 | tf_op jit(solution)/shard_map/all_gather | solution.py:318
  10.6 306.6 %all-gather.16.cloned.1.call-start = ((), (), s32[]{:S(2)}) async-start(), calls=%async_computation.2 | async-start | bytes 9437184 | tf_op jit(solution)/shard_map/all_gather | solution.py:319
  11.1 10.9 copy-start.46
  11.2 321.1 %all-gather.18.cloned.1.call-start = ((), (), s32[]{:S(2)}) async-start(), calls=%async_computation.3 | async-start | bytes 9437184 | tf_op jit(solution)/shard_map/all_gather | solution.py:320
  11.9 342.1 %all-gather.24.cloned.1.call-start = ((), (), s32[]{:S(2)}) async-start(), calls=%async_computation.6 | async-start | bytes 4718592 | tf_op jit(solution)/shard_map/all_gather | solution.py:326
  12.7 372.8 %all-gather.28.cloned.1.call-start = ((), (), s32[]{:S(2)}) async-start(), calls=%async_computation.8 | async-start | bytes 2359296 | tf_op jit(solution)/shard_map/all_gather | solution.py:327
  13.4 418.5 %all-gather.30.cloned.1.call-start = ((), (), s32[]{:S(2)}) async-start(), calls=%async_computation.9 | async-start | bytes 9437184 | tf_op jit(solution)/shard_map/all_gather | solution.py:328
  14.0 474.2 %all-gather.32.cloned.1.call-start = ((), (), s32[]{:S(2)}) async-start(), calls=%async_computation.10 | async-start | bytes 9437184 | tf_op jit(solution)/shard_map/all_gather | solution.py:329
  14.7 1081.6 %all-reduce.4.cloned.1.call-start = ((), (), s32[]{:S(2)}) async-start(), calls=%async_computation.11 | async-start | bytes 16777216 | tf_op jit(solution)/shard_map/psum | solution.py:387
  16.2 101.6 %copy-start.67 = (f32[1,1024]{1,0:T(1,128)}, f32[1,1024]{1,0:T(1,128)S(1)}, u32[]{:S(2)}) copy-start(f32[1,1024]{1,0:T(1,128)S(1)} %get-tuple-element.374) | copy-start | bytes 12292
  16.2 42.0 %copy-start.60 = (bf16[256,1024]{1,0:T(8,128)(2,1)S(1)}, bf16[256,1024]{1,0:T(8,128)(2,1)}, u32[]{:S(2)}) copy-start(bf16[256,1024]{1,0:T(8,128)(2,1)} %param.27) | copy-start | bytes 1572868
  88.0 77.1 %copy-start.47 = (bf16[1024,1024]{1,0:T(8,128)(2,1)S(1)}, bf16[1024,1024]{1,0:T(8,128)(2,1)}, u32[]{:S(2)}) copy-start(bf16[1024,1024]{1,0:T(8,128)(2,1)} %param.26) | copy-start | bytes 6291460
  91.4 83.3 %copy-start.16 = (f32[256,1024]{1,0:T(8,128)}, f32[256,1024]{1,0:T(8,128)S(1)}, u32[]{:S(2)}) copy-start(f32[256,1024]{1,0:T(8,128)S(1)} %get-tuple-element.350) | copy-start | bytes 3145732
  91.4 83.3 %copy-start.73 = (f32[256]{0:T(256)}, f32[256]{0:T(256)S(1)}, u32[]{:S(2)}) copy-start(f32[256]{0:T(256)S(1)} %broadcast_multiply_fusion.4) | copy-start | bytes 3076
  92.4 82.4 %copy-start.81 = (f32[256]{0:T(256)}, f32[256]{0:T(256)S(1)}, u32[]{:S(2)}) copy-start(f32[256]{0:T(256)S(1)} %fusion.136) | copy-start | bytes 3076
  221.4 15.7 %copy-start.6 = (bf16[1024,16,64]{0,2,1:T(8,128)(2,1)S(1)}, bf16[1024,16,64]{0,2,1:T(8,128)(2,1)}, u32[]{:S(2)}) copy-start(bf16[1024,16,64]{0,2,1:T(8,128)(2,1)} %get-tuple-element.533) | copy-start | bytes 6291460 | tf_op jit(solution)/shard_map/while
  268.5 15.9 %copy-start.6 = (bf16[1024,16,64]{0,2,1:T(8,128)(2,1)S(1)}, bf16[1024,16,64]{0,2,1:T(8,128)(2,1)}, u32[]{:S(2)}) copy-start(bf16[1024,16,64]{0,2,1:T(8,128)(2,1)} %get-tuple-element.533) | copy-start | bytes 6291460 | tf_op jit(solution)/shard_map/while
  311.5 37.6 %copy-start.71 = (f32[1024]{0:T(1024)}, f32[1024]{0:T(1024)S(1)}, u32[]{:S(2)}) copy-start(f32[1024]{0:T(1024)S(1)} %broadcast_multiply_fusion.1) | copy-start | bytes 12292
  313.4 35.7 %copy-start.77 = (f32[1024]{0:T(1024)}, f32[1024]{0:T(1024)S(1)}, u32[]{:S(2)}) copy-start(f32[1024]{0:T(1024)S(1)} %fusion.134) | copy-start | bytes 12292
  332.2 16.9 %copy-start.96 = (f32[512,1024]{1,0:T(8,128)S(1)}, f32[512,1024]{1,0:T(8,128)}, u32[]{:S(2)}) copy-start(f32[512,1024]{1,0:T(8,128)} %param.43) | copy-start | bytes 6291460
  332.2 16.9 %copy-start.14 = (f32[1024,1024]{0,1:T(8,128)S(1)}, f32[1024,1024]{0,1:T(8,128)}, u32[]{:S(2)}) copy-start(f32[1024,1024]{0,1:T(8,128)} %copy-done.13) | copy-start | bytes 12582916
  332.2 16.9 %copy-start.99 = (f32[1024,512]{1,0:T(8,128)S(1)}, f32[1024,512]{1,0:T(8,128)}, u32[]{:S(2)}) copy-start(f32[1024,512]{1,0:T(8,128)} %fusion.131) | copy-start | bytes 6291460
  354.0 7.9 copy-start.25
  364.4 7.6 copy-start.26
  364.4 7.6 copy-start.92
  367.4 7.2 copy-start.19
  389.1 106.2 %copy-start.34 = (f32[256,512]{1,0:T(8,128)}, f32[256,512]{1,0:T(8,128)S(1)}, u32[]{:S(2)}) copy-start(f32[256,512]{1,0:T(8,128)S(1)} %fusion.122) | copy-start | bytes 1572868
  488.2 7.1 copy-start.48
  519.9 14.6 %copy-start.28 = (bf16[256,1024]{0,1:T(8,128)(2,1)S(1)}, bf16[256,1024]{0,1:T(8,128)(2,1)}, u32[]{:S(2)}) copy-start(bf16[256,1024]{0,1:T(8,128)(2,1)} %copy.77) | copy-start | bytes 1572868
  519.9 28.2 %slice-start = ((s8[16777216]{0:T(1024)(128)(4,1)}), s8[4194304]{0:T(1024)(128)(4,1)S(1)}, s32[]{:S(2)}) async-start(s8[16777216]{0:T(1024)(128)(4,1)} %bitcast.207), calls=%async_computation.12 | async-start | bytes 8388608
  519.9 28.2 %slice-start.1 = ((s8[16777216]{0:T(1024)(128)(4,1)}), s8[4194304]{0:T(1024)(128)(4,1)S(1)}, s32[]{:S(2)}) async-start(s8[16777216]{0:T(1024)(128)(4,1)} %bitcast.207), calls=%async_computation.13 | async-start | bytes 8388608
  519.9 28.2 %slice-start.2 = ((s8[16777216]{0:T(1024)(128)(4,1)}), s8[4194304]{0:T(1024)(128)(4,1)S(1)}, s32[]{:S(2)}) async-start(s8[16777216]{0:T(1024)(128)(4,1)} %bitcast.207), calls=%async_computation.14 | async-start | bytes 8388608
  534.5 9.7 copy-start.36
  534.5 13.6 %slice-start.3 = ((s8[16777216]{0:T(1024)(128)(4,1)}), s8[4194304]{0:T(1024)(128)(4,1)S(1)}, s32[]{:S(2)}) async-start(s8[16777216]{0:T(1024)(128)(4,1)} %bitcast.207), calls=%async_computation.15 | async-start | bytes 8388608
  548.2 8.2 copy-start.27
  570.3 7.4 slice-start.4
  583.5 6.7 copy-start.95
  588.3 49.5 %copy-start.40 = (f32[256,1024]{1,0:T(8,128)S(1)}, f32[256,1024]{1,0:T(8,128)}, u32[]{:S(2)}) copy-start(f32[256,1024]{1,0:T(8,128)} %copy-done.39) | copy-start | bytes 3145732
  594.6 45.9 %copy-start.87 = (f32[256]{0:T(256)S(1)}, f32[256]{0:T(256)}, u32[]{:S(2)}) copy-start(f32[256]{0:T(256)} %copy-done.86) | copy-start | bytes 3076
  643.7 21.2 %copy-start.15 = (f32[1024,1024]{0,1:T(8,128)S(1)}, f32[1024,1024]{0,1:T(8,128)}, u32[]{:S(2)}) copy-start(f32[1024,1024]{0,1:T(8,128)} %copy-done.13) | copy-start | bytes 12582916
  643.7 21.2 %copy-start.21 = (f32[1024,1024]{0,1:T(8,128)S(1)}, f32[1024,1024]{0,1:T(8,128)}, u32[]{:S(2)}) copy-start(f32[1024,1024]{0,1:T(8,128)} %fusion.129) | copy-start | bytes 12582916
  643.7 21.2 %copy-start.38 = (f32[1024,1024]{0,1:T(8,128)S(1)}, f32[1024,1024]{0,1:T(8,128)}, u32[]{:S(2)}) copy-start(f32[1024,1024]{0,1:T(8,128)} %copy-done.37) | copy-start | bytes 12582916
  643.7 21.2 %copy-start.72 = (f32[1024]{0:T(1024)S(1)}, f32[1024]{0:T(1024)}, u32[]{:S(2)}) copy-start(f32[1024]{0:T(1024)} %copy-done.71) | copy-start | bytes 12292
  643.7 21.2 %copy-start.84 = (f32[1,1024]{1,0:T(1,128)S(1)}, f32[1,1024]{1,0:T(1,128)}, u32[]{:S(2)}) copy-start(f32[1,1024]{1,0:T(1,128)} %get-tuple-element.376) | copy-start | bytes 12292
  664.9 14.5 %copy-start.80 = (f32[1024]{0:T(1024)S(1)}, f32[1024]{0:T(1024)}, u32[]{:S(2)}) copy-start(f32[1024]{0:T(1024)} %copy-done.79) | copy-start | bytes 12292
  664.9 14.6 %copy-start.78 = (f32[1024]{0:T(1024)S(1)}, f32[1024]{0:T(1024)}, u32[]{:S(2)}) copy-start(f32[1024]{0:T(1024)} %copy-done.77) | copy-start | bytes 12292
  689.1 7.2 copy-start.2
  689.1 7.2 copy-start.62
  696.6 15.3 %copy-start.7 = (bf16[1024,16,64]{0,2,1:T(8,128)(2,1)S(1)}, bf16[1024,16,64]{0,2,1:T(8,128)(2,1)}, u32[]{:S(2)}) copy-start(bf16[1024,16,64]{0,2,1:T(8,128)(2,1)} %get-tuple-element.568) | copy-start | bytes 6291460 | tf_op jit(solution)/shard_map/while
  696.6 15.3 %copy-start.18 = (bf16[2,512,16,64]{1,3,2,0:T(8,128)(2,1)S(1)}, bf16[2,512,16,64]{1,3,2,0:T(8,128)(2,1)}, u32[]{:S(2)}) copy-start(bf16[2,512,16,64]{1,3,2,0:T(8,128)(2,1)} %get-tuple-element.567) | copy-start | bytes 6291460 | tf_op jit(solution)/shard_map/while
  762.9 12.3 %copy-start = (bf16[16,512,1024]{2,1,0:T(8,128)(2,1)S(1)}, bf16[16,512,1024]{2,1,0:T(8,128)(2,1)}, u32[]{:S(2)}) copy-start(bf16[16,512,1024]{2,1,0:T(8,128)(2,1)} %multiply_convert_fusion.23) | copy-start | bytes 50331652 | tf_op jit(solution)/shard_map/while
  782.9 17.1 %copy-start.3 = (bf16[1024,16,64]{0,2,1:T(8,128)(2,1)S(1)}, bf16[1024,16,64]{0,2,1:T(8,128)(2,1)}, u32[]{:S(2)}) copy-start(bf16[1024,16,64]{0,2,1:T(8,128)(2,1)} %get-tuple-element.612) | copy-start | bytes 6291460 | tf_op jit(solution)/shard_map/while
  800.0 15.3 %copy-start.7 = (bf16[1024,16,64]{0,2,1:T(8,128)(2,1)S(1)}, bf16[1024,16,64]{0,2,1:T(8,128)(2,1)}, u32[]{:S(2)}) copy-start(bf16[1024,16,64]{0,2,1:T(8,128)(2,1)} %get-tuple-element.568) | copy-start | bytes 6291460 | tf_op jit(solution)/shard_map/while
  800.0 15.3 %copy-start.18 = (bf16[2,512,16,64]{1,3,2,0:T(8,128)(2,1)S(1)}, bf16[2,512,16,64]{1,3,2,0:T(8,128)(2,1)}, u32[]{:S(2)}) copy-start(bf16[2,512,16,64]{1,3,2,0:T(8,128)(2,1)} %get-tuple-element.567) | copy-start | bytes 6291460 | tf_op jit(solution)/shard_map/while
  866.2 13.5 %copy-start = (bf16[16,512,1024]{2,1,0:T(8,128)(2,1)S(1)}, bf16[16,512,1024]{2,1,0:T(8,128)(2,1)}, u32[]{:S(2)}) copy-start(bf16[16,512,1024]{2,1,0:T(8,128)(2,1)} %multiply_convert_fusion.23) | copy-start | bytes 50331652 | tf_op jit(solution)/shard_map/while
  887.5 18.3 %copy-start.3 = (bf16[1024,16,64]{0,2,1:T(8,128)(2,1)S(1)}, bf16[1024,16,64]{0,2,1:T(8,128)(2,1)}, u32[]{:S(2)}) copy-start(bf16[1024,16,64]{0,2,1:T(8,128)(2,1)} %get-tuple-element.612) | copy-start | bytes 6291460 | tf_op jit(solution)/shard_map/while
  928.6 8.0 copy-start.29
  928.6 8.0 copy-start.45
  928.6 8.0 copy-start.63
  (62 other events, 190.9 us)
Sparse Core Ops, SparseCore 0:
  9.9 48.2 all-gather.19
  60.0 27.8 all-gather.21
  89.9 27.8 all-gather.25
  119.5 45.5 all-gather.11
  166.8 27.8 all-gather.13
  196.5 54.3 all-gather.15
  252.8 54.3 all-gather.17
  309.1 36.7 all-gather.23
  347.8 27.8 all-gather.27
  377.4 54.4 all-gather.29
  433.8 54.3 all-gather.31
  915.7 180.5 all-reduce.3
where the time goes:
time: 1120 us; the launch traced here: 1110 us
  matrix products  443 us (40%)
  waiting for transfers between devices  369 us (33%)
  local copies, waits for them, and re-layouts  122 us (11%)
  other arithmetic  119 us (11%)
  blocking collectives  39.3 us (4%)
  between operations  16.9 us (2%)
    psum x1, waiting for transfers between devices, shards(): lax.psum((enc_down_grad, enc_up_grad, dec_down_grad, dec_up_grad, statist...  150 us
    dot_general x15, matrix products, product(): return jnp.dot(former, latter, preferred_element_type=jnp.float32)  90.2 us
    dot_general x14, matrix products, times_trans(): lax.dot_general(former, latter, (((1,), (1,)), ((), ())), preferred_eleme...  89 us
    convert_element_type x4, other arithmetic, one_block(): scores_grad = (probs * (probs_grad - row_inner)).astype(jnp.bfloat16)  64.8 us
    dot_general x4, matrix products, one_block(): jnp.einsum('qhd,khd->hqk', upstream_block, value_heads, preferred_element...  64.4 us
    dot_general x6, matrix products, masked_scores(): jnp.einsum('qhd,khd->hqk', query_block, key_heads, preferred_element_type...  63.4 us
    unnamed x219, local copies, waits for them, and re-layouts  53.1 us
    all_gather x1, waiting for transfers between devices, shards(): lax.all_gather(dec_ffn_out, 'fsdp', axis=0, tiled=True)  48.4 us
  transfers between devices with their start and end apart: 12, of which 7 were waited for; matrix products, arithmetic and copies ran while one was open for 25% of the time, Pallas kernels for 0%

commit v1 on v0

v1 whole, which is shorter than its diff:
```python
import functools
import math

import jax
import jax.numpy as jnp
from jax import lax
from jax.experimental import pallas as pl
from jax.experimental.pallas import tpu as pltpu
from jax.sharding import PartitionSpec as P

HEAD = 64
PAIR = 2 * HEAD
EPSILON = 1e-05
F32 = jnp.float32
BF16 = jnp.bfloat16
VMEM_BYTES = 58 * 2**20


def nn(former, latter):
    return jnp.dot(former, latter, preferred_element_type=F32)


def nt(former, latter):
    return lax.dot_general(
        former, latter, (((1,), (1,)), ((), ())), preferred_element_type=F32
    )


def tn(former, latter):
    return lax.dot_general(
        former, latter, (((0,), (0,)), ((), ())), preferred_element_type=F32
    )


def standardize(entries):
    centered = entries - jnp.mean(entries, axis=-1, keepdims=True)
    spread = jnp.mean(centered * centered, axis=-1, keepdims=True)
    inverse = lax.rsqrt(spread + EPSILON)
    return centered * inverse, inverse


def standardize_grad(unit, inverse, scaled):
    return inverse * (
        scaled
        - jnp.mean(scaled, axis=-1, keepdims=True)
        - unit * jnp.mean(scaled * unit, axis=-1, keepdims=True)
    )


class Fetch:
    def __init__(self, source, whole, sems, chunks):
        self.source, self.whole, self.sems, self.chunks = source, whole, sems, chunks

    def copy(self, chunk):
        width = self.whole.shape[1] // self.chunks
        columns = pl.ds(chunk * width, width)
        return pltpu.make_async_copy(
            self.source.at[:, columns], self.whole.at[:, columns], self.sems.at[chunk]
        )

    def start(self):
        for chunk in range(self.chunks):
            self.copy(chunk).start()

    def wait(self, chunk):
        @pl.when(pl.program_id(0) == 0)
        def _():
            self.copy(chunk).wait()

    def wait_all(self):
        for chunk in range(self.chunks):
            self.wait(chunk)


UNIT_US = 5.8
LEAD_US = 4.0


class Gather:
    def __init__(self, owns, wholes, splits, sends, recvs, locals_):
        self.owns, self.wholes, self.splits = owns, wholes, splits
        self.sends, self.recvs, self.locals = sends, recvs, locals_
        self.units = [(m, part) for m, split in enumerate(splits) for part in range(split)]
        f, z = lax.axis_index("fsdp"), lax.axis_index("dp")
        odd = z % 2
        y, x, core = f // 4, (f // 2) % 2, f % 2
        beside, above = f + 2 - 4 * x, f + 4 - 8 * y
        self.own = f
        self.direct = beside + odd * (above - beside)
        self.onward = above + odd * (beside - above)
        self.far = beside + 4 - 8 * y
        self.twin = f + 1 - 2 * core
        self.partner = z + 1 - 2 * odd

    def meet(self):
        barrier = pltpu.get_barrier_semaphore()
        mesh = pl.DeviceIdType.MESH
        for to in ({"fsdp": self.direct}, {"fsdp": self.onward}, {"fsdp": self.twin}, {"dp": self.partner}):
            pl.semaphore_signal(barrier, inc=1, device_id=to, device_id_type=mesh)
        pl.semaphore_wait(barrier, 4)

    def transfer(self, unit, kind):
        m, part = self.units[unit]
        whole, own = self.wholes[m], self.owns[m]
        block = own.shape[0]
        rows = block // self.splits[m]
        owner = (self.own, self.direct, self.direct, self.own, self.direct, self.far, self.onward)[kind]
        there = whole.at[pl.ds(pl.multiple_of(owner * block + part * rows, 16), rows), :]
        here = own.at[pl.ds(part * rows, rows), :] if kind in (0, 3) else there
        to = {"fsdp": (self.direct, self.onward, None, self.twin, self.twin, self.twin, self.twin)[kind]}
        if kind == 2:
            to = {"dp": self.partner}
        return pltpu.make_async_remote_copy(
            src_ref=here,
            dst_ref=there,
            send_sem=self.sends.at[unit, kind],
            recv_sem=self.recvs.at[unit, kind],
            device_id=to,
            device_id_type=pl.DeviceIdType.MESH,
        )

    def keep(self, m):
        block = self.owns[m].shape[0]
        rows = pl.ds(pl.multiple_of(self.own * block, 16), block)
        return pltpu.make_async_copy(self.owns[m], self.wholes[m].at[rows, :], self.locals.at[m])

    def begin(self):
        self.meet()
        for unit in range(len(self.units)):
            self.transfer(unit, 0).start()
        for unit in range(len(self.units)):
            self.transfer(unit, 3).start()
        for m in range(len(self.owns)):
            self.keep(m).start()

    def pass_on(self, unit):
        self.transfer(unit, 0).wait_recv()
        for kind in (1, 2, 4):
            self.transfer(unit, kind).start()

    def share(self, unit):
        self.transfer(unit, 1).wait_recv()
        self.transfer(unit, 5).start()
        self.transfer(unit, 2).wait_recv()
        self.transfer(unit, 6).start()

    def arrived(self, unit):
        for kind in (3, 4, 5, 6):
            self.transfer(unit, kind).wait_recv()

    def first(self, count):
        for unit in range(count):
            self.pass_on(unit)
            if unit:
                self.share(unit - 1)
        self.share(count - 1)
        for unit in range(count):
            self.arrived(unit)
        self.keep(0).wait()

    def plan(self, skip, slots, steps, pace, lead):
        acts = {}
        for unit in range(skip, len(self.units)):
            due = lead + LEAD_US + UNIT_US * (unit - skip + 1)
            for act, at in ((self.pass_on, due), (self.share, due + UNIT_US + 2.0)):
                tick = min(math.ceil(at / pace), steps * slots - 1)
                acts.setdefault((tick // slots, tick % slots), []).append((act, unit))
        return acts

    def poll(self, acts, slot):
        for (step, at), todo in acts.items():
            if at == slot:

                @pl.when(pl.program_id(0) == step)
                def _(todo=todo):
                    for act, unit in todo:
                        act(unit)

    def finish(self, skip):
        for unit in range(len(self.units)):
            if unit >= skip:
                self.arrived(unit)
            for kind in range(7):
                self.transfer(unit, kind).wait_send()
        for m in range(len(self.owns)):
            if not (m == 0 and skip):
                self.keep(m).wait()


class Hosted:
    def __init__(self, owns, skip_first=False, fsdp=8):
        self.owns = list(owns)
        self.fsdp = fsdp
        self.splits = [max(1, a.size // 131072) for a in self.owns]
        self.splits = [4 if a.shape == (128, 3072) else n for a, n in zip(self.owns, self.splits)]
        self.skip = self.splits[0] if skip_first else 0

    def out_shapes(self):
        return [
            jax.ShapeDtypeStruct((a.shape[0] * self.fsdp, a.shape[1]), a.dtype) for a in self.owns
        ]

    def scratch(self):
        units = sum(self.splits)
        return [
            pltpu.SemaphoreType.DMA((units, 7)),
            pltpu.SemaphoreType.DMA((units, 7)),
            pltpu.SemaphoreType.DMA((len(self.owns),)),
        ]

    def run(self, own_refs, whole_refs, scratch):
        return Gather(own_refs, whole_refs, self.splits, *scratch)


ANY = pl.BlockSpec(memory_space=pl.ANY)
SCALAR = pl.BlockSpec(memory_space=pltpu.SMEM)


def rows_spec(rows, width):
    return pl.BlockSpec((rows, width), lambda i: (i, 0))


def whole_spec(shape):
    return pl.BlockSpec(shape, lambda i: (0,) * len(shape))


def hosted_call(body, name, grid, ins, outs, scratch, flops, moved, hosted=None, collective=None):
    count = len(hosted.owns) if hosted else 0

    def kernel(*refs):
        refs = list(refs)

        def take(n):
            taken = refs[:n]
            del refs[:n]
            return taken

        own_refs, in_refs, whole_refs, out_refs = take(count), take(len(ins)), take(count), take(len(outs))
        gather = None
        if hosted:
            gather = hosted.run(own_refs, whole_refs, refs[-3:])
            refs = refs[:-3]

            @pl.when(pl.program_id(0) == 0)
            def _():
                gather.begin()

        body(in_refs, out_refs, refs, gather)
        if hosted:

            @pl.when(pl.program_id(0) == grid[0] - 1)
            def _():
                gather.finish(hosted.skip)

    out = pl.pallas_call(
        kernel,
        grid=grid,
        in_specs=[ANY] * count + [s for _, s in ins],
        out_specs=[ANY] * count + [s for _, _, s in outs],
        scratch_shapes=[*scratch, *(hosted.scratch() if hosted else [])],
        out_shape=(hosted.out_shapes() if hosted else [])
        + [jax.ShapeDtypeStruct(s, d) for s, d, _ in outs],
        compiler_params=pltpu.CompilerParams(
            vmem_limit_bytes=VMEM_BYTES,
            **({"collective_id": collective, "has_side_effects": True} if hosted else {}),
        ),
        cost_estimate=pl.CostEstimate(flops=flops, bytes_accessed=moved, transcendentals=0),
        name=name,
    )(*(hosted.owns if hosted else []), *[a for a, _ in ins])
    return list(out[count:]), list(out[:count])


def staged_call(
    body, name, grid, limit, mats, ins, outs, scratch=(), flops=0, hosted=None, collective=None
):
    holders = []
    for mat, chunks in mats:
        like = hosted.out_shapes()[0] if mat is None else mat
        holders.append(pltpu.VMEM(like.shape, like.dtype))
        holders.append(pltpu.SemaphoreType.DMA((chunks,)))
    given = [mat for mat, _ in mats if mat is not None]

    def staged(in_refs, out_refs, rest, gather):
        sources = list(in_refs[1 : 1 + len(given)])
        fetches = []
        for at, (mat, chunks) in enumerate(mats):
            source = gather.wholes[0] if mat is None else sources.pop(0)
            fetches.append(Fetch(source, rest[2 * at], rest[2 * at + 1], chunks))

        @pl.when(pl.program_id(0) == 0)
        def _():
            for fetch, (mat, _) in zip(fetches, mats):
                if mat is not None:
                    fetch.start()

        args = (in_refs[0], fetches, in_refs[1 + len(given) :], out_refs, rest[2 * len(mats) :])
        body(*args, gather)

    moved = sum(a.size * a.dtype.itemsize for a in given)
    moved += sum(a.size * a.dtype.itemsize for a, _ in ins)
    moved += sum(math.prod(s) * jnp.dtype(d).itemsize for s, d, _ in outs)
    return hosted_call(
        staged,
        name,
        grid,
        [(limit, SCALAR)] + [(mat, ANY) for mat in given] + list(ins),
        outs,
        [*holders, *scratch],
        flops,
        moved,
        hosted,
        collective,
    )


def project(name, limit, rows_in, mat, width, chunks, hosted=None, collective=None):
    total, depth = rows_in.shape
    block = min(256, total)
    step = width // chunks

    def body(limit, fetches, ins, outs, extra, gather):
        (fetch,) = fetches
        acts = gather.plan(hosted.skip, chunks, total // block, 1.1, 0.0) if gather else {}
        if gather and mat is None:

            @pl.when(pl.program_id(0) == 0)
            def _():
                gather.first(hosted.skip)
                fetch.start()

        left = ins[0][...]
        for chunk in range(chunks):
            if gather:
                gather.poll(acts, chunk)
            fetch.wait(chunk)
            columns = slice(chunk * step, (chunk + 1) * step)
            outs[0][:, columns] = nn(left, fetch.whole[:, columns]).astype(BF16)

    outs, wholes = staged_call(
        body,
        name,
        (total // block,),
        limit,
        [(mat, chunks)],
        [(rows_in, rows_spec(block, depth))],
        [((total, width), BF16, rows_spec(block, width))],
        flops=2 * total * depth * width,
        hosted=hosted,
        collective=collective,
    )
    return outs[0], wholes


def attend(name, limit, queries, keys, values, causal, hosted=None, collective=None, pace=3.3):
    q_len, k_len = queries[0].shape[0], keys[0].shape[0]
    pairs = 1024 // PAIR
    step = min(256, q_len)

    def body(ins, outs, extra, gather):
        limit_ref, q_ref, k_ref, v_ref = ins
        e_ref, o_ref, inv_ref = outs
        acts = gather.plan(0, 2, pairs, pace, 0.0) if gather else {}
        lanes = lax.broadcasted_iota(jnp.int32, (1, PAIR), 1)
        places = lax.broadcasted_iota(jnp.int32, (k_len, 1), 0)
        bias = jnp.where(places < limit_ref[0], 0.0, -1000000000.0)
        q_two = q_ref[...].astype(F32) * (1.0 / math.sqrt(HEAD))
        k_two = k_ref[...].astype(F32)
        v_two = v_ref[...].astype(F32)
        mixed = []
        for half in range(2):
            if gather:
                gather.poll(acts, half)
            own = (lanes >= HEAD * half) & (lanes < HEAD * (half + 1))
            spare = lanes == HEAD * (1 - half)
            q_own = jnp.where(own, q_two, jnp.where(spare, 1.0, 0.0)).astype(BF16)
            k_own = jnp.where(own, k_two, jnp.where(spare, bias, 0.0)).astype(BF16)
            v_own = jnp.where(own, v_two, jnp.where(spare, 1.0, 0.0)).T.astype(BF16)
            parts = []
            for start in range(0, q_len, step):
                scores = nt(k_own, q_own[start : start + step])
                if causal:
                    shape = (k_len, step)
                    key_at = lax.broadcasted_iota(jnp.int32, shape, 0)
                    query_at = lax.broadcasted_iota(jnp.int32, shape, 1) + start
                    scores = jnp.where(key_at <= query_at, scores, -1000000000.0)
                highest = jnp.max(scores, axis=0, keepdims=True)
                weights = jnp.exp(scores - highest).astype(BF16)
                e_ref[0, :, half * q_len + start : half * q_len + start + step] = weights
                parts.append(nn(v_own, weights))
            out = jnp.concatenate(parts, axis=1) if len(parts) > 1 else parts[0]
            at = HEAD * (1 - half)
            inverse = 1.0 / out[at : at + 1]
            own_rows = out[HEAD * half : HEAD * (half + 1)]
            mixed.append((own_rows * inverse, jnp.broadcast_to(inverse, own_rows.shape)))
        o_ref[...] = jnp.concatenate([mixed[0][0], mixed[1][0]], axis=0).T.astype(BF16)
        inv_ref[...] = jnp.concatenate([mixed[0][1], mixed[1][1]], axis=0).T

    def columns(rows, first):
        return pl.BlockSpec((rows, PAIR), lambda i: (0, first + i))

    outs, wholes = hosted_call(
        body,
        name,
        (pairs,),
        [
            (limit, SCALAR),
            (queries[0], columns(q_len, queries[1])),
            (keys[0], columns(k_len, keys[1])),
            (values[0], columns(k_len, values[1])),
        ],
        [
            (
                (pairs, k_len, 2 * q_len),
                BF16,
                pl.BlockSpec((1, k_len, 2 * q_len), lambda i: (i, 0, 0)),
            ),
            ((q_len, 1024), BF16, columns(q_len, 0)),
            ((q_len, 1024), F32, columns(q_len, 0)),
        ],
        [],
        16 * pairs * q_len * k_len * PAIR,
        4 * pairs * q_len * k_len,
        hosted,
        collective,
    )
    return *outs, wholes


def attend_grad(name, queries, keys, values, weights, mixture, inverse, upstream):
    q_len, k_len = queries[0].shape[0], keys[0].shape[0]
    pairs = 1024 // PAIR
    step = min(256, q_len)
    factor = 1.0 / math.sqrt(HEAD)

    def kernel(q_ref, k_ref, v_ref, e_ref, o_ref, inv_ref, do_ref, dq_ref, dk_ref, dv_ref, ds_ref):
        lanes = lax.broadcasted_iota(jnp.int32, (1, PAIR), 1)
        first = lanes < HEAD
        scaled = do_ref[...].astype(F32) * inv_ref[...]
        inner = scaled.astype(BF16).astype(F32) * o_ref[...].astype(F32)
        coarse = inner.astype(BF16)
        fine = (inner - coarse.astype(F32)).astype(BF16)
        picks = lax.broadcasted_iota(jnp.int32, (8, PAIR), 1)
        ones = [
            jnp.where(picks < HEAD, 1.0, 0.0).astype(BF16),
            jnp.where(picks < HEAD, 0.0, 1.0).astype(BF16),
        ]
        delta = [(nt(one, coarse) + nt(one, fine))[0:1] for one in ones]
        do_two = jnp.concatenate(
            [jnp.where(first, scaled, 0.0).astype(BF16), jnp.where(first, 0.0, scaled).astype(BF16)],
            axis=0,
        )
        q_all = q_ref[...].astype(F32) * factor
        q_two = jnp.concatenate(
            [jnp.where(first, q_all, 0.0).astype(BF16), jnp.where(first, 0.0, q_all).astype(BF16)],
            axis=0,
        )
        k_flip = k_ref[...].astype(F32).T.astype(BF16)
        v_all = v_ref[...]
        for half in range(2):
            for start in range(0, q_len, step):
                at = half * q_len + start
                probs_grad = nt(v_all, do_two[at : at + step])
                held = e_ref[0, :, at : at + step].astype(F32)
                ds_ref[:, at : at + step] = (
                    held * (probs_grad - delta[half][:, start : start + step])
                ).astype(BF16)
        dv_ref[...] = nn(e_ref[0], do_two).astype(BF16)
        dk_ref[...] = nn(ds_ref[...], q_two).astype(BF16)
        turned = nn(k_flip, ds_ref[...]) * factor
        rows = lax.broadcasted_iota(jnp.int32, (PAIR, 1), 0)
        dq_ref[...] = jnp.where(rows < HEAD, turned[:, :q_len], turned[:, q_len:]).T.astype(BF16)

    def columns(rows, at):
        return pl.BlockSpec((rows, PAIR), lambda i: (0, at + i))

    return pl.pallas_call(
        kernel,
        grid=(pairs,),
        in_specs=[
            columns(q_len, queries[1]),
            columns(k_len, keys[1]),
            columns(k_len, values[1]),
            pl.BlockSpec((1, k_len, 2 * q_len), lambda i: (i, 0, 0)),
            columns(q_len, 0),
            columns(q_len, 0),
            columns(q_len, 0),
        ],
        out_specs=[columns(q_len, 0), columns(k_len, 0), columns(k_len, 0)],
        out_shape=[
            jax.ShapeDtypeStruct((q_len, 1024), BF16),
            jax.ShapeDtypeStruct((k_len, 1024), BF16),
            jax.ShapeDtypeStruct((k_len, 1024), BF16),
        ],
        scratch_shapes=[pltpu.VMEM((k_len, 2 * q_len), BF16)],
        compiler_params=pltpu.CompilerParams(vmem_limit_bytes=VMEM_BYTES),
        cost_estimate=pl.CostEstimate(
            flops=32 * pairs * q_len * k_len * PAIR,
            bytes_accessed=4 * pairs * q_len * k_len,
            transcendentals=0,
        ),
        name=name,
    )(queries[0], keys[0], values[0], weights, mixture, inverse, upstream)


def row_mask(limit, block):
    at = lax.broadcasted_iota(jnp.int32, (block, 1), 0) + pl.program_id(0) * block
    return (at < limit).astype(F32)


def add_squares(ref, row, entries, mask):
    sums = jnp.sum(entries * entries * mask, axis=0, keepdims=True)
    first = pl.program_id(0) == 0

    @pl.when(first)
    def _():
        ref[row : row + 1, :] = sums

    @pl.when(jnp.logical_not(first))
    def _():
        ref[row : row + 1, :] += sums


def spread_lanes(column):
    return jnp.broadcast_to(column, (column.shape[0], 128))


def out_norm(name, limit, mixture, residual, gain, mat, next_mat=None, residual_gain=None):
    total, width = mixture.shape
    block = min(256, total)
    mats = [(mat, 1)] + ([] if next_mat is None else [(next_mat, 1)])

    def body(limit, fetches, ins, outs, extra, gather):
        o_ref, r_ref, g_ref, rg_ref = ins
        fetches[0].wait_all()
        added = nn(o_ref[...], fetches[0].whole[...])
        base = r_ref[...].astype(F32)
        if residual_gain is not None:
            base = base * rg_ref[...]
        unit, inverse = standardize(base + added)
        outs[0][...] = unit.astype(BF16)
        outs[1][...] = spread_lanes(inverse)
        add_squares(outs[2], 0, added, row_mask(limit[0], block))
        if next_mat is not None:
            fetches[1].wait_all()
            hidden = (unit * g_ref[...]).astype(BF16)
            outs[3][...] = nn(hidden, fetches[1].whole[...]).astype(BF16)

    outs = [
        ((total, width), BF16, rows_spec(block, width)),
        ((total, 128), F32, rows_spec(block, 128)),
        ((8, width), F32, whole_spec((8, width))),
    ]
    if next_mat is not None:
        outs.append(((total, width), BF16, rows_spec(block, width)))
    return staged_call(
        body,
        name,
        (total // block,),
        limit,
        mats,
        [
            (mixture, rows_spec(block, width)),
            (residual, rows_spec(block, width)),
            (gain, whole_spec((1, width))),
            (gain if residual_gain is None else residual_gain, whole_spec((1, width))),
        ],
        outs,
        flops=2 * total * width * width * len(mats),
    )[0]


def branch(
    name, limit, unit, gain, gain_out, w_in, w_back, down_low, up_low,
    hosted=None, collective=None, pace=2.4,
):
    total, width = unit.shape
    hidden_units = w_in.shape[1]
    adapter = down_low.shape[1]
    block = min(256, total)
    chunks = 4
    step = hidden_units // chunks

    def body(limit, fetches, ins, outs, extra, gather):
        u_ref, g_ref, go_ref, ad_ref, au_ref = ins
        y_ref, unit_ref, inv_ref, slope_ref, wa_ref, ad_slope_ref, sq_ref = outs
        (act,) = extra
        first, second = fetches
        hidden = u_ref[...].astype(F32) * g_ref[...]
        low = hidden.astype(BF16)
        pre = nn(low, ad_ref[...])
        gate = jax.nn.sigmoid(pre)
        wa = (pre * gate).astype(BF16)
        wa_ref[...] = wa
        ad_slope_ref[...] = (gate * (1.0 + pre * (1.0 - gate))).astype(BF16)
        adapted = 4.0 * nn(wa, au_ref[...])
        acts = gather.plan(0, chunks, total // block, pace, 0.0) if gather else {}
        for chunk in range(chunks):
            if gather:
                gather.poll(acts, chunk)
            first.wait(chunk)
            columns = slice(chunk * step, (chunk + 1) * step)
            fp = nn(low, first.whole[:, columns])
            cdf = 0.5 * (1.0 + lax.erf(fp * (1.0 / math.sqrt(2.0))))
            act[:, columns] = (fp * cdf).astype(BF16)
            bell = jnp.exp(-0.5 * fp * fp) * (1.0 / math.sqrt(2.0 * math.pi))
            slope_ref[:, columns] = (cdf + fp * bell).astype(BF16)
        second.wait_all()
        added = nn(act[...], second.whole[...]) + adapted
        out_unit, inverse = standardize(hidden + added)
        result = out_unit * go_ref[...]
        y_ref[...] = result.astype(BF16)
        unit_ref[...] = out_unit.astype(BF16)
        inv_ref[...] = spread_lanes(inverse)
        mask = row_mask(limit[0], block)
        add_squares(sq_ref, 0, added, mask)
        add_squares(sq_ref, 1, result, mask)

    outs, wholes = staged_call(
        body,
        name,
        (total // block,),
        limit,
        [(w_in, chunks), (w_back, 1)],
        [
            (unit, rows_spec(block, width)),
            (gain, whole_spec((1, width))),
            (gain_out, whole_spec((1, width))),
            (down_low, whole_spec(down_low.shape)),
            (up_low, whole_spec(up_low.shape)),
        ],
        [
            ((total, width), BF16, rows_spec(block, width)),
            ((total, width), BF16, rows_spec(block, width)),
            ((total, 128), F32, rows_spec(block, 128)),
            ((total, hidden_units), BF16, rows_spec(block, hidden_units)),
            ((total, adapter), BF16, rows_spec(block, adapter)),
            ((total, adapter), BF16, rows_spec(block, adapter)),
            ((8, width), F32, whole_spec((8, width))),
        ],
        scratch=[pltpu.VMEM((block, hidden_units), BF16)],
        flops=4 * total * width * (hidden_units + adapter),
        hosted=hosted,
        collective=collective,
    )
    return *outs, wholes


def adapter_grad(upstream, refs):
    (uo_ref, io_ref, go_ref, ui_ref, gi_ref, wa_ref, as_ref, ad_ref, au_ref) = refs
    grad_two = standardize_grad(uo_ref[...].astype(F32), io_ref[:, 0:1], upstream * go_ref[...])
    dvd = (4.0 * grad_two).astype(BF16)
    low = (ui_ref[...].astype(F32) * gi_ref[...]).astype(BF16)
    du = (nt(dvd, au_ref[...]) * as_ref[...].astype(F32)).astype(BF16)
    total = grad_two + nt(du, ad_ref[...])
    return grad_two.astype(BF16), total, tn(low, du), tn(wa_ref[...], dvd)


def hidden_grad(dz, total, fetches, refs, dfp, chunks):
    slope_ref, ui_ref, ii_ref, gi_ref = refs
    back, within, last = fetches
    step = dfp.shape[1] // chunks
    back.wait_all()
    for chunk in range(chunks):
        columns = slice(chunk * step, (chunk + 1) * step)
        act_grad = nt(dz, back.whole[columns, :])
        dfp[:, columns] = (act_grad * slope_ref[:, columns].astype(F32)).astype(BF16)
    within.wait_all()
    total = total + nt(dfp[...], within.whole[...])
    grad_one = standardize_grad(ui_ref[...].astype(F32), ii_ref[:, 0:1], total * gi_ref[...])
    last.wait_all()
    return grad_one, nt(grad_one.astype(BF16), last.whole[...]).astype(BF16)


def dec_branch_grad(
    name, limits, cot, saved_out, gain_out, saved_in, gain_in, slope, wa, ad_slope,
    w_back, w_in, w_out, down_low, up_low, squares,
):
    total, width = cot.shape
    hidden_units = w_in.shape[1]
    adapter = down_low.shape[1]
    whole = [
        cot, saved_out[0], saved_out[1], gain_out, saved_in[0], gain_in, wa, ad_slope, down_low,
        up_low, slope, saved_in[1], *squares,
    ]

    def body(limit, fetches, ins, outs, extra, gather):
        grad_ref, mix_ref, down_ref, up_ref = outs
        (other,), cot_ref, slope_ref, ii_ref = ins[:1], ins[1], ins[11], ins[12]
        dz, part, down_ref[...], up_ref[:adapter] = adapter_grad(cot_ref[...].astype(F32), ins[2:11])
        sums = [ref[row : row + 1, :] for ref, rows in zip(ins[13:], (1, 2, 1, 1, 2)) for row in range(rows)]
        lanes = lax.broadcasted_iota(jnp.int32, (1, width), 1)
        counts = jnp.where(lanes == 0, limit[0], jnp.where(lanes == 1, other[0], 0)).astype(F32)
        up_ref[adapter:] = jnp.concatenate([*sums, counts], axis=0)
        grad_ref[...], mix_ref[...] = hidden_grad(
            dz, part, fetches, (slope_ref, ins[5], ii_ref, ins[6]), extra[0], 4
        )

    return staged_call(
        body,
        name,
        (1,),
        limits[0],
        [(w_back, 1), (w_in, 1), (w_out, 1)],
        [(limits[1], SCALAR)] + [(a, whole_spec(a.shape)) for a in whole],
        [
            (cot.shape, F32, whole_spec(cot.shape)),
            (cot.shape, BF16, whole_spec(cot.shape)),
            (down_low.shape, F32, whole_spec(down_low.shape)),
            ((adapter + 8, width), F32, whole_spec((adapter + 8, width))),
        ],
        scratch=[pltpu.VMEM((total, hidden_units), BF16)],
        flops=4 * total * width * (hidden_units + 2 * adapter),
    )[0]


def enc_adapter_grad(
    name, limit, cot, cross, cross_mat, saved_out, gain_out, saved_in, gain_in, wa, ad_slope,
    down_low, up_low,
):
    total, width = cot.shape
    adapter = down_low.shape[1]
    block = min(256, total)
    rows = rows_spec(block, width)

    def body(limit, fetches, ins, outs, extra, gather):
        dz_ref, part_ref, down_ref, up_ref = outs
        down_sum, up_sum = extra
        fetches[0].wait_all()
        upstream = ins[0][...].astype(F32)
        for at in range(2):
            upstream = upstream + nt(ins[1 + at][...], fetches[0].whole[:, at * width : (at + 1) * width])
        dz_ref[...], part_ref[...], down_part, up_part = adapter_grad(upstream, ins[3:])
        at = pl.program_id(0)

        @pl.when(at == 0)
        def _():
            up_sum[...] = up_part
            down_sum[...] = down_part

        @pl.when(at > 0)
        def _():
            up_sum[...] += up_part
            down_sum[...] += down_part

        @pl.when(at == total // block - 1)
        def _():
            up_ref[...] = up_sum[...].astype(BF16)
            down_ref[...] = down_sum[...].astype(BF16)

    return staged_call(
        body,
        name,
        (total // block,),
        limit,
        [(cross_mat, 1)],
        [
            (cot, rows),
            (cross[0], rows),
            (cross[1], rows),
            (saved_out[0], rows),
            (saved_out[1], rows_spec(block, 128)),
            (gain_out, whole_spec((1, width))),
            (saved_in[0], rows),
            (gain_in, whole_spec((1, width))),
            (wa, rows_spec(block, adapter)),
            (ad_slope, rows_spec(block, adapter)),
            (down_low, whole_spec(down_low.shape)),
            (up_low, whole_spec(up_low.shape)),
        ],
        [
            ((total, width), BF16, rows),
            ((total, width), F32, rows),
            (down_low.shape, BF16, whole_spec(down_low.shape)),
            (up_low.shape, BF16, whole_spec(up_low.shape)),
        ],
        scratch=[pltpu.VMEM(down_low.shape, F32), pltpu.VMEM(up_low.shape, F32)],
        flops=4 * total * width * (width + 2 * adapter),
    )[0]


def enc_hidden_grad(name, limit, dz, part, slope, saved_in, gain_in, w_back, w_in, w_out):
    total, width = dz.shape
    hidden_units = w_in.shape[1]
    block = min(256, total)
    rows = rows_spec(block, width)

    def body(limit, fetches, ins, outs, extra, gather):
        outs[0][...], outs[1][...] = hidden_grad(
            ins[0][...], ins[1][...], fetches, ins[2:], extra[0], 4
        )

    return staged_call(
        body,
        name,
        (total // block,),
        limit,
        [(w_back, 1), (w_in, 1), (w_out, 1)],
        [
            (dz, rows),
            (part, rows),
            (slope, rows_spec(block, hidden_units)),
            (saved_in[0], rows),
            (saved_in[1], rows_spec(block, 128)),
            (gain_in, whole_spec((1, width))),
        ],
        [((total, width), F32, rows), ((total, width), BF16, rows)],
        scratch=[pltpu.VMEM((block, hidden_units), BF16)],
        flops=4 * total * width * hidden_units,
    )[0]


def middle_grad(name, limit, grad_cross, dq, saved, gain, w_cq, w_so):
    total, width = dq.shape
    block = min(256, total)
    unit, inv = saved

    def body(limit, fetches, ins, outs, extra, gather):
        gc_ref, dq_ref, u_ref, i_ref, g_ref = ins
        fetches[0].wait_all()
        hidden_grad = gc_ref[...] + nt(dq_ref[...], fetches[0].whole[...])
        grad_self = standardize_grad(
            u_ref[...].astype(F32), i_ref[:, 0:1], hidden_grad * g_ref[...]
        )
        outs[0][...] = grad_self
        fetches[1].wait_all()
        outs[1][...] = nt(grad_self.astype(BF16), fetches[1].whole[...]).astype(BF16)

    return staged_call(
        body,
        name,
        (total // block,),
        limit,
        [(w_cq, 1), (w_so, 1)],
        [
            (grad_cross, rows_spec(block, width)),
            (dq, rows_spec(block, width)),
            (unit, rows_spec(block, width)),
            (inv, rows_spec(block, 128)),
            (gain, whole_spec((1, width))),
        ],
        [
            ((total, width), F32, rows_spec(block, width)),
            ((total, width), BF16, rows_spec(block, width)),
        ],
        flops=4 * total * width * width,
    )[0]


def input_grad(name, limit, base, parts, mat):
    total, width = base.shape
    block = min(256, total)
    count = len(parts)

    def body(limit, fetches, ins, outs, extra, gather):
        (fetch,) = fetches
        result = ins[0][...]
        for at in range(count):
            fetch.wait(at)
            result = result + nt(ins[1 + at][...], fetch.whole[:, at * width : (at + 1) * width])
        outs[0][...] = result

    return staged_call(
        body,
        name,
        (total // block,),
        limit,
        [(mat, count)],
        [(base, rows_spec(block, width))] + [(p, rows_spec(block, width)) for p in parts],
        [((total, width), F32, rows_spec(block, width))],
        flops=2 * total * width * width * count,
    )[0][0]


NAMES = (
    "enc_qkv",
    "enc_attn_out",
    "enc_ffn_in",
    "enc_ffn_out",
    "dec_self_qkv",
    "dec_self_out",
    "dec_cross_q",
    "dec_cross_kv",
    "dec_cross_out",
    "dec_ffn_in",
    "dec_ffn_out",
)


class Weights(dict):
    def __init__(self, blocks, hosting, fsdp):
        super().__init__()
        self.blocks, self.hosting, self.fsdp = blocks, hosting, fsdp
        if not hosting:
            for name, block in blocks.items():
                self[name] = lax.all_gather(block, "fsdp", axis=0, tiled=True)

    def host(self, collective, *names, skip_first=False):
        self.names = names
        if not self.hosting:
            return {}
        owns = [self.blocks[name] for name in names]
        return {"hosted": Hosted(owns, skip_first, self.fsdp), "collective": collective}

    def take(self, wholes):
        self.update(zip(self.names, wholes))


def layers(enc_limit, dec_limit, enc_input, dec_input, enc_cot, dec_cot, w, gains, adapters):
    gain = [gains[k : k + 1] for k in range(5)]
    enc_down, enc_up, dec_down, dec_up = (a.astype(BF16) for a in adapters)
    host = w.host(1, "enc_qkv", "enc_attn_out", "dec_self_out", skip_first=True)
    qkv, wholes = project("enc_project", enc_limit, enc_input, w.get("enc_qkv"), 3072, 3, **host)
    w.take(wholes)
    host = w.host(2, "enc_ffn_in", "enc_ffn_out")
    e_enc, o_enc, inv_enc, wholes = attend(
        "enc_attend", enc_limit, (qkv, 0), (qkv, 8), (qkv, 16), False, **host
    )
    w.take(wholes)
    unit1, dev1, sq_a = out_norm("enc_out_norm", enc_limit, o_enc, enc_input, gain[0], w["enc_attn_out"])
    host = w.host(3, "dec_self_qkv", "dec_cross_kv", "dec_cross_q")
    enc_out, unit2, dev2, slope_e, wa_e, ads_e, sq_b, wholes = branch(
        "enc_branch", enc_limit, unit1, gain[0], gain[1], w["enc_ffn_in"], w["enc_ffn_out"],
        enc_down, enc_up, **host,
    )
    w.take(wholes)
    sqkv, _ = project("dec_project", dec_limit, dec_input, w["dec_self_qkv"], 3072, 3)
    e_self, o_self, inv_self, _ = attend(
        "dec_attend", dec_limit, (sqkv, 0), (sqkv, 8), (sqkv, 16), True
    )
    unit3, dev3, sq_c, cross_q = out_norm(
        "dec_out_norm", dec_limit, o_self, dec_input, gain[2], w["dec_self_out"], w["dec_cross_q"]
    )
    kv, _ = project("cross_project", enc_limit, enc_out, w["dec_cross_kv"], 2048, 2)
    host = w.host(4, "dec_cross_out", "dec_ffn_in", "dec_ffn_out")
    e_cross, o_cross, inv_cross, wholes = attend(
        "cross_attend", enc_limit, (cross_q, 0), (kv, 0), (kv, 8), False, pace=1.0, **host
    )
    w.take(wholes)
    unit4, dev4, sq_d = out_norm(
        "cross_out_norm", dec_limit, o_cross, unit3, gain[3], w["dec_cross_out"], residual_gain=gain[2]
    )
    dec_out, unit5, dev5, slope_d, wa_d, ads_d, sq_e, _ = branch(
        "dec_branch", dec_limit, unit4, gain[3], gain[4], w["dec_ffn_in"], w["dec_ffn_out"],
        dec_down, dec_up,
    )
    grad_cross, do_cross, dec_down_grad, dec_up_grad = dec_branch_grad(
        "dec_branch_grad", (enc_limit, dec_limit), dec_cot, (unit5, dev5), gain[4], (unit4, dev4), gain[3],
        slope_d, wa_d, ads_d, w["dec_ffn_out"], w["dec_ffn_in"], w["dec_cross_out"], dec_down, dec_up,
        (sq_a, sq_b, sq_c, sq_d, sq_e),
    )
    dcq, dck, dcv = attend_grad(
        "cross_attend_grad", (cross_q, 0), (kv, 0), (kv, 8), e_cross, o_cross, inv_cross, do_cross
    )
    dz, part, enc_down_grad, enc_up_grad = enc_adapter_grad(
        "enc_adapter_grad", enc_limit, enc_cot, (dck, dcv), w["dec_cross_kv"], (unit2, dev2), gain[1],
        (unit1, dev1), gain[0], wa_e, ads_e, enc_down, enc_up,
    )
    grad_self, do_self = middle_grad(
        "dec_middle_grad", dec_limit, grad_cross, dcq, (unit3, dev3), gain[2], w["dec_cross_q"], w["dec_self_out"]
    )
    dsq, dsk, dsv = attend_grad(
        "dec_attend_grad", (sqkv, 0), (sqkv, 8), (sqkv, 16), e_self, o_self, inv_self, do_self
    )
    dec_grad = input_grad("dec_input_grad", dec_limit, grad_self, [dsq, dsk, dsv], w["dec_self_qkv"])
    grad_one, do_enc = enc_hidden_grad(
        "enc_hidden_grad", enc_limit, dz, part, slope_e, (unit1, dev1), gain[0],
        w["enc_ffn_out"], w["enc_ffn_in"], w["enc_attn_out"],
    )
    deq, dek, dev = attend_grad(
        "enc_attend_grad", (qkv, 0), (qkv, 8), (qkv, 16), e_enc, o_enc, inv_enc, do_enc
    )
    enc_grad = input_grad("enc_input_grad", enc_limit, grad_one, [deq, dek, dev], w["enc_qkv"])
    return (
        (enc_out, dec_out, enc_grad, dec_grad),
        (enc_down_grad, enc_up_grad),
        (dec_down_grad, dec_up_grad),
    )


def shards(fsdp, dp, enc_input, dec_input, enc_cot, dec_cot, *rest):
    mats, (gains, enc_down, enc_up, dec_down, dec_up, enc_lengths, dec_lengths) = rest[:11], rest[11:]
    weights = Weights(dict(zip(NAMES, mats)), fsdp == 8 and dp % 2 == 0, fsdp)
    results, enc_grads, dec_grads = layers(
        enc_lengths, dec_lengths, enc_input, dec_input, enc_cot, dec_cot, weights, gains,
        (enc_down, enc_up, dec_down, dec_up),
    )
    everyone = ("fsdp", "dp")
    dec_down_grad, dec_up_grad = lax.psum(dec_grads, everyone)
    enc_down_grad, enc_up_grad = lax.psum(enc_grads, everyone)
    width = enc_input.shape[1]
    adapter = dec_up.shape[0]
    statistics = dec_up_grad[adapter:]
    rows = jnp.stack([statistics[7, 0]] * 3 + [statistics[7, 1]] * 4)
    rms = jnp.sqrt(jnp.sum(statistics[:7], axis=1) / (rows * width))
    return (
        *results,
        enc_down_grad.astype(F32),
        enc_up_grad.astype(F32),
        dec_down_grad,
        dec_up_grad[:adapter],
        rms,
    )


def solution(mesh):
    by_rows = P(("fsdp", "dp"), None)
    placed = (by_rows,) * 4 + (P("fsdp", None),) * 11 + (P(),) * 5 + (P(("fsdp", "dp")),) * 2
    return jax.shard_map(
        functools.partial(shards, mesh.shape["fsdp"], mesh.shape["dp"]),
        mesh=mesh,
        in_specs=placed,
        out_specs=(by_rows,) * 4 + (P(),) * 5,
        check_vma=False,
    )
```

time: 1120 us -> 720 us (0.64)
  Pallas kernels: 0 us -> 491 us
  matrix products: 443 us -> 0 us
  waiting for transfers between devices: 369 us -> 175 us
  other arithmetic: 119 us -> 12.1 us
  local copies, waits for them, and re-layouts: 122 us -> 16.1 us
  blocking collectives: 39.3 us -> 0 us
    pallas_call x0 -> x20, Pallas kernels: none -> 491 us  [the longest x17 431 us: hosted_call(): pl.pallas_call(kernel, grid=grid, in_specs=[ANY] * count + [s for _, s in...]
    dot_general x59 -> x0, matrix products: 443 us -> none  [the longest x15 90.2 us: product(): return jnp.dot(former, latter, preferred_element_type=jnp.float32)]
    all_gather x11 -> x0, waiting for transfers between devices: 212 us -> none  [the longest x1 48.4 us: shards(): lax.all_gather(dec_ffn_out, 'fsdp', axis=0, tiled=True)]
    convert_element_type x7 -> x6, other arithmetic: 66.4 us -> 10.6 us  [the longest x4 6.16 us: layers(): enc_down, enc_up, dec_down, dec_up = (a.astype(BF16) for a in adapters)]
    unnamed x219 -> x14, local copies, waits for them, and re-layouts: 53.1 us -> 5.33 us
    reduce_sum x20 -> x1, other arithmetic: 45.7 us -> 0.88 us  [shards(): rms = jnp.sqrt(jnp.sum(statistics[:7], axis=1) / (rows * width))]
    psum x1 -> x0, blocking collectives: 39.3 us -> none  [shards(): lax.psum((enc_down_grad, enc_up_grad, dec_down_grad, dec_up_grad, statist...]
    split x10 -> x0, local copies, waits for them, and re-layouts: 30.8 us -> none  [the longest x3 20 us: encoder_forward(): queries, key_rows, value_rows = jnp.split(qkv_low, 3, axis=1)]
  transfers between devices with their start and end apart: 12 -> 2, of which waited for: 7 -> 2; matrix products, arithmetic and copies ran while one was open for 25% -> 1% of each run, Pallas kernels for 0% -> 14%
where the time goes in v1:
time: 720 us; the launch traced here: 711 us
  Pallas kernels  491 us (68%)
  waiting for transfers between devices  175 us (24%)
  local copies, waits for them, and re-layouts  16.1 us (2%)
  between operations  16 us (2%)
  other arithmetic  12.1 us (2%)
    pallas_call x17, Pallas kernels, hosted_call(): pl.pallas_call(kernel, grid=grid, in_specs=[ANY] * count + [s for _, s in...  431 us
    psum x1, waiting for transfers between devices, shards(): dec_down_grad, dec_up_grad = lax.psum(dec_grads, everyone)  145 us
    pallas_call x3, Pallas kernels, attend_grad(): pl.pallas_call(kernel, grid=(pairs,), in_specs=[columns(q_len, queries[1]...  60 us
    psum x1, waiting for transfers between devices, shards(): enc_down_grad, enc_up_grad = lax.psum(enc_grads, everyone)  29.8 us
  transfers between devices with their start and end apart: 2, of which 2 were waited for; matrix products, arithmetic and copies ran while one was open for 1% of the time, Pallas kernels for 14%

profile of v1, /device:TPU:0, one launch (start us, length us, event | category | flops | bytes accessed | tf_op | source)
XLA Modules:
  0.0 710.8 jit_solution(5240924988402247451)
XLA Ops:
  7.2 0.0 copy-start
  7.2 0.0 all-reduce.7.cloned.1.call-start
  8.7 1.6 fusion.2
  10.2 2.7 convert_element_type.18.refs_9_.refs_12_
  12.9 0.0 copy-done
  12.9 0.0 copy-start.1
  12.9 1.2 convert_element_type.19.refs_10_.refs_13_
  14.1 0.8 copy-done.1
  14.9 0.0 copy-start.2
  14.9 1.1 convert_element_type.20.refs_6_.refs_13_
  16.0 0.9 copy-done.2
  16.9 1.2 convert_element_type.21.refs_7_.refs_14_
  18.0 57.9 %enc_project.1 = (bf16[1024,3072]{1,0:T(8,128)(2,1)}, bf16[1024,1024]{1,0:T(8,128)(2,1)}, bf16[1024,1024]{1,0:T(8,128)(2,1)}, bf16[1024,3072]{1,0:T(8,128)(2,1)}) custom-call(bf16[128,3072]{1,0:T(8,128)(2,1)} %refs_0_.17, bf16[128,1024]{1,0:T(8,128)(2,1)} %refs_1_.4, bf16[128,1024]{1,0:T(8,128)(2,1)} %refs_2_.6, s32[1]{0:T(128)S(6)} %copy.36.refs_3_.refs_2_.refs_0_, ...), custom_call_target="tpu_custom_call" | custom-call | flops 6442450944 | bytes 8388608 | tf_op jit(solution)/shard_map/enc_project/pallas_call | solution.py:255
  76.0 74.2 %enc_attend.1 = (bf16[1024,4096]{1,0:T(8,128)(2,1)}, bf16[4096,1024]{1,0:T(8,128)(2,1)}, bf16[8,1024,2048]{2,1,0:T(8,128)(2,1)}, bf16[1024,1024]{1,0:T(8,128)(2,1)}, f32[1024,1024]{1,0:T(8,128)}) custom-call(bf16[128,4096]{1,0:T(8,128)(2,1)} %refs_0_.18, bf16[512,1024]{1,0:T(8,128)(2,1)} %refs_1_.5, s32[1]{0:T(128)S(6)} %copy.36.refs_3_.refs_2_.refs_0_, ...), custom_call_target="tpu_custom_call" | custom-call | flops 17179869184 | bytes 33554432 | tf_op jit(solution)/shard_map/enc_attend/pallas_call | solution.py:255
  150.2 8.4 %enc_out_norm.1 = (bf16[1024,1024]{1,0:T(8,128)(2,1)}, f32[1024,128]{1,0:T(8,128)}, f32[8,1024]{1,0:T(8,128)}) custom-call(s32[1]{0:T(128)S(6)} %copy.36.refs_3_.refs_2_.refs_0_, bf16[1024,1024]{1,0:T(8,128)(2,1)} %get-tuple-element.78.refs_1_.refs_3_, bf16[1024,1024]{1,0:T(8,128)(2,1)} %get-tuple-element.79.refs_2_.o_ref, bf16[1024,1024]{1,0:T(8,128)(2,1)} %refs_3_.4, ...), custom_call_target="tpu_custom_call" | custom-call | flops 2147483648 | bytes 8953856 | tf_op jit(solution)/shard_map/enc_out_norm/pallas_call | solution.py:255
  158.6 62.3 %enc_branch.1 = (bf16[1024,3072]{1,0:T(8,128)(2,1)}, bf16[1024,2048]{1,0:T(8,128)(2,1)}, bf16[1024,1024]{1,0:T(8,128)(2,1)}, bf16[1024,1024]{1,0:T(8,128)(2,1)},...) custom-call(bf16[128,3072]{1,0:T(8,128)(2,1)} %refs_0_.19, ...), custom_call_target="tpu_custom_call" | custom-call | flops 19327352832 | bytes 36216832 | tf_op jit(solution)/shard_map/enc_branch/pallas_call | solution.py:255
  220.9 6.0 dec_project.1.refs_1_.refs_2_.refs_3_.q_ref.k_ref.v_ref
  226.9 8.6 %dec_attend.1 = (bf16[8,256,512]{2,1,0:T(8,128)(2,1)}, bf16[256,1024]{1,0:T(8,128)(2,1)}, f32[256,1024]{1,0:T(8,128)}) custom-call(s32[1]{0:T(128)S(6)} %copy.37.refs_0_.refs_4_, bf16[256,3072]{1,0:T(8,128)(2,1)} %dec_project.1.refs_1_.refs_2_.refs_3_.q_ref.k_ref.v_ref, bf16[256,3072]{1,0:T(8,128)(2,1)} %dec_project.1.refs_1_.refs_2_.refs_3_.q_ref.k_ref.v_ref, ...), custom_call_target="tpu_custom_call" | custom-call | flops 1073741824 | bytes 2097152 | tf_op jit(solution)/shard_map/dec_attend/pallas_call | solution.py:255
  235.5 9.5 %cross_project.1.refs_5_.refs_6_.k_ref.v_ref = bf16[1024,2048]{1,0:T(8,128)(2,1)} custom-call(s32[1]{0:T(128)S(6)} %copy.36.refs_3_.refs_2_.refs_0_, bf16[1024,2048]{1,0:T(8,128)(2,1)} %get-tuple-element.87.refs_1_, bf16[1024,1024]{1,0:T(8,128)(2,1)} %get-tuple-element.161.refs_2_), custom_call_target="tpu_custom_call" | custom-call | flops 4294967296 | bytes 10485760 | tf_op jit(solution)/shard_map/cross_project/pallas_call | solution.py:255
  245.0 5.3 dec_out_norm.1
  250.3 92.6 %cross_attend.1 = (bf16[1024,1024]{1,0:T(8,128)(2,1)}, bf16[1024,4096]{1,0:T(8,128)(2,1)}, bf16[4096,1024]{1,0:T(8,128)(2,1)}, bf16[8,1024,512]{2,1,0:T(8,128)(2...) custom-call(bf16[128,1024]{1,0:T(8,128)(2,1)} %refs_0_.20, bf16[128,4096]{1,0:T(8,128)(2,1)} %refs_1_.7, ...), custom_call_target="tpu_custom_call" | custom-call | flops 4294967296 | bytes 8388608 | tf_op jit(solution)/shard_map/cross_attend/pallas_call | solution.py:255
  342.9 4.6 cross_out_norm.1
  347.5 11.4 %dec_branch.1 = (bf16[256,1024]{1,0:T(8,128)(2,1)}, bf16[256,1024]{1,0:T(8,128)(2,1)}, f32[256,128]{1,0:T(8,128)}, bf16[256,4096]{1,0:T(8,128)(2,1)}, bf16[256,5...) custom-call(s32[1]{0:T(128)S(6)} %copy.37.refs_0_.refs_4_, ...), custom_call_target="tpu_custom_call" | custom-call | flops 4831838208 | bytes 23240704 | tf_op jit(solution)/shard_map/dec_branch/pallas_call | solution.py:255
  358.9 14.3 %dec_branch_grad.1 = (f32[256,1024]{1,0:T(8,128)}, bf16[256,1024]{1,0:T(8,128)(2,1)}, f32[1024,512]{1,0:T(8,128)}, f32[520,1024]{1,0:T(8,128)}) custom-call(s32[1]{0:T(128)S(6)} %copy.36.refs_3_.refs_2_.refs_0_, bf16[4096,1024]{1,0:T(8,128)(2,1)} %get-tuple-element.89.refs_2_.refs_1_, bf16[1024,4096]{1,0:T(8,128)(2,1)} %get-tuple-element.88.refs_1_.refs_2_, ...), custom_call_target="tpu_custom_call" | custom-call | flops 5368709120 | bytes 31399940 | tf_op jit(solution)/shard_map/dec_branch_grad/pallas_call | solution.py:255
  373.2 13.0 %cross_attend_grad.1 = (bf16[256,1024]{1,0:T(8,128)(2,1)}, bf16[1024,1024]{1,0:T(8,128)(2,1)}, bf16[1024,1024]{1,0:T(8,128)(2,1)}) custom-call(bf16[256,1024]{1,0:T(8,128)(2,1)} %get-tuple-element.86.refs_4_.q_ref, bf16[1024,2048]{1,0:T(8,128)(2,1)} %cross_project.1.refs_5_.refs_6_.k_ref.v_ref, bf16[1024,2048]{1,0:T(8,128)(2,1)} %cross_project.1.refs_5_.refs_6_.k_ref.v_ref, ...), custom_call_target="tpu_custom_call" | custom-call | flops 8589934592 | bytes 8388608 | tf_op jit(solution)/shard_map/cross_attend_grad/pallas_call | solution.py:476
  386.2 20.4 %enc_adapter_grad.1 = (bf16[1024,1024]{1,0:T(8,128)(2,1)}, f32[1024,1024]{1,0:T(8,128)}, bf16[1024,512]{1,0:T(8,128)(2,1)}, bf16[512,1024]{1,0:T(8,128)(2,1)}) custom-call(s32[1]{0:T(128)S(6)} %copy.36.refs_3_.refs_2_.refs_0_, bf16[1024,2048]{1,0:T(8,128)(2,1)} %get-tuple-element.87.refs_1_, bf16[1024,1024]{1,0:T(8,128)(2,1)} %refs_2_.10, ...), custom_call_target="tpu_custom_call" | custom-call | flops 8589934592 | bytes 27795456 | tf_op jit(solution)/shard_map/enc_adapter_grad/pallas_call | solution.py:255
  406.6 0.0 all-reduce.7.cloned.1.call-update
  406.6 0.0 all-reduce.5.cloned.1.call-start
  406.7 0.7 all-reduce.5.cloned.1.call-update
  407.4 31.0 %enc_hidden_grad.1 = (f32[1024,1024]{1,0:T(8,128)}, bf16[1024,1024]{1,0:T(8,128)(2,1)}) custom-call(s32[1]{0:T(128)S(6)} %copy.36.refs_3_.refs_2_.refs_0_, bf16[4096,1024]{1,0:T(8,128)(2,1)} %get-tuple-element.77.refs_5_.refs_1_, bf16[1024,4096]{1,0:T(8,128)(2,1)} %get-tuple-element.76.refs_4_.refs_2_, bf16[1024,1024]{1,0:T(8,128)(2,1)} %get-tuple-element.78.refs_1_.refs_3_, ...), custom_call_target="tpu_custom_call" | custom-call | flops 17179869184 | bytes 42471424 | tf_op jit(solution)/shard_map/enc_hidden_grad/pallas_call | solution.py:255
  438.4 39.0 %enc_attend_grad.1 = (bf16[1024,1024]{1,0:T(8,128)(2,1)}, bf16[1024,1024]{1,0:T(8,128)(2,1)}, bf16[1024,1024]{1,0:T(8,128)(2,1)}) custom-call(bf16[1024,3072]{1,0:T(8,128)(2,1)} %get-tuple-element.75.refs_3_.refs_4_.refs_5_.q_ref.k_ref.v_ref, bf16[1024,3072]{1,0:T(8,128)(2,1)} %get-tuple-element.75.refs_3_.refs_4_.refs_5_.q_ref.k_ref.v_ref, ...), custom_call_target="tpu_custom_call" | custom-call | flops 34359738368 | bytes 33554432 | tf_op jit(solution)/shard_map/enc_attend_grad/pallas_call | solution.py:476
  477.4 5.7 dec_middle_grad.1
  483.2 8.0 %dec_attend_grad.1 = (bf16[256,1024]{1,0:T(8,128)(2,1)}, bf16[256,1024]{1,0:T(8,128)(2,1)}, bf16[256,1024]{1,0:T(8,128)(2,1)}) custom-call(bf16[256,3072]{1,0:T(8,128)(2,1)} %dec_project.1.refs_1_.refs_2_.refs_3_.q_ref.k_ref.v_ref, bf16[256,3072]{1,0:T(8,128)(2,1)} %dec_project.1.refs_1_.refs_2_.refs_3_.q_ref.k_ref.v_ref, ...), custom_call_target="tpu_custom_call" | custom-call | flops 2147483648 | bytes 2097152 | tf_op jit(solution)/shard_map/dec_attend_grad/pallas_call | solution.py:476
  491.2 6.4 dec_input_grad.1
  497.5 12.7 %enc_input_grad.1 = f32[1024,1024]{1,0:T(8,128)} custom-call(s32[1]{0:T(128)S(6)} %copy.36.refs_3_.refs_2_.refs_0_, bf16[1024,3072]{1,0:T(8,128)(2,1)} %get-tuple-element.95.refs_1_, f32[1024,1024]{1,0:T(8,128)} %get-tuple-element.120.refs_2_, bf16[1024,1024]{1,0:T(8,128)(2,1)} %get-tuple-element.124.refs_3_, bf16[1024,1024]{1,0:T(8,128)(2,1)} %get-tuple-element.125.refs_4_, ...), custom_call_target="tpu_custom_call" | custom-call | flops 6442450944 | bytes 20971520 | tf_op jit(solution)/shard_map/enc_input_grad/pallas_call | solution.py:255
  510.3 29.8 %all-reduce.7.cloned.1.call-done = (bf16[1024,512]{1,0:T(8,128)(2,1)}, bf16[512,1024]{1,0:T(8,128)(2,1)}) async-done(((bf16[1024,512]{1,0:T(8,128)(2,1)}, bf16[512,1024]{1,0:T(8,128)(2,1)}), (bf16[1024,512]{1,0:T(8,128)(2,1)}, bf16[512,1024]{1,0:T(8,128)(2,1)})) %all-reduce.7.cloned.1.call-update) | async-done | bytes 2097168 | tf_op jit(solution)/shard_map/psum | solution.py:989
  540.1 0.0 copy-start.5
  540.1 2.9 convert_element_type.22
  543.0 0.0 copy-done.5
  543.0 1.6 convert_element_type.23
  544.6 144.7 %all-reduce.5.cloned.1.call-done = (f32[1024,512]{1,0:T(8,128)}, f32[520,1024]{1,0:T(8,128)}) async-done(((f32[1024,512]{1,0:T(8,128)}, f32[520,1024]{1,0:T(8,128)}), (f32[1024,512]{1,0:T(8,128)}, f32[520,1024]{1,0:T(8,128)})) %all-reduce.5.cloned.1.call-update) | async-done | bytes 4227088 | tf_op jit(solution)/shard_map/psum | solution.py:988
  689.3 0.9 slice_reduce_fusion
  690.1 1.3 fusion.1
  691.5 0.0 copy-start.3
  691.5 3.3 slice.40
  694.8 4.6 stack.3
  699.4 0.5 fusion
  699.9 0.0 copy-done.3
  699.9 0.0 copy-start.4
  699.9 1.3 copy.38
  701.3 1.0 copy-done.4
  702.3 1.3 copy.39
Async XLA Ops:
  7.2 5.7 copy-start
  7.2 532.9 %all-reduce.7.cloned.1.call-start = ((), (), s32[]{:S(2)}) async-start(), calls=%async_computation.1 | async-start | bytes 4194304 | tf_op jit(solution)/shard_map/psum | solution.py:989
  12.9 2.0 copy-start.1
  14.9 2.0 copy-start.2
  406.6 282.6 %all-reduce.5.cloned.1.call-start = ((), (), s32[]{:S(2)}) async-start(), calls=%async_computation | async-start | bytes 8454144 | tf_op jit(solution)/shard_map/psum | solution.py:988
  540.1 2.9 copy-start.5
  691.5 8.4 %copy-start.3 = (bf16[1024,1024]{1,0:T(8,128)(2,1)S(1)}, bf16[1024,1024]{1,0:T(8,128)(2,1)}, u32[]{:S(2)}) copy-start(bf16[1024,1024]{1,0:T(8,128)(2,1)} %get-tuple-element.161.refs_2_) | copy-start | bytes 6291460
  699.9 2.3 copy-start.4
Sparse Core Ops, SparseCore 0:
  406.7 133.2 all-reduce.6
  547.4 141.8 all-reduce.4

commit v2 on v1

--- a/solution.py
+++ b/solution.py
@@ -73,7 +73,7 @@
 
 
 UNIT_US = 5.8
-LEAD_US = 4.0
+LEAD_US = 5.0
 
 
 class Gather:
@@ -144,72 +144,17 @@
         self.transfer(unit, 2).wait_recv()
         self.transfer(unit, 6).start()
 
-    def arrived(self, unit):
-        for kind in (3, 4, 5, 6):
-            self.transfer(unit, kind).wait_recv()
-
-    def first(self, count):
-        for unit in range(count):
-            self.pass_on(unit)
-            if unit:
-                self.share(unit - 1)
-        self.share(count - 1)
-        for unit in range(count):
-            self.arrived(unit)
-        self.keep(0).wait()
-
-    def plan(self, skip, slots, steps, pace, lead):
-        acts = {}
-        for unit in range(skip, len(self.units)):
-            due = lead + LEAD_US + UNIT_US * (unit - skip + 1)
-            for act, at in ((self.pass_on, due), (self.share, due + UNIT_US + 2.0)):
-                tick = min(math.ceil(at / pace), steps * slots - 1)
-                acts.setdefault((tick // slots, tick % slots), []).append((act, unit))
-        return acts
-
-    def poll(self, acts, slot):
-        for (step, at), todo in acts.items():
-            if at == slot:
-
-                @pl.when(pl.program_id(0) == step)
-                def _(todo=todo):
-                    for act, unit in todo:
-                        act(unit)
-
-    def finish(self, skip):
+    def complete(self, m):
+        for unit, (of, _) in enumerate(self.units):
+            if of == m:
+                for kind in (3, 4, 5, 6):
+                    self.transfer(unit, kind).wait_recv()
+        self.keep(m).wait()
+
+    def finish(self):
         for unit in range(len(self.units)):
-            if unit >= skip:
-                self.arrived(unit)
             for kind in range(7):
                 self.transfer(unit, kind).wait_send()
-        for m in range(len(self.owns)):
-            if not (m == 0 and skip):
-                self.keep(m).wait()
-
-
-class Hosted:
-    def __init__(self, owns, skip_first=False, fsdp=8):
-        self.owns = list(owns)
-        self.fsdp = fsdp
-        self.splits = [max(1, a.size // 131072) for a in self.owns]
-        self.splits = [4 if a.shape == (128, 3072) else n for a, n in zip(self.owns, self.splits)]
-        self.skip = self.splits[0] if skip_first else 0
-
-    def out_shapes(self):
-        return [
-            jax.ShapeDtypeStruct((a.shape[0] * self.fsdp, a.shape[1]), a.dtype) for a in self.owns
-        ]
-
-    def scratch(self):
-        units = sum(self.splits)
-        return [
-            pltpu.SemaphoreType.DMA((units, 7)),
-            pltpu.SemaphoreType.DMA((units, 7)),
-            pltpu.SemaphoreType.DMA((len(self.owns),)),
-        ]
-
-    def run(self, own_refs, whole_refs, scratch):
-        return Gather(own_refs, whole_refs, self.splits, *scratch)
 
 
 ANY = pl.BlockSpec(memory_space=pl.ANY)
@@ -224,82 +169,206 @@
     return pl.BlockSpec(shape, lambda i: (0,) * len(shape))
 
 
-def hosted_call(body, name, grid, ins, outs, scratch, flops, moved, hosted=None, collective=None):
-    count = len(hosted.owns) if hosted else 0
+class Later:
+    def __init__(self, shape, dtype):
+        self.shape, self.dtype = tuple(shape), jnp.dtype(dtype)
+        self.size = math.prod(self.shape)
+
+
+class Recorder:
+    def __init__(self, blocks, fsdp):
+        self.names = list(blocks)
+        self.owns = list(blocks.values())
+        self.wholes = [Later((a.shape[0] * fsdp, a.shape[1]), a.dtype) for a in self.owns]
+        self.splits = [4 if a.shape[1] == 3072 else max(1, a.size // 131072) for a in self.owns]
+        self.stages = []
+
+    def add(self, **stage):
+        stage["results"] = [Later(shape, dtype) for shape, dtype, _ in stage["outs"]]
+        self.stages.append(stage)
+        return stage["results"]
+
+    def schedule(self):
+        acts, unit, due = [], 0, LEAD_US
+        last_of = {}
+        for m, split in enumerate(self.splits):
+            for _ in range(split):
+                time = UNIT_US * self.owns[m].size / split / 131072
+                due += time
+                acts.append((due, "pass_on", unit))
+                acts.append((due + time + 2.0, "share", unit))
+                last_of[m] = unit
+                unit += 1
+        acts.sort(key=lambda act: act[0])
+        clock, plans = 0.0, []
+        for stage in self.stages:
+            before, ticks = [], {}
+            needed = [last_of[self.wholes.index(mat)] for mat in stage["needs"]]
+            if needed:
+                while any(act[2] <= max(needed) for act in acts):
+                    clock = max(clock, acts[0][0])
+                    before.append(acts.pop(0)[1:])
+            pace = stage["time"] / stage["grid"][0] / stage["slots"]
+            for tick in range(stage["grid"][0] * stage["slots"]):
+                while acts and acts[0][0] <= clock:
+                    ticks.setdefault(divmod(tick, stage["slots"]), []).append(acts.pop(0)[1:])
+                clock += pace
+            plans.append((before, ticks))
+        return plans, [act[1:] for act in acts]
+
+    def run(self):
+        given = []
+        for stage in self.stages:
+            for array, spec in stage["ins"]:
+                if not isinstance(array, Later) and not any(array is g for g, _ in given):
+                    given.append((array, SCALAR if spec is SCALAR else ANY))
+        results = self.wholes + [r for stage in self.stages for r in stage["results"]]
+        plans, left = self.schedule()
+        units = sum(self.splits)
+
+        def kernel(*refs):
+            refs = list(refs)
+            owns = refs[: len(self.owns)]
+            of = {}
+            for (array, _), ref in zip(given, refs[len(self.owns) :]):
+                of[id(array)] = ref
+            rest = refs[len(self.owns) + len(given) :]
+            for result, ref in zip(results, rest):
+                of[id(result)] = ref
+            gather = Gather(owns, [of[id(w)] for w in self.wholes], self.splits, *rest[len(results) :])
+            gather.begin()
+            waited = set()
+
+            def act(kind, unit):
+                getattr(gather, kind)(unit)
+
+            for stage, (before, ticks) in zip(self.stages, plans):
+                for kind, unit in before:
+                    act(kind, unit)
+                for mat in stage["needs"]:
+                    m = self.wholes.index(mat)
+                    if m not in waited:
+                        waited.add(m)
+                        gather.complete(m)
+                self.run_stage(stage, ticks, act, of)
+            for kind, unit in left:
+                act(kind, unit)
+            for m in range(len(self.owns)):
+                if m not in waited:
+                    gather.complete(m)
+            gather.finish()
+
+        out = pl.pallas_call(
+            kernel,
+            in_specs=[ANY] * len(self.owns) + [spec for _, spec in given],
+            out_specs=[ANY] * len(results),
+            scratch_shapes=[
+                pltpu.SemaphoreType.DMA((units, 7)),
+                pltpu.SemaphoreType.DMA((units, 7)),
+                pltpu.SemaphoreType.DMA((len(self.owns),)),
+            ],
+            out_shape=[jax.ShapeDtypeStruct(r.shape, r.dtype) for r in results],
+            compiler_params=pltpu.CompilerParams(
+                vmem_limit_bytes=VMEM_BYTES, collective_id=1, has_side_effects=True
+            ),
+            name="forward",
+        )(*self.owns, *[array for array, _ in given])
+        arrays = {id(result): array for result, array in zip(results, out)}
+        return lambda later: arrays[id(later)]
+
+    def run_stage(self, stage, ticks, act, of):
+        ins, outs = stage["ins"], stage["outs"]
+        piped = [at for at, (_, spec) in enumerate(ins) if spec is not ANY and spec is not SCALAR]
+        fixed = {at: of[id(a)] for at, (a, _) in enumerate(ins) if at not in piped}
+
+        def poll(slot):
+            for (step, at), todo in ticks.items():
+                if at == slot:
+
+                    @pl.when(pl.program_id(0) == step)
+                    def _(todo=todo):
+                        for kind, unit in todo:
+                            act(kind, unit)
+
+        def scoped(*scratch):
+            if stage["prepare"]:
+                stage["prepare"]([fixed.get(at) for at in range(len(ins))], scratch)
+
+            def body(*blocks):
+                in_refs = [fixed.get(at) for at in range(len(ins))]
+                for at, ref in zip(piped, blocks):
+                    in_refs[at] = ref
+                stage["body"](in_refs, list(blocks[len(piped) :]), scratch, poll)
+
+            pltpu.emit_pipeline(
+                body,
+                grid=stage["grid"],
+                in_specs=[ins[at][1] for at in piped],
+                out_specs=[spec for _, _, spec in outs],
+            )(*[of[id(ins[at][0])] for at in piped], *[of[id(r)] for r in stage["results"]])
+
+        pl.run_scoped(scoped, *stage["scratch"])
+
+
+def launch(
+    body, name, grid, ins, outs, scratch, flops, moved, recorder=None, prepare=None, needs=(),
+    slots=1, time=1.0,
+):
+    if recorder is not None:
+        return recorder.add(
+            body=body, grid=grid, ins=ins, outs=outs, scratch=scratch, prepare=prepare, needs=needs,
+            slots=slots, time=time,
+        )
 
     def kernel(*refs):
-        refs = list(refs)
-
-        def take(n):
-            taken = refs[:n]
-            del refs[:n]
-            return taken
-
-        own_refs, in_refs, whole_refs, out_refs = take(count), take(len(ins)), take(count), take(len(outs))
-        gather = None
-        if hosted:
-            gather = hosted.run(own_refs, whole_refs, refs[-3:])
-            refs = refs[:-3]
+        in_refs, out_refs = list(refs[: len(ins)]), list(refs[len(ins) : len(ins) + len(outs)])
+        rest = refs[len(ins) + len(outs) :]
+        if prepare:
 
             @pl.when(pl.program_id(0) == 0)
             def _():
-                gather.begin()
-
-        body(in_refs, out_refs, refs, gather)
-        if hosted:
-
-            @pl.when(pl.program_id(0) == grid[0] - 1)
-            def _():
-                gather.finish(hosted.skip)
-
-    out = pl.pallas_call(
+                prepare(in_refs, rest)
+
+        body(in_refs, out_refs, rest, lambda slot: None)
+
+    return pl.pallas_call(
         kernel,
         grid=grid,
-        in_specs=[ANY] * count + [s for _, s in ins],
-        out_specs=[ANY] * count + [s for _, _, s in outs],
-        scratch_shapes=[*scratch, *(hosted.scratch() if hosted else [])],
-        out_shape=(hosted.out_shapes() if hosted else [])
-        + [jax.ShapeDtypeStruct(s, d) for s, d, _ in outs],
-        compiler_params=pltpu.CompilerParams(
-            vmem_limit_bytes=VMEM_BYTES,
-            **({"collective_id": collective, "has_side_effects": True} if hosted else {}),
-        ),
+        in_specs=[spec for _, spec in ins],
+        out_specs=[spec for _, _, spec in outs],
+        scratch_shapes=scratch,
+        out_shape=[jax.ShapeDtypeStruct(s, d) for s, d, _ in outs],
+        compiler_params=pltpu.CompilerParams(vmem_limit_bytes=VMEM_BYTES),
         cost_estimate=pl.CostEstimate(flops=flops, bytes_accessed=moved, transcendentals=0),
         name=name,
-    )(*(hosted.owns if hosted else []), *[a for a, _ in ins])
-    return list(out[count:]), list(out[:count])
-
-
-def staged_call(
-    body, name, grid, limit, mats, ins, outs, scratch=(), flops=0, hosted=None, collective=None
-):
+    )(*[a for a, _ in ins])
+
+
+def staged_call(body, name, grid, limit, mats, ins, outs, scratch=(), flops=0, **record):
     holders = []
     for mat, chunks in mats:
-        like = hosted.out_shapes()[0] if mat is None else mat
-        holders.append(pltpu.VMEM(like.shape, like.dtype))
+        holders.append(pltpu.VMEM(mat.shape, mat.dtype))
         holders.append(pltpu.SemaphoreType.DMA((chunks,)))
-    given = [mat for mat, _ in mats if mat is not None]
-
-    def staged(in_refs, out_refs, rest, gather):
-        sources = list(in_refs[1 : 1 + len(given)])
-        fetches = []
-        for at, (mat, chunks) in enumerate(mats):
-            source = gather.wholes[0] if mat is None else sources.pop(0)
-            fetches.append(Fetch(source, rest[2 * at], rest[2 * at + 1], chunks))
-
-        @pl.when(pl.program_id(0) == 0)
-        def _():
-            for fetch, (mat, _) in zip(fetches, mats):
-                if mat is not None:
-                    fetch.start()
-
-        args = (in_refs[0], fetches, in_refs[1 + len(given) :], out_refs, rest[2 * len(mats) :])
-        body(*args, gather)
+    given = [mat for mat, _ in mats]
+
+    def fetches(in_refs, rest):
+        return [
+            Fetch(in_refs[1 + at], rest[2 * at], rest[2 * at + 1], chunks)
+            for at, (_, chunks) in enumerate(mats)
+        ]
+
+    def prepare(in_refs, rest):
+        for fetch in fetches(in_refs, rest):
+            fetch.start()
+
+    def staged(in_refs, out_refs, rest, poll):
+        args = (in_refs[0], fetches(in_refs, rest), in_refs[1 + len(given) :], out_refs)
+        body(*args, rest[2 * len(mats) :], poll)
 
     moved = sum(a.size * a.dtype.itemsize for a in given)
     moved += sum(a.size * a.dtype.itemsize for a, _ in ins)
     moved += sum(math.prod(s) * jnp.dtype(d).itemsize for s, d, _ in outs)
-    return hosted_call(
+    return launch(
         staged,
         name,
         grid,
@@ -308,35 +377,28 @@
         [*holders, *scratch],
         flops,
         moved,
-        hosted,
-        collective,
-    )
-
-
-def project(name, limit, rows_in, mat, width, chunks, hosted=None, collective=None):
+        prepare=prepare,
+        needs=given if record else (),
+        **record,
+    )
+
+
+def project(name, limit, rows_in, mat, chunks, **record):
     total, depth = rows_in.shape
+    width = mat.shape[1]
     block = min(256, total)
     step = width // chunks
 
-    def body(limit, fetches, ins, outs, extra, gather):
+    def body(limit, fetches, ins, outs, extra, poll):
         (fetch,) = fetches
-        acts = gather.plan(hosted.skip, chunks, total // block, 1.1, 0.0) if gather else {}
-        if gather and mat is None:
-
-            @pl.when(pl.program_id(0) == 0)
-            def _():
-                gather.first(hosted.skip)
-                fetch.start()
-
         left = ins[0][...]
         for chunk in range(chunks):
-            if gather:
-                gather.poll(acts, chunk)
+            poll(chunk)
             fetch.wait(chunk)
             columns = slice(chunk * step, (chunk + 1) * step)
             outs[0][:, columns] = nn(left, fetch.whole[:, columns]).astype(BF16)
 
-    outs, wholes = staged_call(
+    return staged_call(
         body,
         name,
         (total // block,),
@@ -345,21 +407,18 @@
         [(rows_in, rows_spec(block, depth))],
         [((total, width), BF16, rows_spec(block, width))],
         flops=2 * total * depth * width,
-        hosted=hosted,
-        collective=collective,
-    )
-    return outs[0], wholes
-
-
-def attend(name, limit, queries, keys, values, causal, hosted=None, collective=None, pace=3.3):
+        **record,
+    )[0]
+
+
+def attend(name, limit, queries, keys, values, causal, **record):
     q_len, k_len = queries[0].shape[0], keys[0].shape[0]
     pairs = 1024 // PAIR
     step = min(256, q_len)
 
-    def body(ins, outs, extra, gather):
+    def body(ins, outs, extra, poll):
         limit_ref, q_ref, k_ref, v_ref = ins
         e_ref, o_ref, inv_ref = outs
-        acts = gather.plan(0, 2, pairs, pace, 0.0) if gather else {}
         lanes = lax.broadcasted_iota(jnp.int32, (1, PAIR), 1)
         places = lax.broadcasted_iota(jnp.int32, (k_len, 1), 0)
         bias = jnp.where(places < limit_ref[0], 0.0, -1000000000.0)
@@ -368,8 +427,7 @@
         v_two = v_ref[...].astype(F32)
         mixed = []
         for half in range(2):
-            if gather:
-                gather.poll(acts, half)
+            poll(half)
             own = (lanes >= HEAD * half) & (lanes < HEAD * (half + 1))
             spare = lanes == HEAD * (1 - half)
             q_own = jnp.where(own, q_two, jnp.where(spare, 1.0, 0.0)).astype(BF16)
@@ -398,7 +456,7 @@
     def columns(rows, first):
         return pl.BlockSpec((rows, PAIR), lambda i: (0, first + i))
 
-    outs, wholes = hosted_call(
+    return launch(
         body,
         name,
         (pairs,),
@@ -420,10 +478,8 @@
         [],
         16 * pairs * q_len * k_len * PAIR,
         4 * pairs * q_len * k_len,
-        hosted,
-        collective,
-    )
-    return *outs, wholes
+        **record,
+    )
 
 
 def attend_grad(name, queries, keys, values, weights, mixture, inverse, upstream):
@@ -524,12 +580,13 @@
     return jnp.broadcast_to(column, (column.shape[0], 128))
 
 
-def out_norm(name, limit, mixture, residual, gain, mat, next_mat=None, residual_gain=None):
+def out_norm(name, limit, mixture, residual, gain, mat, next_mat=None, residual_gain=None, **record):
     total, width = mixture.shape
     block = min(256, total)
     mats = [(mat, 1)] + ([] if next_mat is None else [(next_mat, 1)])
 
-    def body(limit, fetches, ins, outs, extra, gather):
+    def body(limit, fetches, ins, outs, extra, poll):
+        poll(0)
         o_ref, r_ref, g_ref, rg_ref = ins
         fetches[0].wait_all()
         added = nn(o_ref[...], fetches[0].whole[...])
@@ -566,13 +623,11 @@
         ],
         outs,
         flops=2 * total * width * width * len(mats),
-    )[0]
-
-
-def branch(
-    name, limit, unit, gain, gain_out, w_in, w_back, down_low, up_low,
-    hosted=None, collective=None, pace=2.4,
-):
+        **record,
+    )
+
+
+def branch(name, limit, unit, gain, gain_out, w_in, w_back, down_low, up_low, **record):
     total, width = unit.shape
     hidden_units = w_in.shape[1]
     adapter = down_low.shape[1]
@@ -580,23 +635,21 @@
     chunks = 4
     step = hidden_units // chunks
 
-    def body(limit, fetches, ins, outs, extra, gather):
+    def body(limit, fetches, ins, outs, extra, poll):
         u_ref, g_ref, go_ref, ad_ref, au_ref = ins
         y_ref, unit_ref, inv_ref, slope_ref, wa_ref, ad_slope_ref, sq_ref = outs
         (act,) = extra
         first, second = fetches
         hidden = u_ref[...].astype(F32) * g_ref[...]
         low = hidden.astype(BF16)
-        pre = nn(low, ad_ref[...])
+        pre = nn(low, ad_ref[...].astype(BF16))
         gate = jax.nn.sigmoid(pre)
         wa = (pre * gate).astype(BF16)
         wa_ref[...] = wa
         ad_slope_ref[...] = (gate * (1.0 + pre * (1.0 - gate))).astype(BF16)
-        adapted = 4.0 * nn(wa, au_ref[...])
-        acts = gather.plan(0, chunks, total // block, pace, 0.0) if gather else {}
+        adapted = 4.0 * nn(wa, au_ref[...].astype(BF16))
         for chunk in range(chunks):
-            if gather:
-                gather.poll(acts, chunk)
+            poll(chunk)
             first.wait(chunk)
             columns = slice(chunk * step, (chunk + 1) * step)
             fp = nn(low, first.whole[:, columns])
@@ -615,7 +668,7 @@
         add_squares(sq_ref, 0, added, mask)
         add_squares(sq_ref, 1, result, mask)
 
-    outs, wholes = staged_call(
+    return staged_call(
         body,
         name,
         (total // block,),
@@ -639,10 +692,8 @@
         ],
         scratch=[pltpu.VMEM((block, hidden_units), BF16)],
         flops=4 * total * width * (hidden_units + adapter),
-        hosted=hosted,
-        collective=collective,
-    )
-    return *outs, wholes
+        **record,
+    )
 
 
 def adapter_grad(upstream, refs):
@@ -650,8 +701,8 @@
     grad_two = standardize_grad(uo_ref[...].astype(F32), io_ref[:, 0:1], upstream * go_ref[...])
     dvd = (4.0 * grad_two).astype(BF16)
     low = (ui_ref[...].astype(F32) * gi_ref[...]).astype(BF16)
-    du = (nt(dvd, au_ref[...]) * as_ref[...].astype(F32)).astype(BF16)
-    total = grad_two + nt(du, ad_ref[...])
+    du = (nt(dvd, au_ref[...].astype(BF16)) * as_ref[...].astype(F32)).astype(BF16)
+    total = grad_two + nt(du, ad_ref[...].astype(BF16))
     return grad_two.astype(BF16), total, tn(low, du), tn(wa_ref[...], dvd)
 
 
@@ -683,7 +734,7 @@
         up_low, slope, saved_in[1], *squares,
     ]
 
-    def body(limit, fetches, ins, outs, extra, gather):
+    def body(limit, fetches, ins, outs, extra, poll):
         grad_ref, mix_ref, down_ref, up_ref = outs
         (other,), cot_ref, slope_ref, ii_ref = ins[:1], ins[1], ins[11], ins[12]
         dz, part, down_ref[...], up_ref[:adapter] = adapter_grad(cot_ref[...].astype(F32), ins[2:11])
@@ -710,7 +761,7 @@
         ],
         scratch=[pltpu.VMEM((total, hidden_units), BF16)],
         flops=4 * total * width * (hidden_units + 2 * adapter),
-    )[0]
+    )
 
 
 def enc_adapter_grad(
@@ -722,7 +773,7 @@
     block = min(256, total)
     rows = rows_spec(block, width)
 
-    def body(limit, fetches, ins, outs, extra, gather):
+    def body(limit, fetches, ins, outs, extra, poll):
         dz_ref, part_ref, down_ref, up_ref = outs
         down_sum, up_sum = extra
         fetches[0].wait_all()
@@ -775,7 +826,7 @@
         ],
         scratch=[pltpu.VMEM(down_low.shape, F32), pltpu.VMEM(up_low.shape, F32)],
         flops=4 * total * width * (width + 2 * adapter),
-    )[0]
+    )
 
 
 def enc_hidden_grad(name, limit, dz, part, slope, saved_in, gain_in, w_back, w_in, w_out):
@@ -784,7 +835,7 @@
     block = min(256, total)
     rows = rows_spec(block, width)
 
-    def body(limit, fetches, ins, outs, extra, gather):
+    def body(limit, fetches, ins, outs, extra, poll):
         outs[0][...], outs[1][...] = hidden_grad(
             ins[0][...], ins[1][...], fetches, ins[2:], extra[0], 4
         )
@@ -806,7 +857,7 @@
         [((total, width), F32, rows), ((total, width), BF16, rows)],
         scratch=[pltpu.VMEM((block, hidden_units), BF16)],
         flops=4 * total * width * hidden_units,
-    )[0]
+    )
 
 
 def middle_grad(name, limit, grad_cross, dq, saved, gain, w_cq, w_so):
@@ -814,7 +865,7 @@
     block = min(256, total)
     unit, inv = saved
 
-    def body(limit, fetches, ins, outs, extra, gather):
+    def body(limit, fetches, ins, outs, extra, poll):
         gc_ref, dq_ref, u_ref, i_ref, g_ref = ins
         fetches[0].wait_all()
         hidden_grad = gc_ref[...] + nt(dq_ref[...], fetches[0].whole[...])
@@ -843,7 +894,7 @@
             ((total, width), BF16, rows_spec(block, width)),
         ],
         flops=4 * total * width * width,
-    )[0]
+    )
 
 
 def input_grad(name, limit, base, parts, mat):
@@ -851,7 +902,7 @@
     block = min(256, total)
     count = len(parts)
 
-    def body(limit, fetches, ins, outs, extra, gather):
+    def body(limit, fetches, ins, outs, extra, poll):
         (fetch,) = fetches
         result = ins[0][...]
         for at in range(count):
@@ -868,7 +919,7 @@
         [(base, rows_spec(block, width))] + [(p, rows_spec(block, width)) for p in parts],
         [((total, width), F32, rows_spec(block, width))],
         flops=2 * total * width * width * count,
-    )[0][0]
+    )[0]
 
 
 NAMES = (
@@ -886,63 +937,68 @@
 )
 
 
-class Weights(dict):
-    def __init__(self, blocks, hosting, fsdp):
-        super().__init__()
-        self.blocks, self.hosting, self.fsdp = blocks, hosting, fsdp
-        if not hosting:
-            for name, block in blocks.items():
-                self[name] = lax.all_gather(block, "fsdp", axis=0, tiled=True)
-
-    def host(self, collective, *names, skip_first=False):
-        self.names = names
-        if not self.hosting:
-            return {}
-        owns = [self.blocks[name] for name in names]
-        return {"hosted": Hosted(owns, skip_first, self.fsdp), "collective": collective}
-
-    def take(self, wholes):
-        self.update(zip(self.names, wholes))
-
-
-def layers(enc_limit, dec_limit, enc_input, dec_input, enc_cot, dec_cot, w, gains, adapters):
+def layers(enc_limit, dec_limit, enc_input, dec_input, enc_cot, dec_cot, blocks, hosting, fsdp, gains, adapters):
     gain = [gains[k : k + 1] for k in range(5)]
-    enc_down, enc_up, dec_down, dec_up = (a.astype(BF16) for a in adapters)
-    host = w.host(1, "enc_qkv", "enc_attn_out", "dec_self_out", skip_first=True)
-    qkv, wholes = project("enc_project", enc_limit, enc_input, w.get("enc_qkv"), 3072, 3, **host)
-    w.take(wholes)
-    host = w.host(2, "enc_ffn_in", "enc_ffn_out")
-    e_enc, o_enc, inv_enc, wholes = attend(
-        "enc_attend", enc_limit, (qkv, 0), (qkv, 8), (qkv, 16), False, **host
-    )
-    w.take(wholes)
-    unit1, dev1, sq_a = out_norm("enc_out_norm", enc_limit, o_enc, enc_input, gain[0], w["enc_attn_out"])
-    host = w.host(3, "dec_self_qkv", "dec_cross_kv", "dec_cross_q")
-    enc_out, unit2, dev2, slope_e, wa_e, ads_e, sq_b, wholes = branch(
+    enc_down, enc_up, dec_down, dec_up = adapters
+    if hosting:
+        recorder = Recorder(blocks, fsdp)
+        w = dict(zip(recorder.names, recorder.wholes))
+    else:
+        recorder = None
+        w = {name: lax.all_gather(b, "fsdp", axis=0, tiled=True) for name, b in blocks.items()}
+
+    def at(slots, time):
+        return {"recorder": recorder, "slots": slots, "time": time} if hosting else {}
+
+    qkv = project("enc_project", enc_limit, enc_input, w["enc_qkv"], 3, **at(3, 13.0))
+    e_enc, o_enc, inv_enc = attend(
+        "enc_attend", enc_limit, (qkv, 0), (qkv, 8), (qkv, 16), False, **at(2, 53.0)
+    )
+    unit1, dev1, sq_a = out_norm(
+        "enc_out_norm", enc_limit, o_enc, enc_input, gain[0], w["enc_attn_out"], **at(1, 9.0)
+    )
+    enc_out, unit2, dev2, slope_e, wa_e, ads_e, sq_b = branch(
         "enc_branch", enc_limit, unit1, gain[0], gain[1], w["enc_ffn_in"], w["enc_ffn_out"],
-        enc_down, enc_up, **host,
-    )
-    w.take(wholes)
-    sqkv, _ = project("dec_project", dec_limit, dec_input, w["dec_self_qkv"], 3072, 3)
-    e_self, o_self, inv_self, _ = attend(
-        "dec_attend", dec_limit, (sqkv, 0), (sqkv, 8), (sqkv, 16), True
+        enc_down, enc_up, **at(4, 38.0),
+    )
+    sqkv = project("dec_project", dec_limit, dec_input, w["dec_self_qkv"], 3, **at(3, 6.0))
+    e_self, o_self, inv_self = attend(
+        "dec_attend", dec_limit, (sqkv, 0), (sqkv, 8), (sqkv, 16), True, **at(2, 8.5)
     )
     unit3, dev3, sq_c, cross_q = out_norm(
-        "dec_out_norm", dec_limit, o_self, dec_input, gain[2], w["dec_self_out"], w["dec_cross_q"]
-    )
-    kv, _ = project("cross_project", enc_limit, enc_out, w["dec_cross_kv"], 2048, 2)
-    host = w.host(4, "dec_cross_out", "dec_ffn_in", "dec_ffn_out")
-    e_cross, o_cross, inv_cross, wholes = attend(
-        "cross_attend", enc_limit, (cross_q, 0), (kv, 0), (kv, 8), False, pace=1.0, **host
-    )
-    w.take(wholes)
+        "dec_out_norm", dec_limit, o_self, dec_input, gain[2], w["dec_self_out"], w["dec_cross_q"],
+        **at(1, 5.3),
+    )
+    kv = project("cross_project", enc_limit, enc_out, w["dec_cross_kv"], 2, **at(2, 9.5))
+    e_cross, o_cross, inv_cross = attend(
+        "cross_attend", enc_limit, (cross_q, 0), (kv, 0), (kv, 8), False, **at(2, 16.0)
+    )
     unit4, dev4, sq_d = out_norm(
-        "cross_out_norm", dec_limit, o_cross, unit3, gain[3], w["dec_cross_out"], residual_gain=gain[2]
-    )
-    dec_out, unit5, dev5, slope_d, wa_d, ads_d, sq_e, _ = branch(
+        "cross_out_norm", dec_limit, o_cross, unit3, gain[3], w["dec_cross_out"],
+        residual_gain=gain[2], **at(1, 4.6),
+    )
+    dec_out, unit5, dev5, slope_d, wa_d, ads_d, sq_e = branch(
         "dec_branch", dec_limit, unit4, gain[3], gain[4], w["dec_ffn_in"], w["dec_ffn_out"],
-        dec_down, dec_up,
-    )
+        dec_down, dec_up, **at(4, 11.4),
+    )
+    if hosting:
+        value = recorder.run()
+        w = {name: value(mat) for name, mat in w.items()}
+        qkv, e_enc, o_enc, inv_enc, unit1, dev1, sq_a = map(
+            value, (qkv, e_enc, o_enc, inv_enc, unit1, dev1, sq_a)
+        )
+        enc_out, unit2, dev2, slope_e, wa_e, ads_e, sq_b = map(
+            value, (enc_out, unit2, dev2, slope_e, wa_e, ads_e, sq_b)
+        )
+        sqkv, e_self, o_self, inv_self, unit3, dev3, sq_c, cross_q = map(
+            value, (sqkv, e_self, o_self, inv_self, unit3, dev3, sq_c, cross_q)
+        )
+        kv, e_cross, o_cross, inv_cross, unit4, dev4, sq_d = map(
+            value, (kv, e_cross, o_cross, inv_cross, unit4, dev4, sq_d)
+        )
+        dec_out, unit5, dev5, slope_d, wa_d, ads_d, sq_e = map(
+            value, (dec_out, unit5, dev5, slope_d, wa_d, ads_d, sq_e)
+        )
     grad_cross, do_cross, dec_down_grad, dec_up_grad = dec_branch_grad(
         "dec_branch_grad", (enc_limit, dec_limit), dec_cot, (unit5, dev5), gain[4], (unit4, dev4), gain[3],
         slope_d, wa_d, ads_d, w["dec_ffn_out"], w["dec_ffn_in"], w["dec_cross_out"], dec_down, dec_up,
@@ -979,10 +1035,9 @@
 
 def shards(fsdp, dp, enc_input, dec_input, enc_cot, dec_cot, *rest):
     mats, (gains, enc_down, enc_up, dec_down, dec_up, enc_lengths, dec_lengths) = rest[:11], rest[11:]
-    weights = Weights(dict(zip(NAMES, mats)), fsdp == 8 and dp % 2 == 0, fsdp)
     results, enc_grads, dec_grads = layers(
-        enc_lengths, dec_lengths, enc_input, dec_input, enc_cot, dec_cot, weights, gains,
-        (enc_down, enc_up, dec_down, dec_up),
+        enc_lengths, dec_lengths, enc_input, dec_input, enc_cot, dec_cot, dict(zip(NAMES, mats)),
+        fsdp == 8 and dp % 2 == 0, fsdp, gains, (enc_down, enc_up, dec_down, dec_up),
     )
     everyone = ("fsdp", "dp")
     dec_down_grad, dec_up_grad = lax.psum(dec_grads, everyone)

time: 720 us -> 629 us (0.87)
  Pallas kernels: 491 us -> 407 us
    pallas_call x17 -> x7, Pallas kernels: 431 us -> 346 us  [the longest x1 255 us: run(): pl.pallas_call(kernel, in_specs=[ANY] * len(self.owns) + [spec for _, spe...]
  transfers between devices with their start and end apart: 2 -> 2, of which waited for: 2 -> 2; matrix products, arithmetic and copies ran while one was open for 1% -> 1% of each run, Pallas kernels for 14% -> 17%
where the time goes in v2:
time: 629 us; the launch traced here: 620 us
  Pallas kernels  407 us (65%)
  waiting for transfers between devices  177 us (28%)
  between operations  15.6 us (2%)
  local copies, waits for them, and re-layouts  14.8 us (2%)
    pallas_call x1, Pallas kernels, run(): pl.pallas_call(kernel, in_specs=[ANY] * len(self.owns) + [spec for _, spe...  255 us
    psum x1, waiting for transfers between devices, shards(): dec_down_grad, dec_up_grad = lax.psum(dec_grads, everyone)  145 us
    pallas_call x6, Pallas kernels, launch(): pl.pallas_call(kernel, grid=grid, in_specs=[spec for _, spec in ins], out...  91.7 us
    pallas_call x3, Pallas kernels, attend_grad(): pl.pallas_call(kernel, grid=(pairs,), in_specs=[columns(q_len, queries[1]...  60.1 us
    psum x1, waiting for transfers between devices, shards(): enc_down_grad, enc_up_grad = lax.psum(enc_grads, everyone)  32 us
  transfers between devices with their start and end apart: 2, of which 2 were waited for; matrix products, arithmetic and copies ran while one was open for 1% of the time, Pallas kernels for 17%

profile of v2, /device:TPU:0, one launch (start us, length us, event | category | flops | bytes accessed | tf_op | source)
XLA Modules:
  0.0 620.3 jit_solution(839539514597761197)
XLA Ops:
  7.2 0.0 all-reduce.7.cloned.1.call-start
  8.5 1.6 fusion.2
  10.1 254.8 %forward.1 = (bf16[1024,3072]{1,0:T(8,128)(2,1)}, bf16[1024,1024]{1,0:T(8,128)(2,1)}, bf16[1024,4096]{1,0:T(8,128)(2,1)}, bf16[4096,1024]{1,0:T(8,128)(2,1)}, bf...) custom-call(bf16[128,3072]{1,0:T(8,128)(2,1)} %refs_0_.7, ...), custom_call_target="tpu_custom_call" | custom-call | tf_op jit(solution)/shard_map/forward/pallas_call | solution.py:261
  264.9 14.9 %dec_branch_grad.1 = (f32[256,1024]{1,0:T(8,128)}, bf16[256,1024]{1,0:T(8,128)(2,1)}, f32[1024,512]{1,0:T(8,128)}, f32[520,1024]{1,0:T(8,128)}) custom-call(s32[1]{0:T(128)S(6)} %copy.37.refs_11_.refs_0_, bf16[4096,1024]{1,0:T(8,128)(2,1)} %get-tuple-element.89.refs_1_, bf16[1024,4096]{1,0:T(8,128)(2,1)} %get-tuple-element.90.refs_2_, ...), custom_call_target="tpu_custom_call" | custom-call | flops 5368709120 | bytes 33497092 | tf_op jit(solution)/shard_map/dec_branch_grad/pallas_call | solution.py:334
  279.7 13.0 %cross_attend_grad.1 = (bf16[256,1024]{1,0:T(8,128)(2,1)}, bf16[1024,1024]{1,0:T(8,128)(2,1)}, bf16[1024,1024]{1,0:T(8,128)(2,1)}) custom-call(bf16[256,1024]{1,0:T(8,128)(2,1)} %get-tuple-element.84.q_ref, bf16[1024,2048]{1,0:T(8,128)(2,1)} %get-tuple-element.85.k_ref.v_ref, bf16[1024,2048]{1,0:T(8,128)(2,1)} %get-tuple-element.85.k_ref.v_ref, ...), custom_call_target="tpu_custom_call" | custom-call | flops 8589934592 | bytes 8388608 | tf_op jit(solution)/shard_map/cross_attend_grad/pallas_call | solution.py:532
  292.7 21.0 %enc_adapter_grad.1 = (bf16[1024,1024]{1,0:T(8,128)(2,1)}, f32[1024,1024]{1,0:T(8,128)}, bf16[1024,512]{1,0:T(8,128)(2,1)}, bf16[512,1024]{1,0:T(8,128)(2,1)}) custom-call(s32[1]{0:T(128)S(6)} %copy.37.refs_11_.refs_0_, bf16[1024,2048]{1,0:T(8,128)(2,1)} %get-tuple-element.83.refs_1_, bf16[1024,1024]{1,0:T(8,128)(2,1)} %refs_2_.3, ...), custom_call_target="tpu_custom_call" | custom-call | flops 8589934592 | bytes 29892608 | tf_op jit(solution)/shard_map/enc_adapter_grad/pallas_call | solution.py:334
  313.7 0.0 all-reduce.7.cloned.1.call-update
  313.7 0.0 all-reduce.5.cloned.1.call-start
  313.8 0.7 all-reduce.5.cloned.1.call-update
  314.5 31.0 %enc_hidden_grad.1 = (f32[1024,1024]{1,0:T(8,128)}, bf16[1024,1024]{1,0:T(8,128)(2,1)}) custom-call(s32[1]{0:T(128)S(6)} %copy.37.refs_11_.refs_0_, bf16[4096,1024]{1,0:T(8,128)(2,1)} %get-tuple-element.80.refs_1_, bf16[1024,4096]{1,0:T(8,128)(2,1)} %get-tuple-element.81.refs_2_, bf16[1024,1024]{1,0:T(8,128)(2,1)} %get-tuple-element.82.refs_3_, ...), custom_call_target="tpu_custom_call" | custom-call | flops 17179869184 | bytes 42471424 | tf_op jit(solution)/shard_map/enc_hidden_grad/pallas_call | solution.py:334
  345.5 39.1 %enc_attend_grad.1 = (bf16[1024,1024]{1,0:T(8,128)(2,1)}, bf16[1024,1024]{1,0:T(8,128)(2,1)}, bf16[1024,1024]{1,0:T(8,128)(2,1)}) custom-call(bf16[1024,3072]{1,0:T(8,128)(2,1)} %get-tuple-element.117.q_ref.k_ref.v_ref, bf16[1024,3072]{1,0:T(8,128)(2,1)} %get-tuple-element.117.q_ref.k_ref.v_ref, bf16[1024,3072]{1,0:T(8,128)(2,1)} %get-tuple-element.117.q_ref.k_ref.v_ref, ...), custom_call_target="tpu_custom_call" | custom-call | flops 34359738368 | bytes 33554432 | tf_op jit(solution)/shard_map/enc_attend_grad/pallas_call | solution.py:532
  384.6 5.7 dec_middle_grad.1
  390.3 8.0 %dec_attend_grad.1 = (bf16[256,1024]{1,0:T(8,128)(2,1)}, bf16[256,1024]{1,0:T(8,128)(2,1)}, bf16[256,1024]{1,0:T(8,128)(2,1)}) custom-call(bf16[256,3072]{1,0:T(8,128)(2,1)} %get-tuple-element.133.q_ref.k_ref.v_ref, bf16[256,3072]{1,0:T(8,128)(2,1)} %get-tuple-element.133.q_ref.k_ref.v_ref, bf16[256,3072]{1,0:T(8,128)(2,1)} %get-tuple-element.133.q_ref.k_ref.v_ref, ...), custom_call_target="tpu_custom_call" | custom-call | flops 2147483648 | bytes 2097152 | tf_op jit(solution)/shard_map/dec_attend_grad/pallas_call | solution.py:532
  398.3 6.3 %dec_input_grad.1 = f32[256,1024]{1,0:T(8,128)} custom-call(s32[1]{0:T(128)S(6)} %copy.38.refs_17_.refs_4_.refs_0_, bf16[1024,3072]{1,0:T(8,128)(2,1)} %get-tuple-element.125.refs_1_, f32[256,1024]{1,0:T(8,128)} %get-tuple-element.132.refs_2_, bf16[256,1024]{1,0:T(8,128)(2,1)} %get-tuple-element.138.refs_3_, bf16[256,1024]{1,0:T(8,128)(2,1)} %get-tuple-element.139.refs_4_, ...), custom_call_target="tpu_custom_call" | custom-call | flops 1610612736 | bytes 9961472 | tf_op jit(solution)/shard_map/dec_input_grad/pallas_call | solution.py:334
  404.6 12.8 %enc_input_grad.1 = f32[1024,1024]{1,0:T(8,128)} custom-call(s32[1]{0:T(128)S(6)} %copy.37.refs_11_.refs_0_, bf16[1024,3072]{1,0:T(8,128)(2,1)} %get-tuple-element.79.refs_1_, f32[1024,1024]{1,0:T(8,128)} %get-tuple-element.116.refs_2_, bf16[1024,1024]{1,0:T(8,128)(2,1)} %get-tuple-element.122.refs_3_, bf16[1024,1024]{1,0:T(8,128)(2,1)} %get-tuple-element.123.refs_4_, ...), custom_call_target="tpu_custom_call" | custom-call | flops 6442450944 | bytes 20971520 | tf_op jit(solution)/shard_map/enc_input_grad/pallas_call | solution.py:334
  417.4 32.0 %all-reduce.7.cloned.1.call-done = (bf16[1024,512]{1,0:T(8,128)(2,1)}, bf16[512,1024]{1,0:T(8,128)(2,1)}) async-done(((bf16[1024,512]{1,0:T(8,128)(2,1)}, bf16[512,1024]{1,0:T(8,128)(2,1)}), (bf16[1024,512]{1,0:T(8,128)(2,1)}, bf16[512,1024]{1,0:T(8,128)(2,1)})) %all-reduce.7.cloned.1.call-update) | async-done | bytes 2097168 | tf_op jit(solution)/shard_map/psum | solution.py:1044
  449.4 0.0 copy-start.2
  449.4 2.9 convert_element_type.6
  452.3 0.0 copy-done.2
  452.3 1.6 convert_element_type.7
  453.9 144.7 %all-reduce.5.cloned.1.call-done = (f32[1024,512]{1,0:T(8,128)}, f32[520,1024]{1,0:T(8,128)}) async-done(((f32[1024,512]{1,0:T(8,128)}, f32[520,1024]{1,0:T(8,128)}), (f32[1024,512]{1,0:T(8,128)}, f32[520,1024]{1,0:T(8,128)})) %all-reduce.5.cloned.1.call-update) | async-done | bytes 4227088 | tf_op jit(solution)/shard_map/psum | solution.py:1043
  598.6 0.9 slice_reduce_fusion
  599.5 1.3 fusion.1
  600.8 0.0 copy-start
  600.8 3.3 slice.40
  604.1 4.6 stack.3
  608.7 0.5 fusion
  609.3 0.0 copy-done
  609.3 0.0 copy-start.3
  609.3 0.0 copy-start.1
  609.3 1.3 copy.39
  610.6 0.1 copy-done.3
  610.6 0.8 copy.40
  611.4 0.5 copy-done.1
  612.0 1.3 copy.41
Async XLA Ops:
  7.2 442.2 %all-reduce.7.cloned.1.call-start = ((), (), s32[]{:S(2)}) async-start(), calls=%async_computation.1 | async-start | bytes 4194304 | tf_op jit(solution)/shard_map/psum | solution.py:1044
  313.7 284.9 %all-reduce.5.cloned.1.call-start = ((), (), s32[]{:S(2)}) async-start(), calls=%async_computation | async-start | bytes 8454144 | tf_op jit(solution)/shard_map/psum | solution.py:1043
  449.4 2.9 copy-start.2
  600.8 8.4 %copy-start = (bf16[1024,1024]{1,0:T(8,128)(2,1)S(1)}, bf16[1024,1024]{1,0:T(8,128)(2,1)}, u32[]{:S(2)}) copy-start(bf16[1024,1024]{1,0:T(8,128)(2,1)} %get-tuple-element.165) | copy-start | bytes 6291460
  609.3 1.4 copy-start.3
  609.3 2.7 copy-start.1
Sparse Core Ops, SparseCore 0:
  313.9 135.4 all-reduce.6
  456.7 141.8 all-reduce.4

commit v3 on v2

--- a/solution.py
+++ b/solution.py
@@ -76,28 +76,36 @@
 LEAD_US = 5.0
 
 
+class Place:
+    def __init__(self):
+        f, z = lax.axis_index("fsdp"), lax.axis_index("dp")
+        self.core, self.x, self.y = f % 2, (f // 2) % 2, f // 4
+        self.odd, self.high = z % 2, z // 2
+        self.own = f
+        self.twin = {"fsdp": f + 1 - 2 * self.core}
+        self.beside = {"fsdp": f + 2 - 4 * self.x}
+        self.above = {"fsdp": f + 4 - 8 * self.y}
+        self.partner = {"dp": z + 1 - 2 * self.odd}
+        self.distant = {"dp": z + 2 - 4 * self.high}
+
+    def meet(self):
+        barrier = pltpu.get_barrier_semaphore()
+        all_of_them = (self.twin, self.beside, self.above, self.partner, self.distant)
+        for to in all_of_them:
+            pl.semaphore_signal(barrier, inc=1, device_id=to, device_id_type=pl.DeviceIdType.MESH)
+        pl.semaphore_wait(barrier, len(all_of_them))
+
+
 class Gather:
-    def __init__(self, owns, wholes, splits, sends, recvs, locals_):
-        self.owns, self.wholes, self.splits = owns, wholes, splits
+    def __init__(self, place, owns, wholes, splits, sends, recvs, locals_):
+        self.place, self.owns, self.wholes, self.splits = place, owns, wholes, splits
         self.sends, self.recvs, self.locals = sends, recvs, locals_
         self.units = [(m, part) for m, split in enumerate(splits) for part in range(split)]
-        f, z = lax.axis_index("fsdp"), lax.axis_index("dp")
-        odd = z % 2
-        y, x, core = f // 4, (f // 2) % 2, f % 2
-        beside, above = f + 2 - 4 * x, f + 4 - 8 * y
-        self.own = f
-        self.direct = beside + odd * (above - beside)
-        self.onward = above + odd * (beside - above)
-        self.far = beside + 4 - 8 * y
-        self.twin = f + 1 - 2 * core
-        self.partner = z + 1 - 2 * odd
-
-    def meet(self):
-        barrier = pltpu.get_barrier_semaphore()
-        mesh = pl.DeviceIdType.MESH
-        for to in ({"fsdp": self.direct}, {"fsdp": self.onward}, {"fsdp": self.twin}, {"dp": self.partner}):
-            pl.semaphore_signal(barrier, inc=1, device_id=to, device_id_type=mesh)
-        pl.semaphore_wait(barrier, 4)
+        beside, above = place.beside["fsdp"], place.above["fsdp"]
+        self.own = place.own
+        self.direct = beside + place.odd * (above - beside)
+        self.onward = above + place.odd * (beside - above)
+        self.far = beside + 4 - 8 * place.y
 
     def transfer(self, unit, kind):
         m, part = self.units[unit]
@@ -107,9 +115,9 @@
         owner = (self.own, self.direct, self.direct, self.own, self.direct, self.far, self.onward)[kind]
         there = whole.at[pl.ds(pl.multiple_of(owner * block + part * rows, 16), rows), :]
         here = own.at[pl.ds(part * rows, rows), :] if kind in (0, 3) else there
-        to = {"fsdp": (self.direct, self.onward, None, self.twin, self.twin, self.twin, self.twin)[kind]}
-        if kind == 2:
-            to = {"dp": self.partner}
+        to = self.place.twin if kind >= 3 else self.place.partner
+        if kind < 2:
+            to = {"fsdp": (self.direct, self.onward)[kind]}
         return pltpu.make_async_remote_copy(
             src_ref=here,
             dst_ref=there,
@@ -125,7 +133,6 @@
         return pltpu.make_async_copy(self.owns[m], self.wholes[m].at[rows, :], self.locals.at[m])
 
     def begin(self):
-        self.meet()
         for unit in range(len(self.units)):
             self.transfer(unit, 0).start()
         for unit in range(len(self.units)):
@@ -155,6 +162,114 @@
         for unit in range(len(self.units)):
             for kind in range(7):
                 self.transfer(unit, kind).wait_send()
+
+
+LEVELS = 5
+SHAPES = ((1024, 512), (512, 1024))
+
+
+class Reduce:
+    def __init__(self, place, totals, gives, takes, pieces, wholes, sems, tallies=None):
+        self.place, self.totals, self.gives, self.takes = place, totals, gives, takes
+        self.pieces, self.wholes, self.tallies = pieces, wholes, tallies
+        self.sends, self.recvs, self.locals = sems
+        p = place
+        along = [(p.core, p.twin), (p.x, p.beside), (p.y, p.above), (p.odd, p.partner), (p.high, p.distant)]
+        self.ways = [along, [along[0], along[2], along[1], along[3], along[4]]]
+
+    def range(self, part, level):
+        rows = SHAPES[part][0]
+        first = 0
+        for bit, _ in self.ways[part][:level]:
+            rows = rows // 2
+            first = first + bit * rows
+        return first, rows
+
+    def halves(self, part, level):
+        first, rows = self.range(part, level)
+        bit = self.ways[part][level][0]
+        half = rows // 2
+        return pl.multiple_of(first + bit * half, half), pl.multiple_of(first + (1 - bit) * half, half), half
+
+    def slot(self, part, level):
+        rows = SHAPES[part][0]
+        return pl.ds(rows - (rows >> level), rows >> (level + 1))
+
+    def remote(self, src, dst, part, level, back):
+        return pltpu.make_async_remote_copy(
+            src_ref=src,
+            dst_ref=dst,
+            send_sem=self.sends.at[part, level, back],
+            recv_sem=self.recvs.at[part, level, back],
+            device_id=self.ways[part if part < 2 else 0][level][1],
+            device_id_type=pl.DeviceIdType.MESH,
+        )
+
+    def down(self, part, level):
+        rows = self.slot(part, level)
+        return self.remote(self.gives[part].at[rows, :], self.takes[part].at[rows, :], part, level, 0)
+
+    def up(self, part, level):
+        first, rows = self.range(part, level + 1)
+        rows = pl.ds(pl.multiple_of(first, rows), rows)
+        return self.remote(self.wholes[part].at[rows, :], self.wholes[part].at[rows, :], part, level, 1)
+
+    def tally(self, level):
+        return self.remote(self.tallies[0].at[level], self.tallies[1].at[level], 2, level, 0)
+
+    def piece(self, part):
+        first, rows = self.range(part, LEVELS)
+        rows = pl.ds(pl.multiple_of(first, rows), rows)
+        return pltpu.make_async_copy(self.pieces[part], self.wholes[part].at[rows, :], self.locals.at[part])
+
+    def tally_out(self):
+        return pltpu.make_async_copy(self.tallies[0].at[LEVELS], self.tallies[2], self.locals.at[2])
+
+    def step(self, at):
+        for part in range(2):
+            if 0 < at <= LEVELS:
+                keep, _, half = self.halves(part, at - 1)
+                self.down(part, at - 1).wait_recv()
+                rows = pl.ds(keep, half)
+                taken = self.takes[part][self.slot(part, at - 1), :].astype(F32)
+                self.totals[part][rows, :] = self.totals[part][rows, :] + taken
+            if at < LEVELS:
+                _, give, half = self.halves(part, at)
+                self.gives[part][self.slot(part, at), :] = self.totals[part][pl.ds(give, half), :].astype(BF16)
+                self.down(part, at).start()
+            elif at == LEVELS:
+                first, rows = self.range(part, LEVELS)
+                last = pl.ds(pl.multiple_of(first, rows), rows)
+                self.pieces[part][...] = self.totals[part][last, :].astype(BF16)
+                self.piece(part).start()
+                self.piece(part).wait()
+                self.up(part, LEVELS - 1).start()
+            else:
+                level = 2 * LEVELS - at
+                self.up(part, level).wait_recv()
+                if level:
+                    self.up(part, level - 1).start()
+        if self.tallies and at <= LEVELS:
+            if at:
+                self.tally(at - 1).wait_recv()
+                self.tallies[0][at] = self.tallies[0][at - 1] + self.tallies[1][at - 1]
+            if at < LEVELS:
+                self.tally(at).start()
+            else:
+                self.tally_out().start()
+
+    def finish(self):
+        for level in range(LEVELS):
+            for part in range(2):
+                self.down(part, level).wait_send()
+                self.up(part, level).wait_send()
+            if self.tallies:
+                self.tally(level).wait_send()
+        if self.tallies:
+            self.tally_out().wait()
+
+
+REDUCE_US = (0.0, 5.0, 9.0, 6.5, 6.0, 6.0, 6.0, 6.0, 6.5, 9.0, 5.0)
 
 
 ANY = pl.BlockSpec(memory_space=pl.ANY)
@@ -182,6 +297,13 @@
         self.wholes = [Later((a.shape[0] * fsdp, a.shape[1]), a.dtype) for a in self.owns]
         self.splits = [4 if a.shape[1] == 3072 else max(1, a.size // 131072) for a in self.owns]
         self.stages = []
+        self.sums = {}
+
+    def reduce(self, name, tallied):
+        self.sums[name] = [Later(shape, BF16) for shape in SHAPES]
+        if tallied:
+            self.sums[name].append(Later((8, 1024), F32))
+        return self.sums[name]
 
     def add(self, **stage):
         stage["results"] = [Later(shape, dtype) for shape, dtype, _ in stage["outs"]]
@@ -200,12 +322,13 @@
                 last_of[m] = unit
                 unit += 1
         acts.sort(key=lambda act: act[0])
-        clock, plans = 0.0, []
+        clock, plans, started = 0.0, [], []
         for stage in self.stages:
-            before, ticks = [], {}
+            before, ticks = started, {}
+            started = []
             needed = [last_of[self.wholes.index(mat)] for mat in stage["needs"]]
             if needed:
-                while any(act[2] <= max(needed) for act in acts):
+                while any(act[1] in ("pass_on", "share") and act[2] <= max(needed) for act in acts):
                     clock = max(clock, acts[0][0])
                     before.append(acts.pop(0)[1:])
             pace = stage["time"] / stage["grid"][0] / stage["slots"]
@@ -214,6 +337,14 @@
                     ticks.setdefault(divmod(tick, stage["slots"]), []).append(acts.pop(0)[1:])
                 clock += pace
             plans.append((before, ticks))
+            if stage["sums"]:
+                started = [("step", (stage["sums"], 0))]
+                due = clock
+                for at, time in enumerate(REDUCE_US):
+                    due += time
+                    if at:
+                        acts.append((due, "step", (stage["sums"], at)))
+                acts.sort(key=lambda act: act[0])
         return plans, [act[1:] for act in acts]
 
     def run(self):
@@ -223,6 +354,7 @@
                 if not isinstance(array, Later) and not any(array is g for g, _ in given):
                     given.append((array, SCALAR if spec is SCALAR else ANY))
         results = self.wholes + [r for stage in self.stages for r in stage["results"]]
+        results += [r for sums in self.sums.values() for r in sums]
         plans, left = self.schedule()
         units = sum(self.splits)
 
@@ -235,12 +367,27 @@
             rest = refs[len(self.owns) + len(given) :]
             for result, ref in zip(results, rest):
                 of[id(result)] = ref
-            gather = Gather(owns, [of[id(w)] for w in self.wholes], self.splits, *rest[len(results) :])
+            rest = rest[len(results) :]
+            place = Place()
+            gather = Gather(place, owns, [of[id(w)] for w in self.wholes], self.splits, *rest[:3])
+            rest = rest[3:]
+            sums = {}
+            for name, whole in self.sums.items():
+                tallies = [*rest[11:13], of[id(whole[2])]] if len(whole) > 2 else None
+                sums[name] = Reduce(
+                    place, rest[:2], rest[2:4], rest[4:6], rest[6:8], [of[id(w)] for w in whole[:2]],
+                    rest[8:11], tallies,
+                )
+                rest = rest[13:] if tallies else rest[11:]
+            place.meet()
             gather.begin()
             waited = set()
 
             def act(kind, unit):
-                getattr(gather, kind)(unit)
+                if kind == "step":
+                    sums[unit[0]].step(unit[1])
+                else:
+                    getattr(gather, kind)(unit)
 
             for stage, (before, ticks) in zip(self.stages, plans):
                 for kind, unit in before:
@@ -250,13 +397,25 @@
                     if m not in waited:
                         waited.add(m)
                         gather.complete(m)
-                self.run_stage(stage, ticks, act, of)
+                self.run_stage(stage, ticks, act, of, sums)
             for kind, unit in left:
                 act(kind, unit)
             for m in range(len(self.owns)):
                 if m not in waited:
                     gather.complete(m)
             gather.finish()
+            for each in sums.values():
+                each.finish()
+
+        buffers = []
+        for whole in self.sums.values():
+            for kind, share in ((F32, 1), (BF16, 1), (BF16, 1), (BF16, 32)):
+                buffers += [pltpu.VMEM((rows // share, width), kind) for rows, width in SHAPES]
+            buffers += [pltpu.SemaphoreType.DMA((3, LEVELS, 2)), pltpu.SemaphoreType.DMA((3, LEVELS, 2))]
+            buffers.append(pltpu.SemaphoreType.DMA((3,)))
+            if len(whole) > 2:
+                buffers.append(pltpu.VMEM((LEVELS + 1, 8, 1024), F32))
+                buffers.append(pltpu.VMEM((LEVELS, 8, 1024), F32))
 
         out = pl.pallas_call(
             kernel,
@@ -266,17 +425,18 @@
                 pltpu.SemaphoreType.DMA((units, 7)),
                 pltpu.SemaphoreType.DMA((units, 7)),
                 pltpu.SemaphoreType.DMA((len(self.owns),)),
+                *buffers,
             ],
             out_shape=[jax.ShapeDtypeStruct(r.shape, r.dtype) for r in results],
             compiler_params=pltpu.CompilerParams(
                 vmem_limit_bytes=VMEM_BYTES, collective_id=1, has_side_effects=True
             ),
-            name="forward",
+            name="everything",
         )(*self.owns, *[array for array, _ in given])
         arrays = {id(result): array for result, array in zip(results, out)}
         return lambda later: arrays[id(later)]
 
-    def run_stage(self, stage, ticks, act, of):
+    def run_stage(self, stage, ticks, act, of, sums):
         ins, outs = stage["ins"], stage["outs"]
         piped = [at for at, (_, spec) in enumerate(ins) if spec is not ANY and spec is not SCALAR]
         fixed = {at: of[id(a)] for at, (a, _) in enumerate(ins) if at not in piped}
@@ -289,6 +449,8 @@
                     def _(todo=todo):
                         for kind, unit in todo:
                             act(kind, unit)
+
+        poll.sums = sums.get(stage["sums"])
 
         def scoped(*scratch):
             if stage["prepare"]:
@@ -312,12 +474,12 @@
 
 def launch(
     body, name, grid, ins, outs, scratch, flops, moved, recorder=None, prepare=None, needs=(),
-    slots=1, time=1.0,
+    slots=1, time=1.0, sums=None,
 ):
     if recorder is not None:
         return recorder.add(
             body=body, grid=grid, ins=ins, outs=outs, scratch=scratch, prepare=prepare, needs=needs,
-            slots=slots, time=time,
+            slots=slots, time=time, sums=sums,
         )
 
     def kernel(*refs):
@@ -482,13 +644,17 @@
     )
 
 
-def attend_grad(name, queries, keys, values, weights, mixture, inverse, upstream):
+def attend_grad(name, queries, keys, values, weights, mixture, inverse, upstream, **record):
     q_len, k_len = queries[0].shape[0], keys[0].shape[0]
     pairs = 1024 // PAIR
     step = min(256, q_len)
     factor = 1.0 / math.sqrt(HEAD)
 
-    def kernel(q_ref, k_ref, v_ref, e_ref, o_ref, inv_ref, do_ref, dq_ref, dk_ref, dv_ref, ds_ref):
+    def body(ins, outs, extra, poll):
+        q_ref, k_ref, v_ref, e_ref, o_ref, inv_ref, do_ref = ins
+        dq_ref, dk_ref, dv_ref = outs
+        (ds_ref,) = extra
+        poll(0)
         lanes = lax.broadcasted_iota(jnp.int32, (1, PAIR), 1)
         first = lanes < HEAD
         scaled = do_ref[...].astype(F32) * inv_ref[...]
@@ -529,33 +695,29 @@
     def columns(rows, at):
         return pl.BlockSpec((rows, PAIR), lambda i: (0, at + i))
 
-    return pl.pallas_call(
-        kernel,
-        grid=(pairs,),
-        in_specs=[
-            columns(q_len, queries[1]),
-            columns(k_len, keys[1]),
-            columns(k_len, values[1]),
-            pl.BlockSpec((1, k_len, 2 * q_len), lambda i: (i, 0, 0)),
-            columns(q_len, 0),
-            columns(q_len, 0),
-            columns(q_len, 0),
+    return launch(
+        body,
+        name,
+        (pairs,),
+        [
+            (queries[0], columns(q_len, queries[1])),
+            (keys[0], columns(k_len, keys[1])),
+            (values[0], columns(k_len, values[1])),
+            (weights, pl.BlockSpec((1, k_len, 2 * q_len), lambda i: (i, 0, 0))),
+            (mixture, columns(q_len, 0)),
+            (inverse, columns(q_len, 0)),
+            (upstream, columns(q_len, 0)),
         ],
-        out_specs=[columns(q_len, 0), columns(k_len, 0), columns(k_len, 0)],
-        out_shape=[
-            jax.ShapeDtypeStruct((q_len, 1024), BF16),
-            jax.ShapeDtypeStruct((k_len, 1024), BF16),
-            jax.ShapeDtypeStruct((k_len, 1024), BF16),
+        [
+            ((q_len, 1024), BF16, columns(q_len, 0)),
+            ((k_len, 1024), BF16, columns(k_len, 0)),
+            ((k_len, 1024), BF16, columns(k_len, 0)),
         ],
-        scratch_shapes=[pltpu.VMEM((k_len, 2 * q_len), BF16)],
-        compiler_params=pltpu.CompilerParams(vmem_limit_bytes=VMEM_BYTES),
-        cost_estimate=pl.CostEstimate(
-            flops=32 * pairs * q_len * k_len * PAIR,
-            bytes_accessed=4 * pairs * q_len * k_len,
-            transcendentals=0,
-        ),
-        name=name,
-    )(queries[0], keys[0], values[0], weights, mixture, inverse, upstream)
+        [pltpu.VMEM((k_len, 2 * q_len), BF16)],
+        32 * pairs * q_len * k_len * PAIR,
+        4 * pairs * q_len * k_len,
+        **record,
+    )
 
 
 def row_mask(limit, block):
@@ -706,16 +868,18 @@
     return grad_two.astype(BF16), total, tn(low, du), tn(wa_ref[...], dvd)
 
 
-def hidden_grad(dz, total, fetches, refs, dfp, chunks):
+def hidden_grad(dz, total, fetches, refs, dfp, chunks, poll=lambda slot: None):
     slope_ref, ui_ref, ii_ref, gi_ref = refs
     back, within, last = fetches
     step = dfp.shape[1] // chunks
     back.wait_all()
+    poll(0)
     for chunk in range(chunks):
         columns = slice(chunk * step, (chunk + 1) * step)
         act_grad = nt(dz, back.whole[columns, :])
         dfp[:, columns] = (act_grad * slope_ref[:, columns].astype(F32)).astype(BF16)
     within.wait_all()
+    poll(1)
     total = total + nt(dfp[...], within.whole[...])
     grad_one = standardize_grad(ui_ref[...].astype(F32), ii_ref[:, 0:1], total * gi_ref[...])
     last.wait_all()
@@ -724,7 +888,7 @@
 
 def dec_branch_grad(
     name, limits, cot, saved_out, gain_out, saved_in, gain_in, slope, wa, ad_slope,
-    w_back, w_in, w_out, down_low, up_low, squares,
+    w_back, w_in, w_out, down_low, up_low, squares, **record,
 ):
     total, width = cot.shape
     hidden_units = w_in.shape[1]
@@ -735,13 +899,17 @@
     ]
 
     def body(limit, fetches, ins, outs, extra, poll):
-        grad_ref, mix_ref, down_ref, up_ref = outs
+        grad_ref, mix_ref = outs[:2]
+        if record:
+            (down_ref, up_ref), tally_ref = poll.sums.totals, poll.sums.tallies[0].at[0]
+        else:
+            down_ref, up_ref, tally_ref = outs[2], outs[3].at[:adapter], outs[3].at[adapter:]
         (other,), cot_ref, slope_ref, ii_ref = ins[:1], ins[1], ins[11], ins[12]
-        dz, part, down_ref[...], up_ref[:adapter] = adapter_grad(cot_ref[...].astype(F32), ins[2:11])
+        dz, part, down_ref[...], up_ref[...] = adapter_grad(cot_ref[...].astype(F32), ins[2:11])
         sums = [ref[row : row + 1, :] for ref, rows in zip(ins[13:], (1, 2, 1, 1, 2)) for row in range(rows)]
         lanes = lax.broadcasted_iota(jnp.int32, (1, width), 1)
         counts = jnp.where(lanes == 0, limit[0], jnp.where(lanes == 1, other[0], 0)).astype(F32)
-        up_ref[adapter:] = jnp.concatenate([*sums, counts], axis=0)
+        tally_ref[...] = jnp.concatenate([*sums, counts], axis=0)
         grad_ref[...], mix_ref[...] = hidden_grad(
             dz, part, fetches, (slope_ref, ins[5], ii_ref, ins[6]), extra[0], 4
         )
@@ -756,17 +924,20 @@
         [
             (cot.shape, F32, whole_spec(cot.shape)),
             (cot.shape, BF16, whole_spec(cot.shape)),
-            (down_low.shape, F32, whole_spec(down_low.shape)),
-            ((adapter + 8, width), F32, whole_spec((adapter + 8, width))),
+        ]
+        + [
+            (shape, F32, whole_spec(shape))
+            for shape in (() if record else (down_low.shape, (adapter + 8, width)))
         ],
         scratch=[pltpu.VMEM((total, hidden_units), BF16)],
         flops=4 * total * width * (hidden_units + 2 * adapter),
+        **record,
     )
 
 
 def enc_adapter_grad(
     name, limit, cot, cross, cross_mat, saved_out, gain_out, saved_in, gain_in, wa, ad_slope,
-    down_low, up_low,
+    down_low, up_low, **record,
 ):
     total, width = cot.shape
     adapter = down_low.shape[1]
@@ -774,8 +945,9 @@
     rows = rows_spec(block, width)
 
     def body(limit, fetches, ins, outs, extra, poll):
-        dz_ref, part_ref, down_ref, up_ref = outs
-        down_sum, up_sum = extra
+        poll(0)
+        dz_ref, part_ref = outs[:2]
+        down_sum, up_sum = poll.sums.totals if record else extra
         fetches[0].wait_all()
         upstream = ins[0][...].astype(F32)
         for at in range(2):
@@ -793,10 +965,12 @@
             up_sum[...] += up_part
             down_sum[...] += down_part
 
-        @pl.when(at == total // block - 1)
-        def _():
-            up_ref[...] = up_sum[...].astype(BF16)
-            down_ref[...] = down_sum[...].astype(BF16)
+        if not record:
+
+            @pl.when(at == total // block - 1)
+            def _():
+                outs[2][...] = down_sum[...].astype(BF16)
+                outs[3][...] = up_sum[...].astype(BF16)
 
     return staged_call(
         body,
@@ -821,15 +995,15 @@
         [
             ((total, width), BF16, rows),
             ((total, width), F32, rows),
-            (down_low.shape, BF16, whole_spec(down_low.shape)),
-            (up_low.shape, BF16, whole_spec(up_low.shape)),
-        ],
-        scratch=[pltpu.VMEM(down_low.shape, F32), pltpu.VMEM(up_low.shape, F32)],
+        ]
+        + [(a.shape, BF16, whole_spec(a.shape)) for a in (() if record else (down_low, up_low))],
+        scratch=[pltpu.VMEM(a.shape, F32) for a in (() if record else (down_low, up_low))],
         flops=4 * total * width * (width + 2 * adapter),
-    )
-
-
-def enc_hidden_grad(name, limit, dz, part, slope, saved_in, gain_in, w_back, w_in, w_out):
+        **record,
+    )
+
+
+def enc_hidden_grad(name, limit, dz, part, slope, saved_in, gain_in, w_back, w_in, w_out, **record):
     total, width = dz.shape
     hidden_units = w_in.shape[1]
     block = min(256, total)
@@ -837,7 +1011,7 @@
 
     def body(limit, fetches, ins, outs, extra, poll):
         outs[0][...], outs[1][...] = hidden_grad(
-            ins[0][...], ins[1][...], fetches, ins[2:], extra[0], 4
+            ins[0][...], ins[1][...], fetches, ins[2:], extra[0], 4, poll
         )
 
     return staged_call(
@@ -857,15 +1031,17 @@
         [((total, width), F32, rows), ((total, width), BF16, rows)],
         scratch=[pltpu.VMEM((block, hidden_units), BF16)],
         flops=4 * total * width * hidden_units,
-    )
-
-
-def middle_grad(name, limit, grad_cross, dq, saved, gain, w_cq, w_so):
+        **record,
+    )
+
+
+def middle_grad(name, limit, grad_cross, dq, saved, gain, w_cq, w_so, **record):
     total, width = dq.shape
     block = min(256, total)
     unit, inv = saved
 
     def body(limit, fetches, ins, outs, extra, poll):
+        poll(0)
         gc_ref, dq_ref, u_ref, i_ref, g_ref = ins
         fetches[0].wait_all()
         hidden_grad = gc_ref[...] + nt(dq_ref[...], fetches[0].whole[...])
@@ -894,12 +1070,14 @@
             ((total, width), BF16, rows_spec(block, width)),
         ],
         flops=4 * total * width * width,
-    )
-
-
-def input_grad(name, limit, base, parts, mat):
+        **record,
+    )
+
+
+def input_grad(name, limit, base, parts, mat, narrow=(), tally=None):
     total, width = base.shape
     block = min(256, total)
+    steps = total // block
     count = len(parts)
 
     def body(limit, fetches, ins, outs, extra, poll):
@@ -909,17 +1087,30 @@
             fetch.wait(at)
             result = result + nt(ins[1 + at][...], fetch.whole[:, at * width : (at + 1) * width])
         outs[0][...] = result
-
+        for at in range(len(narrow)):
+            outs[1 + at][...] = ins[1 + count + at][...].astype(F32)
+        if tally is not None:
+            rows = ins[-1][...]
+            at = lax.broadcasted_iota(jnp.int32, (8, 1), 0)
+            numbers = jnp.where(at < 3, rows[7:8, 0:1], rows[7:8, 1:2])
+            outs[-1][...] = spread_lanes(
+                jnp.sqrt(jnp.sum(rows, axis=1, keepdims=True) / (numbers * width))
+            )
+
+    slices = [(a, rows_spec(a.shape[0] // steps, a.shape[1])) for a in narrow]
+    tallies = [] if tally is None else [(tally, whole_spec(tally.shape))]
     return staged_call(
         body,
         name,
-        (total // block,),
+        (steps,),
         limit,
         [(mat, count)],
-        [(base, rows_spec(block, width))] + [(p, rows_spec(block, width)) for p in parts],
-        [((total, width), F32, rows_spec(block, width))],
+        [(base, rows_spec(block, width))] + [(p, rows_spec(block, width)) for p in parts] + slices + tallies,
+        [((total, width), F32, rows_spec(block, width))]
+        + [(a.shape, F32, spec) for a, spec in slices]
+        + [((8, 128), F32, whole_spec((8, 128))) for _ in tallies],
         flops=2 * total * width * width * count,
-    )[0]
+    )
 
 
 NAMES = (
@@ -947,8 +1138,10 @@
         recorder = None
         w = {name: lax.all_gather(b, "fsdp", axis=0, tiled=True) for name, b in blocks.items()}
 
-    def at(slots, time):
-        return {"recorder": recorder, "slots": slots, "time": time} if hosting else {}
+    def at(slots, time, sums=None):
+        if not hosting:
+            return {}
+        return {"recorder": recorder, "slots": slots, "time": time, "sums": sums}
 
     qkv = project("enc_project", enc_limit, enc_input, w["enc_qkv"], 3, **at(3, 13.0))
     e_enc, o_enc, inv_enc = attend(
@@ -981,79 +1174,62 @@
         "dec_branch", dec_limit, unit4, gain[3], gain[4], w["dec_ffn_in"], w["dec_ffn_out"],
         dec_down, dec_up, **at(4, 11.4),
     )
+    dec_sums = recorder.reduce("dec", True) if hosting else []
+    grad_cross, do_cross, *dec_grads = dec_branch_grad(
+        "dec_branch_grad", (enc_limit, dec_limit), dec_cot, (unit5, dev5), gain[4], (unit4, dev4), gain[3],
+        slope_d, wa_d, ads_d, w["dec_ffn_out"], w["dec_ffn_in"], w["dec_cross_out"], dec_down, dec_up,
+        (sq_a, sq_b, sq_c, sq_d, sq_e), **at(1, 15.0, "dec"),
+    )
+    dcq, dck, dcv = attend_grad(
+        "cross_attend_grad", (cross_q, 0), (kv, 0), (kv, 8), e_cross, o_cross, inv_cross, do_cross,
+        **at(1, 13.0),
+    )
+    enc_sums = recorder.reduce("enc", False) if hosting else []
+    dz, part, *enc_grads = enc_adapter_grad(
+        "enc_adapter_grad", enc_limit, enc_cot, (dck, dcv), w["dec_cross_kv"], (unit2, dev2), gain[1],
+        (unit1, dev1), gain[0], wa_e, ads_e, enc_down, enc_up, **at(1, 20.0, "enc"),
+    )
+    grad_one, do_enc = enc_hidden_grad(
+        "enc_hidden_grad", enc_limit, dz, part, slope_e, (unit1, dev1), gain[0],
+        w["enc_ffn_out"], w["enc_ffn_in"], w["enc_attn_out"], **at(2, 31.0),
+    )
+    deq, dek, dev = attend_grad(
+        "enc_attend_grad", (qkv, 0), (qkv, 8), (qkv, 16), e_enc, o_enc, inv_enc, do_enc, **at(1, 39.0)
+    )
+    grad_self, do_self = middle_grad(
+        "dec_middle_grad", dec_limit, grad_cross, dcq, (unit3, dev3), gain[2], w["dec_cross_q"],
+        w["dec_self_out"], **at(1, 6.0),
+    )
+    dsq, dsk, dsv = attend_grad(
+        "dec_attend_grad", (sqkv, 0), (sqkv, 8), (sqkv, 16), e_self, o_self, inv_self, do_self,
+        **at(1, 8.0),
+    )
     if hosting:
         value = recorder.run()
         w = {name: value(mat) for name, mat in w.items()}
-        qkv, e_enc, o_enc, inv_enc, unit1, dev1, sq_a = map(
-            value, (qkv, e_enc, o_enc, inv_enc, unit1, dev1, sq_a)
-        )
-        enc_out, unit2, dev2, slope_e, wa_e, ads_e, sq_b = map(
-            value, (enc_out, unit2, dev2, slope_e, wa_e, ads_e, sq_b)
-        )
-        sqkv, e_self, o_self, inv_self, unit3, dev3, sq_c, cross_q = map(
-            value, (sqkv, e_self, o_self, inv_self, unit3, dev3, sq_c, cross_q)
-        )
-        kv, e_cross, o_cross, inv_cross, unit4, dev4, sq_d = map(
-            value, (kv, e_cross, o_cross, inv_cross, unit4, dev4, sq_d)
-        )
-        dec_out, unit5, dev5, slope_d, wa_d, ads_d, sq_e = map(
-            value, (dec_out, unit5, dev5, slope_d, wa_d, ads_d, sq_e)
-        )
-    grad_cross, do_cross, dec_down_grad, dec_up_grad = dec_branch_grad(
-        "dec_branch_grad", (enc_limit, dec_limit), dec_cot, (unit5, dev5), gain[4], (unit4, dev4), gain[3],
-        slope_d, wa_d, ads_d, w["dec_ffn_out"], w["dec_ffn_in"], w["dec_cross_out"], dec_down, dec_up,
-        (sq_a, sq_b, sq_c, sq_d, sq_e),
-    )
-    dcq, dck, dcv = attend_grad(
-        "cross_attend_grad", (cross_q, 0), (kv, 0), (kv, 8), e_cross, o_cross, inv_cross, do_cross
-    )
-    dz, part, enc_down_grad, enc_up_grad = enc_adapter_grad(
-        "enc_adapter_grad", enc_limit, enc_cot, (dck, dcv), w["dec_cross_kv"], (unit2, dev2), gain[1],
-        (unit1, dev1), gain[0], wa_e, ads_e, enc_down, enc_up,
-    )
-    grad_self, do_self = middle_grad(
-        "dec_middle_grad", dec_limit, grad_cross, dcq, (unit3, dev3), gain[2], w["dec_cross_q"], w["dec_self_out"]
-    )
-    dsq, dsk, dsv = attend_grad(
-        "dec_attend_grad", (sqkv, 0), (sqkv, 8), (sqkv, 16), e_self, o_self, inv_self, do_self
-    )
-    dec_grad = input_grad("dec_input_grad", dec_limit, grad_self, [dsq, dsk, dsv], w["dec_self_qkv"])
-    grad_one, do_enc = enc_hidden_grad(
-        "enc_hidden_grad", enc_limit, dz, part, slope_e, (unit1, dev1), gain[0],
-        w["enc_ffn_out"], w["enc_ffn_in"], w["enc_attn_out"],
-    )
-    deq, dek, dev = attend_grad(
-        "enc_attend_grad", (qkv, 0), (qkv, 8), (qkv, 16), e_enc, o_enc, inv_enc, do_enc
-    )
-    enc_grad = input_grad("enc_input_grad", enc_limit, grad_one, [deq, dek, dev], w["enc_qkv"])
-    return (
-        (enc_out, dec_out, enc_grad, dec_grad),
-        (enc_down_grad, enc_up_grad),
-        (dec_down_grad, dec_up_grad),
-    )
+        enc_out, dec_out, grad_one, grad_self = map(value, (enc_out, dec_out, grad_one, grad_self))
+        deq, dek, dev, dsq, dsk, dsv = map(value, (deq, dek, dev, dsq, dsk, dsv))
+        *dec_grads, tally = map(value, dec_sums)
+        enc_grads = [value(a) for a in enc_sums]
+    else:
+        everyone = ("fsdp", "dp")
+        down, up = lax.psum(dec_grads, everyone)
+        dec_grads, tally = [down, up[: dec_up.shape[0]]], up[dec_up.shape[0] :]
+        enc_grads = lax.psum(enc_grads, everyone)
+    dec_grad, *dec_grads = input_grad(
+        "dec_input_grad", dec_limit, grad_self, [dsq, dsk, dsv], w["dec_self_qkv"], dec_grads
+    )
+    enc_grad, *enc_grads, rms = input_grad(
+        "enc_input_grad", enc_limit, grad_one, [deq, dek, dev], w["enc_qkv"], enc_grads, tally
+    )
+    return enc_out, dec_out, enc_grad, dec_grad, *enc_grads, *dec_grads, rms[:7, 0]
 
 
 def shards(fsdp, dp, enc_input, dec_input, enc_cot, dec_cot, *rest):
     mats, (gains, enc_down, enc_up, dec_down, dec_up, enc_lengths, dec_lengths) = rest[:11], rest[11:]
-    results, enc_grads, dec_grads = layers(
+    return layers(
         enc_lengths, dec_lengths, enc_input, dec_input, enc_cot, dec_cot, dict(zip(NAMES, mats)),
-        fsdp == 8 and dp % 2 == 0, fsdp, gains, (enc_down, enc_up, dec_down, dec_up),
-    )
-    everyone = ("fsdp", "dp")
-    dec_down_grad, dec_up_grad = lax.psum(dec_grads, everyone)
-    enc_down_grad, enc_up_grad = lax.psum(enc_grads, everyone)
-    width = enc_input.shape[1]
-    adapter = dec_up.shape[0]
-    statistics = dec_up_grad[adapter:]
-    rows = jnp.stack([statistics[7, 0]] * 3 + [statistics[7, 1]] * 4)
-    rms = jnp.sqrt(jnp.sum(statistics[:7], axis=1) / (rows * width))
-    return (
-        *results,
-        enc_down_grad.astype(F32),
-        enc_up_grad.astype(F32),
-        dec_down_grad,
-        dec_up_grad[:adapter],
-        rms,
+        fsdp == 8 and dp == 4, fsdp, gains, (enc_down, enc_up, dec_down, dec_up),
     )
 
 

time: 629 us -> 468 us (0.74)
  waiting for transfers between devices: 177 us -> 0 us
  Pallas kernels: 407 us -> 452 us
  between operations: 15.6 us -> 2.41 us
  local copies, waits for them, and re-layouts: 14.8 us -> 5.07 us
    psum x2 -> x0, waiting for transfers between devices: 177 us -> none  [the longest x1 145 us: shards(): dec_down_grad, dec_up_grad = lax.psum(dec_grads, everyone)]
    pallas_call x1, Pallas kernels: 255 us -> 429 us  [run(): pl.pallas_call(kernel, in_specs=[ANY] * len(self.owns) + [spec for _, spe...]
    pallas_call x6 -> x2, Pallas kernels: 91.7 us -> 22.8 us  [launch(): pl.pallas_call(kernel, grid=grid, in_specs=[spec for _, spec in ins], out...]
    pallas_call x3 -> x0, Pallas kernels: 60.1 us -> none  [attend_grad(): pl.pallas_call(kernel, grid=(pairs,), in_specs=[columns(q_len, queries[1]...]
  transfers between devices with their start and end apart: 2 -> 0, of which waited for: 2 -> 0; matrix products, arithmetic and copies ran while one was open for 1% -> 0% of each run, Pallas kernels for 17% -> 0%
where the time goes in v3:
time: 468 us; the launch traced here: 459 us
  Pallas kernels  452 us (97%)
  local copies, waits for them, and re-layouts  5.07 us (1%)
    pallas_call x1, Pallas kernels, run(): pl.pallas_call(kernel, in_specs=[ANY] * len(self.owns) + [spec for _, spe...  429 us
    pallas_call x2, Pallas kernels, launch(): pl.pallas_call(kernel, grid=grid, in_specs=[spec for _, spec in ins], out...  22.8 us

profile of v3, /device:TPU:0, one launch (start us, length us, event | category | flops | bytes accessed | tf_op | source)
XLA Modules:
  0.0 459.1 jit_solution(191000582899891499)
XLA Ops:
  1.9 1.6 fusion
  3.5 428.9 %everything.1 = (bf16[1024,3072]{1,0:T(8,128)(2,1)}, bf16[1024,1024]{1,0:T(8,128)(2,1)}, bf16[1024,4096]{1,0:T(8,128)(2,1)}, bf16[4096,1024]{1,0:T(8,128)(2,1)},...) custom-call(bf16[128,3072]{1,0:T(8,128)(2,1)} %refs_0_.3, ...), custom_call_target="tpu_custom_call" | custom-call | tf_op jit(solution)/shard_map/everything/pallas_call | solution.py:420
  432.4 8.4 %dec_input_grad.1 = (f32[256,1024]{1,0:T(8,128)}, f32[1024,512]{1,0:T(8,128)}, f32[512,1024]{1,0:T(8,128)}) custom-call(s32[1]{0:T(128)S(6)} %copy.34.refs_17_.refs_0_, bf16[1024,3072]{1,0:T(8,128)(2,1)} %get-tuple-element.44.refs_1_, f32[256,1024]{1,0:T(8,128)} %get-tuple-element.45.refs_2_, bf16[256,1024]{1,0:T(8,128)(2,1)} %get-tuple-element.46.refs_3_, ...), custom_call_target="tpu_custom_call" | custom-call | flops 1610612736 | bytes 16252928 | tf_op jit(solution)/shard_map/dec_input_grad/pallas_call | solution.py:496
  440.8 0.0 copy-start
  440.8 14.4 %enc_input_grad.1 = (f32[1024,1024]{1,0:T(8,128)}, f32[1024,512]{1,0:T(8,128)}, f32[512,1024]{1,0:T(8,128)}, f32[8,128]{1,0:T(8,128)}) custom-call(s32[1]{0:T(128)S(6)} %copy.33.refs_11_.refs_0_, bf16[1024,3072]{1,0:T(8,128)(2,1)} %get-tuple-element.35.refs_1_, f32[1024,1024]{1,0:T(8,128)} %get-tuple-element.36.refs_2_, ...), custom_call_target="tpu_custom_call" | custom-call | flops 6442450944 | bytes 27299840 | tf_op jit(solution)/shard_map/enc_input_grad/pallas_call | solution.py:496
  455.1 1.3 slice_reduce_fusion
  456.5 0.0 copy-done
  456.5 0.0 copy-start.1
  456.5 1.3 copy.35
  457.8 0.1 copy-done.1
  457.9 0.8 copy.36
Async XLA Ops:
  440.8 15.7 %copy-start = (bf16[1024,1024]{1,0:T(8,128)(2,1)S(1)}, bf16[1024,1024]{1,0:T(8,128)(2,1)}, u32[]{:S(2)}) copy-start(bf16[1024,1024]{1,0:T(8,128)(2,1)} %get-tuple-element.71) | copy-start | bytes 6291460
  456.5 1.4 copy-start.1

commit v4 on v3

--- a/solution.py
+++ b/solution.py
@@ -48,14 +48,16 @@
 
 
 class Fetch:
-    def __init__(self, source, whole, sems, chunks):
+    def __init__(self, source, whole, sems, chunks, first=0):
         self.source, self.whole, self.sems, self.chunks = source, whole, sems, chunks
+        self.first = first
 
     def copy(self, chunk):
         width = self.whole.shape[1] // self.chunks
-        columns = pl.ds(chunk * width, width)
         return pltpu.make_async_copy(
-            self.source.at[:, columns], self.whole.at[:, columns], self.sems.at[chunk]
+            self.source.at[:, pl.ds(self.first + chunk * width, width)],
+            self.whole.at[:, pl.ds(chunk * width, width)],
+            self.sems.at[chunk],
         )
 
     def start(self):
@@ -110,11 +112,14 @@
     def transfer(self, unit, kind):
         m, part = self.units[unit]
         whole, own = self.wholes[m], self.owns[m]
-        block = own.shape[0]
-        rows = block // self.splits[m]
+        block, width = own.shape
+        by_columns = width == 3072
+        rows = block if by_columns else block // self.splits[m]
+        wide = width // self.splits[m] if by_columns else width
+        first_row, columns = (0, pl.ds(part * wide, wide)) if by_columns else (part * rows, pl.ds(0, wide))
         owner = (self.own, self.direct, self.direct, self.own, self.direct, self.far, self.onward)[kind]
-        there = whole.at[pl.ds(pl.multiple_of(owner * block + part * rows, 16), rows), :]
-        here = own.at[pl.ds(part * rows, rows), :] if kind in (0, 3) else there
+        there = whole.at[pl.ds(pl.multiple_of(owner * block + first_row, 16), rows), columns]
+        here = own.at[pl.ds(first_row, rows), columns] if kind in (0, 3) else there
         to = self.place.twin if kind >= 3 else self.place.partner
         if kind < 2:
             to = {"fsdp": (self.direct, self.onward)[kind]}
@@ -151,12 +156,11 @@
         self.transfer(unit, 2).wait_recv()
         self.transfer(unit, 6).start()
 
-    def complete(self, m):
-        for unit, (of, _) in enumerate(self.units):
-            if of == m:
-                for kind in (3, 4, 5, 6):
-                    self.transfer(unit, kind).wait_recv()
-        self.keep(m).wait()
+    def complete(self, m, part, first):
+        for kind in (3, 4, 5, 6):
+            self.transfer(self.units.index((m, part)), kind).wait_recv()
+        if first:
+            self.keep(m).wait()
 
     def finish(self):
         for unit in range(len(self.units)):
@@ -290,12 +294,15 @@
         self.size = math.prod(self.shape)
 
 
+HELD = {"within": (1024, 4096), "back": (4096, 1024)}
+
+
 class Recorder:
     def __init__(self, blocks, fsdp):
         self.names = list(blocks)
         self.owns = list(blocks.values())
         self.wholes = [Later((a.shape[0] * fsdp, a.shape[1]), a.dtype) for a in self.owns]
-        self.splits = [4 if a.shape[1] == 3072 else max(1, a.size // 131072) for a in self.owns]
+        self.splits = [max(1, a.size // 131072) for a in self.owns]
         self.stages = []
         self.sums = {}
 
@@ -312,31 +319,47 @@
 
     def schedule(self):
         acts, unit, due = [], 0, LEAD_US
-        last_of = {}
+        last_of, come = {}, {}
         for m, split in enumerate(self.splits):
-            for _ in range(split):
+            for part in range(split):
                 time = UNIT_US * self.owns[m].size / split / 131072
                 due += time
                 acts.append((due, "pass_on", unit))
                 acts.append((due + time + 2.0, "share", unit))
-                last_of[m] = unit
+                last_of[m, part] = unit
+                come[m] = due + time + 6.0
                 unit += 1
         acts.sort(key=lambda act: act[0])
         clock, plans, started = 0.0, [], []
-        for stage in self.stages:
+        for slot in HELD:
+            users = [stage for stage in self.stages if slot in stage["held"]]
+            if users:
+                mat = users[0]["held"][slot]
+                acts.append((come[self.wholes.index(mat)], "fetch", (slot, mat)))
+        acts.sort(key=lambda act: act[0])
+        for index, stage in enumerate(self.stages):
             before, ticks = started, {}
             started = []
-            needed = [last_of[self.wholes.index(mat)] for mat in stage["needs"]]
+            needed = [last_of[m, part] for m, part in self.parts_of(stage)]
             if needed:
                 while any(act[1] in ("pass_on", "share") and act[2] <= max(needed) for act in acts):
                     clock = max(clock, acts[0][0])
                     before.append(acts.pop(0)[1:])
+            while any(act[1] == "fetch" and act[2][1] is stage["held"].get(act[2][0]) for act in acts):
+                clock = max(clock, acts[0][0])
+                before.append(acts.pop(0)[1:])
             pace = stage["time"] / stage["grid"][0] / stage["slots"]
             for tick in range(stage["grid"][0] * stage["slots"]):
                 while acts and acts[0][0] <= clock:
                     ticks.setdefault(divmod(tick, stage["slots"]), []).append(acts.pop(0)[1:])
                 clock += pace
             plans.append((before, ticks))
+            for slot in stage["held"]:
+                after = [at for at in range(index + 1, len(self.stages)) if slot in self.stages[at]["held"]]
+                if after and self.stages[after[0]]["held"][slot] is not stage["held"][slot]:
+                    mat = self.stages[after[0]]["held"][slot]
+                    acts.append((max(clock, come[self.wholes.index(mat)]), "fetch", (slot, mat)))
+                    acts.sort(key=lambda act: act[0])
             if stage["sums"]:
                 started = [("step", (stage["sums"], 0))]
                 due = clock
@@ -345,7 +368,41 @@
                     if at:
                         acts.append((due, "step", (stage["sums"], at)))
                 acts.sort(key=lambda act: act[0])
-        return plans, [act[1:] for act in acts]
+        return self.completed(plans, [act[1:] for act in acts])
+
+    def completed(self, plans, left):
+        waited = []
+
+        def waits(parts):
+            found = []
+            for m, part in parts:
+                if (m, part) not in waited:
+                    found.append(("complete", (m, part, not any(of == m for of, _ in waited))))
+                    waited.append((m, part))
+            return found
+
+        def spread(acts):
+            found = []
+            for kind, unit in acts:
+                if kind == "fetch":
+                    m = self.wholes.index(unit[1])
+                    found += waits((m, part) for part in range(self.splits[m]))
+                found.append((kind, unit))
+            return found
+
+        full = []
+        for stage, (before, ticks) in zip(self.stages, plans):
+            before = spread(before) + waits(self.parts_of(stage))
+            full.append((before, {tick: spread(ticks[tick]) for tick in sorted(ticks)}))
+        every = [(m, part) for m, split in enumerate(self.splits) for part in range(split)]
+        return full, spread(left) + waits(every)
+
+    def parts_of(self, stage):
+        found = []
+        for mat, part in stage["needs"]:
+            m = self.wholes.index(mat)
+            found += [(m, part)] if part is not None else [(m, each) for each in range(self.splits[m])]
+        return found
 
     def run(self):
         given = []
@@ -379,30 +436,32 @@
                     rest[8:11], tallies,
                 )
                 rest = rest[13:] if tallies else rest[11:]
+            held = {slot: (rest[2 * at], rest[2 * at + 1]) for at, slot in enumerate(HELD)}
             place.meet()
             gather.begin()
-            waited = set()
 
             def act(kind, unit):
                 if kind == "step":
                     sums[unit[0]].step(unit[1])
+                elif kind == "fetch":
+                    slot, mat = unit
+                    Fetch(of[id(mat)], *held[slot], 1).start()
+                elif kind == "complete":
+                    gather.complete(*unit)
                 else:
                     getattr(gather, kind)(unit)
 
+            present = {}
             for stage, (before, ticks) in zip(self.stages, plans):
                 for kind, unit in before:
                     act(kind, unit)
-                for mat in stage["needs"]:
-                    m = self.wholes.index(mat)
-                    if m not in waited:
-                        waited.add(m)
-                        gather.complete(m)
-                self.run_stage(stage, ticks, act, of, sums)
+                for slot, mat in stage["held"].items():
+                    if present.get(slot) is not mat:
+                        Fetch(of[id(mat)], *held[slot], 1).copy(0).wait()
+                        present[slot] = mat
+                self.run_stage(stage, ticks, act, of, sums, held)
             for kind, unit in left:
                 act(kind, unit)
-            for m in range(len(self.owns)):
-                if m not in waited:
-                    gather.complete(m)
             gather.finish()
             for each in sums.values():
                 each.finish()
@@ -416,6 +475,9 @@
             if len(whole) > 2:
                 buffers.append(pltpu.VMEM((LEVELS + 1, 8, 1024), F32))
                 buffers.append(pltpu.VMEM((LEVELS, 8, 1024), F32))
+
+        for shape in HELD.values():
+            buffers += [pltpu.VMEM(shape, BF16), pltpu.SemaphoreType.DMA((1,))]
 
         out = pl.pallas_call(
             kernel,
@@ -436,7 +498,7 @@
         arrays = {id(result): array for result, array in zip(results, out)}
         return lambda later: arrays[id(later)]
 
-    def run_stage(self, stage, ticks, act, of, sums):
+    def run_stage(self, stage, ticks, act, of, sums, held):
         ins, outs = stage["ins"], stage["outs"]
         piped = [at for at, (_, spec) in enumerate(ins) if spec is not ANY and spec is not SCALAR]
         fixed = {at: of[id(a)] for at, (a, _) in enumerate(ins) if at not in piped}
@@ -451,6 +513,7 @@
                             act(kind, unit)
 
         poll.sums = sums.get(stage["sums"])
+        poll.held = held
 
         def scoped(*scratch):
             if stage["prepare"]:
@@ -474,12 +537,12 @@
 
 def launch(
     body, name, grid, ins, outs, scratch, flops, moved, recorder=None, prepare=None, needs=(),
-    slots=1, time=1.0, sums=None,
+    slots=1, time=1.0, sums=None, held=(),
 ):
     if recorder is not None:
         return recorder.add(
             body=body, grid=grid, ins=ins, outs=outs, scratch=scratch, prepare=prepare, needs=needs,
-            slots=slots, time=time, sums=sums,
+            slots=slots, time=time, sums=sums, held=dict(held),
         )
 
     def kernel(*refs):
@@ -506,17 +569,34 @@
     )(*[a for a, _ in ins])
 
 
-def staged_call(body, name, grid, limit, mats, ins, outs, scratch=(), flops=0, **record):
+class Ready:
+    def __init__(self, whole):
+        self.whole = whole
+
+    def wait(self, chunk):
+        pass
+
+    def wait_all(self):
+        pass
+
+
+def staged_call(body, name, grid, limit, mats, ins, outs, scratch=(), flops=0, part=None, slots_of=(), **record):
+    held = dict(zip(slots_of, (mat for mat, _ in mats))) if record else {}
+    own = mats[len(held) :]
     holders = []
-    for mat, chunks in mats:
-        holders.append(pltpu.VMEM(mat.shape, mat.dtype))
+    for mat, chunks in own:
+        rows, width = mat.shape
+        holders.append(pltpu.VMEM((rows, width if part is None else width // 3), mat.dtype))
         holders.append(pltpu.SemaphoreType.DMA((chunks,)))
-    given = [mat for mat, _ in mats]
+    given = [mat for mat, _ in own]
 
     def fetches(in_refs, rest):
         return [
-            Fetch(in_refs[1 + at], rest[2 * at], rest[2 * at + 1], chunks)
-            for at, (_, chunks) in enumerate(mats)
+            Fetch(
+                in_refs[1 + at], rest[2 * at], rest[2 * at + 1], chunks,
+                0 if part is None else part * mat.shape[1] // 3,
+            )
+            for at, (mat, chunks) in enumerate(own)
         ]
 
     def prepare(in_refs, rest):
@@ -524,12 +604,15 @@
             fetch.start()
 
     def staged(in_refs, out_refs, rest, poll):
-        args = (in_refs[0], fetches(in_refs, rest), in_refs[1 + len(given) :], out_refs)
-        body(*args, rest[2 * len(mats) :], poll)
+        ready = [Ready(poll.held[slot][0]) for slot in held]
+        args = (in_refs[0], ready + fetches(in_refs, rest), in_refs[1 + len(given) :], out_refs)
+        body(*args, rest[2 * len(own) :], poll)
 
     moved = sum(a.size * a.dtype.itemsize for a in given)
     moved += sum(a.size * a.dtype.itemsize for a, _ in ins)
     moved += sum(math.prod(s) * jnp.dtype(d).itemsize for s, d, _ in outs)
+    if record:
+        record = dict(record, needs=[(mat, part) for mat in given], held=held)
     return launch(
         staged,
         name,
@@ -540,14 +623,13 @@
         flops,
         moved,
         prepare=prepare,
-        needs=given if record else (),
         **record,
     )
 
 
-def project(name, limit, rows_in, mat, chunks, **record):
+def project(name, limit, rows_in, mat, chunks, part=None, **record):
     total, depth = rows_in.shape
-    width = mat.shape[1]
+    width = mat.shape[1] if part is None else mat.shape[1] // 3
     block = min(256, total)
     step = width // chunks
 
@@ -569,6 +651,7 @@
         [(rows_in, rows_spec(block, depth))],
         [((total, width), BF16, rows_spec(block, width))],
         flops=2 * total * depth * width,
+        part=part,
         **record,
     )[0]
 
@@ -576,9 +659,10 @@
 def attend(name, limit, queries, keys, values, causal, **record):
     q_len, k_len = queries[0].shape[0], keys[0].shape[0]
     pairs = 1024 // PAIR
-    step = min(256, q_len)
+    step = min(512, q_len)
 
     def body(ins, outs, extra, poll):
+        poll(0)
         limit_ref, q_ref, k_ref, v_ref = ins
         e_ref, o_ref, inv_ref = outs
         lanes = lax.broadcasted_iota(jnp.int32, (1, PAIR), 1)
@@ -587,27 +671,36 @@
         q_two = q_ref[...].astype(F32) * (1.0 / math.sqrt(HEAD))
         k_two = k_ref[...].astype(F32)
         v_two = v_ref[...].astype(F32)
+        q_own, k_own, v_own = [], [], []
+        for half in range(2):
+            own = (lanes >= HEAD * half) & (lanes < HEAD * (half + 1))
+            spare = lanes == HEAD * (1 - half)
+            q_own.append(jnp.where(own, q_two, jnp.where(spare, 1.0, 0.0)).astype(BF16))
+            k_own.append(jnp.where(own, k_two, jnp.where(spare, bias, 0.0)).astype(BF16))
+            v_own.append(jnp.where(own, v_two, jnp.where(spare, 1.0, 0.0)).T.astype(BF16))
+
+        def score(half, start):
+            scores = nt(k_own[half], q_own[half][start : start + step])
+            if causal:
+                shape = (k_len, step)
+                key_at = lax.broadcasted_iota(jnp.int32, shape, 0)
+                query_at = lax.broadcasted_iota(jnp.int32, shape, 1) + start
+                scores = jnp.where(key_at <= query_at, scores, -1000000000.0)
+            return scores
+
+        blocks = [(half, start) for half in range(2) for start in range(0, q_len, step)]
+        parts = [[], []]
+        scores = score(*blocks[0])
+        for at, (half, start) in enumerate(blocks):
+            later = score(*blocks[at + 1]) if at + 1 < len(blocks) else None
+            highest = jnp.max(scores, axis=0, keepdims=True)
+            weights = jnp.exp(scores - highest).astype(BF16)
+            e_ref[0, :, half * q_len + start : half * q_len + start + step] = weights
+            parts[half].append(nn(v_own[half], weights))
+            scores = later
         mixed = []
         for half in range(2):
-            poll(half)
-            own = (lanes >= HEAD * half) & (lanes < HEAD * (half + 1))
-            spare = lanes == HEAD * (1 - half)
-            q_own = jnp.where(own, q_two, jnp.where(spare, 1.0, 0.0)).astype(BF16)
-            k_own = jnp.where(own, k_two, jnp.where(spare, bias, 0.0)).astype(BF16)
-            v_own = jnp.where(own, v_two, jnp.where(spare, 1.0, 0.0)).T.astype(BF16)
-            parts = []
-            for start in range(0, q_len, step):
-                scores = nt(k_own, q_own[start : start + step])
-                if causal:
-                    shape = (k_len, step)
-                    key_at = lax.broadcasted_iota(jnp.int32, shape, 0)
-                    query_at = lax.broadcasted_iota(jnp.int32, shape, 1) + start
-                    scores = jnp.where(key_at <= query_at, scores, -1000000000.0)
-                highest = jnp.max(scores, axis=0, keepdims=True)
-                weights = jnp.exp(scores - highest).astype(BF16)
-                e_ref[0, :, half * q_len + start : half * q_len + start + step] = weights
-                parts.append(nn(v_own, weights))
-            out = jnp.concatenate(parts, axis=1) if len(parts) > 1 else parts[0]
+            out = jnp.concatenate(parts[half], axis=1) if len(parts[half]) > 1 else parts[half][0]
             at = HEAD * (1 - half)
             inverse = 1.0 / out[at : at + 1]
             own_rows = out[HEAD * half : HEAD * (half + 1)]
@@ -811,7 +904,8 @@
         ad_slope_ref[...] = (gate * (1.0 + pre * (1.0 - gate))).astype(BF16)
         adapted = 4.0 * nn(wa, au_ref[...].astype(BF16))
         for chunk in range(chunks):
-            poll(chunk)
+            if chunk % 2 == 0:
+                poll(chunk // 2)
             first.wait(chunk)
             columns = slice(chunk * step, (chunk + 1) * step)
             fp = nn(low, first.whole[:, columns])
@@ -854,6 +948,7 @@
         ],
         scratch=[pltpu.VMEM((block, hidden_units), BF16)],
         flops=4 * total * width * (hidden_units + adapter),
+        slots_of=("within", "back"),
         **record,
     )
 
@@ -931,6 +1026,7 @@
         ],
         scratch=[pltpu.VMEM((total, hidden_units), BF16)],
         flops=4 * total * width * (hidden_units + 2 * adapter),
+        slots_of=("back", "within"),
         **record,
     )
 
@@ -1031,6 +1127,7 @@
         [((total, width), F32, rows), ((total, width), BF16, rows)],
         scratch=[pltpu.VMEM((block, hidden_units), BF16)],
         flops=4 * total * width * hidden_units,
+        slots_of=("back", "within"),
         **record,
     )
 
@@ -1143,20 +1240,23 @@
             return {}
         return {"recorder": recorder, "slots": slots, "time": time, "sums": sums}
 
-    qkv = project("enc_project", enc_limit, enc_input, w["enc_qkv"], 3, **at(3, 13.0))
+    enc_q, enc_k, enc_v = (
+        project("enc_project", enc_limit, enc_input, w["enc_qkv"], 1, part, **at(1, 5.0))
+        for part in range(3)
+    )
     e_enc, o_enc, inv_enc = attend(
-        "enc_attend", enc_limit, (qkv, 0), (qkv, 8), (qkv, 16), False, **at(2, 53.0)
+        "enc_attend", enc_limit, (enc_q, 0), (enc_k, 0), (enc_v, 0), False, **at(1, 34.0)
     )
     unit1, dev1, sq_a = out_norm(
         "enc_out_norm", enc_limit, o_enc, enc_input, gain[0], w["enc_attn_out"], **at(1, 9.0)
     )
     enc_out, unit2, dev2, slope_e, wa_e, ads_e, sq_b = branch(
         "enc_branch", enc_limit, unit1, gain[0], gain[1], w["enc_ffn_in"], w["enc_ffn_out"],
-        enc_down, enc_up, **at(4, 38.0),
+        enc_down, enc_up, **at(2, 33.0),
     )
     sqkv = project("dec_project", dec_limit, dec_input, w["dec_self_qkv"], 3, **at(3, 6.0))
     e_self, o_self, inv_self = attend(
-        "dec_attend", dec_limit, (sqkv, 0), (sqkv, 8), (sqkv, 16), True, **at(2, 8.5)
+        "dec_attend", dec_limit, (sqkv, 0), (sqkv, 8), (sqkv, 16), True, **at(1, 8.5)
     )
     unit3, dev3, sq_c, cross_q = out_norm(
         "dec_out_norm", dec_limit, o_self, dec_input, gain[2], w["dec_self_out"], w["dec_cross_q"],
@@ -1164,7 +1264,7 @@
     )
     kv = project("cross_project", enc_limit, enc_out, w["dec_cross_kv"], 2, **at(2, 9.5))
     e_cross, o_cross, inv_cross = attend(
-        "cross_attend", enc_limit, (cross_q, 0), (kv, 0), (kv, 8), False, **at(2, 16.0)
+        "cross_attend", enc_limit, (cross_q, 0), (kv, 0), (kv, 8), False, **at(1, 14.0)
     )
     unit4, dev4, sq_d = out_norm(
         "cross_out_norm", dec_limit, o_cross, unit3, gain[3], w["dec_cross_out"],
@@ -1172,13 +1272,13 @@
     )
     dec_out, unit5, dev5, slope_d, wa_d, ads_d, sq_e = branch(
         "dec_branch", dec_limit, unit4, gain[3], gain[4], w["dec_ffn_in"], w["dec_ffn_out"],
-        dec_down, dec_up, **at(4, 11.4),
+        dec_down, dec_up, **at(2, 8.0),
     )
     dec_sums = recorder.reduce("dec", True) if hosting else []
     grad_cross, do_cross, *dec_grads = dec_branch_grad(
         "dec_branch_grad", (enc_limit, dec_limit), dec_cot, (unit5, dev5), gain[4], (unit4, dev4), gain[3],
         slope_d, wa_d, ads_d, w["dec_ffn_out"], w["dec_ffn_in"], w["dec_cross_out"], dec_down, dec_up,
-        (sq_a, sq_b, sq_c, sq_d, sq_e), **at(1, 15.0, "dec"),
+        (sq_a, sq_b, sq_c, sq_d, sq_e), **at(1, 11.0, "dec"),
     )
     dcq, dck, dcv = attend_grad(
         "cross_attend_grad", (cross_q, 0), (kv, 0), (kv, 8), e_cross, o_cross, inv_cross, do_cross,
@@ -1191,10 +1291,10 @@
     )
     grad_one, do_enc = enc_hidden_grad(
         "enc_hidden_grad", enc_limit, dz, part, slope_e, (unit1, dev1), gain[0],
-        w["enc_ffn_out"], w["enc_ffn_in"], w["enc_attn_out"], **at(2, 31.0),
+        w["enc_ffn_out"], w["enc_ffn_in"], w["enc_attn_out"], **at(2, 28.0),
     )
     deq, dek, dev = attend_grad(
-        "enc_attend_grad", (qkv, 0), (qkv, 8), (qkv, 16), e_enc, o_enc, inv_enc, do_enc, **at(1, 39.0)
+        "enc_attend_grad", (enc_q, 0), (enc_k, 0), (enc_v, 0), e_enc, o_enc, inv_enc, do_enc, **at(1, 39.0)
     )
     grad_self, do_self = middle_grad(
         "dec_middle_grad", dec_limit, grad_cross, dcq, (unit3, dev3), gain[2], w["dec_cross_q"],

time: 468 us -> 450 us (0.962)
  Pallas kernels: 452 us -> 434 us
    pallas_call x1, Pallas kernels: 429 us -> 411 us  [run(): pl.pallas_call(kernel, in_specs=[ANY] * len(self.owns) + [spec for _, spe...]
where the time goes in v4:
time: 450 us; the launch traced here: 442 us
  Pallas kernels  434 us (96%)
  local copies, waits for them, and re-layouts  5.07 us (1%)
    pallas_call x1, Pallas kernels, run(): pl.pallas_call(kernel, in_specs=[ANY] * len(self.owns) + [spec for _, spe...  411 us
    pallas_call x2, Pallas kernels, launch(): pl.pallas_call(kernel, grid=grid, in_specs=[spec for _, spec in ins], out...  22.8 us

profile of v4, /device:TPU:0, one launch (start us, length us, event | category | flops | bytes accessed | tf_op | source)
XLA Modules:
  0.0 441.6 jit_solution(16404923903462897125)
XLA Ops:
  1.9 1.6 fusion
  3.5 411.3 %everything.1 = (bf16[1024,3072]{1,0:T(8,128)(2,1)}, bf16[1024,1024]{1,0:T(8,128)(2,1)}, bf16[1024,4096]{1,0:T(8,128)(2,1)}, bf16[4096,1024]{1,0:T(8,128)(2,1)},...) custom-call(bf16[128,3072]{1,0:T(8,128)(2,1)} %refs_0_.3, ...), custom_call_target="tpu_custom_call" | custom-call | tf_op jit(solution)/shard_map/everything/pallas_call | solution.py:482
  414.8 8.4 %dec_input_grad.1 = (f32[256,1024]{1,0:T(8,128)}, f32[1024,512]{1,0:T(8,128)}, f32[512,1024]{1,0:T(8,128)}) custom-call(s32[1]{0:T(128)S(6)} %copy.34.refs_17_.refs_0_, bf16[1024,3072]{1,0:T(8,128)(2,1)} %get-tuple-element.44.refs_1_, f32[256,1024]{1,0:T(8,128)} %get-tuple-element.45.refs_2_, bf16[256,1024]{1,0:T(8,128)(2,1)} %get-tuple-element.46.refs_3_, ...), custom_call_target="tpu_custom_call" | custom-call | flops 1610612736 | bytes 16252928 | tf_op jit(solution)/shard_map/dec_input_grad/pallas_call | solution.py:559
  423.2 0.0 copy-start
  423.2 14.4 %enc_input_grad.1 = (f32[1024,1024]{1,0:T(8,128)}, f32[1024,512]{1,0:T(8,128)}, f32[512,1024]{1,0:T(8,128)}, f32[8,128]{1,0:T(8,128)}) custom-call(s32[1]{0:T(128)S(6)} %copy.33.refs_11_.refs_0_, bf16[1024,3072]{1,0:T(8,128)(2,1)} %get-tuple-element.35.refs_1_, f32[1024,1024]{1,0:T(8,128)} %get-tuple-element.36.refs_2_, ...), custom_call_target="tpu_custom_call" | custom-call | flops 6442450944 | bytes 27299840 | tf_op jit(solution)/shard_map/enc_input_grad/pallas_call | solution.py:559
  437.6 1.3 slice_reduce_fusion
  438.9 0.0 copy-done
  438.9 0.0 copy-start.1
  438.9 1.3 copy.35
  440.2 0.1 copy-done.1
  440.3 0.8 copy.36
Async XLA Ops:
  423.2 15.7 %copy-start = (bf16[1024,1024]{1,0:T(8,128)(2,1)S(1)}, bf16[1024,1024]{1,0:T(8,128)(2,1)}, u32[]{:S(2)}) copy-start(bf16[1024,1024]{1,0:T(8,128)(2,1)} %get-tuple-element.71) | copy-start | bytes 6291460
  438.9 1.4 copy-start.1

commit v5 on v4

--- a/solution.py
+++ b/solution.py
@@ -74,7 +74,7 @@
             self.wait(chunk)
 
 
-UNIT_US = 5.8
+UNIT_US = 6.0
 LEAD_US = 5.0
 
 
@@ -298,7 +298,9 @@
 
 
 class Recorder:
-    def __init__(self, blocks, fsdp):
+    def __init__(self, name, collective, blocks, fsdp):
+        self.name, self.collective = name, collective
+        self.loads = {}
         self.names = list(blocks)
         self.owns = list(blocks.values())
         self.wholes = [Later((a.shape[0] * fsdp, a.shape[1]), a.dtype) for a in self.owns]
@@ -311,6 +313,13 @@
         if tallied:
             self.sums[name].append(Later((8, 1024), F32))
         return self.sums[name]
+
+    def load(self, name, arrays):
+        self.loads[name] = arrays
+
+    def number(self, mat):
+        found = [m for m, whole in enumerate(self.wholes) if whole is mat]
+        return found[0] if found else None
 
     def add(self, **stage):
         stage["results"] = [Later(shape, dtype) for shape, dtype, _ in stage["outs"]]
@@ -335,7 +344,14 @@
             users = [stage for stage in self.stages if slot in stage["held"]]
             if users:
                 mat = users[0]["held"][slot]
-                acts.append((come[self.wholes.index(mat)], "fetch", (slot, mat)))
+                acts.append((come.get(self.number(mat), 0.0), "fetch", (slot, mat)))
+        for name in self.loads:
+            started += [("load", name), ("step", (name, 0))]
+            due = 0.0
+            for at, time in enumerate(REDUCE_US):
+                due += time
+                if at:
+                    acts.append((due, "step", (name, at)))
         acts.sort(key=lambda act: act[0])
         for index, stage in enumerate(self.stages):
             before, ticks = started, {}
@@ -358,7 +374,7 @@
                 after = [at for at in range(index + 1, len(self.stages)) if slot in self.stages[at]["held"]]
                 if after and self.stages[after[0]]["held"][slot] is not stage["held"][slot]:
                     mat = self.stages[after[0]]["held"][slot]
-                    acts.append((max(clock, come[self.wholes.index(mat)]), "fetch", (slot, mat)))
+                    acts.append((max(clock, come.get(self.number(mat), 0.0)), "fetch", (slot, mat)))
                     acts.sort(key=lambda act: act[0])
             if stage["sums"]:
                 started = [("step", (stage["sums"], 0))]
@@ -384,8 +400,8 @@
         def spread(acts):
             found = []
             for kind, unit in acts:
-                if kind == "fetch":
-                    m = self.wholes.index(unit[1])
+                m = self.number(unit[1]) if kind == "fetch" else None
+                if m is not None:
                     found += waits((m, part) for part in range(self.splits[m]))
                 found.append((kind, unit))
             return found
@@ -400,16 +416,18 @@
     def parts_of(self, stage):
         found = []
         for mat, part in stage["needs"]:
-            m = self.wholes.index(mat)
-            found += [(m, part)] if part is not None else [(m, each) for each in range(self.splits[m])]
+            m = self.number(mat)
+            if m is not None:
+                found += [(m, part)] if part is not None else [(m, each) for each in range(self.splits[m])]
         return found
 
     def run(self):
         given = []
         for stage in self.stages:
-            for array, spec in stage["ins"]:
+            for array, spec in stage["ins"] + [(mat, ANY) for mat in stage["held"].values()]:
                 if not isinstance(array, Later) and not any(array is g for g, _ in given):
                     given.append((array, SCALAR if spec is SCALAR else ANY))
+        given += [(array, ANY) for arrays in self.loads.values() for array in arrays]
         results = self.wholes + [r for stage in self.stages for r in stage["results"]]
         results += [r for sums in self.sums.values() for r in sums]
         plans, left = self.schedule()
@@ -426,8 +444,10 @@
                 of[id(result)] = ref
             rest = rest[len(results) :]
             place = Place()
-            gather = Gather(place, owns, [of[id(w)] for w in self.wholes], self.splits, *rest[:3])
-            rest = rest[3:]
+            gather = None
+            if self.owns:
+                gather = Gather(place, owns, [of[id(w)] for w in self.wholes], self.splits, *rest[:3])
+                rest = rest[3:]
             sums = {}
             for name, whole in self.sums.items():
                 tallies = [*rest[11:13], of[id(whole[2])]] if len(whole) > 2 else None
@@ -438,7 +458,8 @@
                 rest = rest[13:] if tallies else rest[11:]
             held = {slot: (rest[2 * at], rest[2 * at + 1]) for at, slot in enumerate(HELD)}
             place.meet()
-            gather.begin()
+            if gather:
+                gather.begin()
 
             def act(kind, unit):
                 if kind == "step":
@@ -448,6 +469,19 @@
                     Fetch(of[id(mat)], *held[slot], 1).start()
                 elif kind == "complete":
                     gather.complete(*unit)
+                elif kind == "load":
+                    first, second = (of[id(array)] for array in self.loads[unit])
+                    into, rows = sums[unit], SHAPES[1][0]
+                    pairs = [(first, into.totals[0]), (second.at[pl.ds(0, rows), :], into.totals[1])]
+                    pairs.append((second.at[pl.ds(rows, 8), :], into.tallies[0].at[0]))
+                    copies = [
+                        pltpu.make_async_copy(source, goal, into.locals.at[at])
+                        for at, (source, goal) in enumerate(pairs)
+                    ]
+                    for copy in copies:
+                        copy.start()
+                    for copy in copies:
+                        copy.wait()
                 else:
                     getattr(gather, kind)(unit)
 
@@ -462,10 +496,15 @@
                 self.run_stage(stage, ticks, act, of, sums, held)
             for kind, unit in left:
                 act(kind, unit)
-            gather.finish()
+            if gather:
+                gather.finish()
             for each in sums.values():
                 each.finish()
 
+        ports = []
+        if self.owns:
+            ports = [pltpu.SemaphoreType.DMA((units, 7)), pltpu.SemaphoreType.DMA((units, 7))]
+            ports.append(pltpu.SemaphoreType.DMA((len(self.owns),)))
         buffers = []
         for whole in self.sums.values():
             for kind, share in ((F32, 1), (BF16, 1), (BF16, 1), (BF16, 32)):
@@ -483,17 +522,12 @@
             kernel,
             in_specs=[ANY] * len(self.owns) + [spec for _, spec in given],
             out_specs=[ANY] * len(results),
-            scratch_shapes=[
-                pltpu.SemaphoreType.DMA((units, 7)),
-                pltpu.SemaphoreType.DMA((units, 7)),
-                pltpu.SemaphoreType.DMA((len(self.owns),)),
-                *buffers,
-            ],
+            scratch_shapes=[*ports, *buffers],
             out_shape=[jax.ShapeDtypeStruct(r.shape, r.dtype) for r in results],
             compiler_params=pltpu.CompilerParams(
-                vmem_limit_bytes=VMEM_BYTES, collective_id=1, has_side_effects=True
+                vmem_limit_bytes=VMEM_BYTES, collective_id=self.collective, has_side_effects=True
             ),
-            name="everything",
+            name=self.name,
         )(*self.owns, *[array for array, _ in given])
         arrays = {id(result): array for result, array in zip(results, out)}
         return lambda later: arrays[id(later)]
@@ -1229,7 +1263,7 @@
     gain = [gains[k : k + 1] for k in range(5)]
     enc_down, enc_up, dec_down, dec_up = adapters
     if hosting:
-        recorder = Recorder(blocks, fsdp)
+        recorder = Recorder("forward", 1, blocks, fsdp)
         w = dict(zip(recorder.names, recorder.wholes))
     else:
         recorder = None
@@ -1266,25 +1300,37 @@
     e_cross, o_cross, inv_cross = attend(
         "cross_attend", enc_limit, (cross_q, 0), (kv, 0), (kv, 8), False, **at(1, 14.0)
     )
+    if hosting:
+        value = recorder.run()
+        w = {name: value(mat) for name, mat in w.items()}
+        enc_q, enc_k, enc_v, e_enc, o_enc, inv_enc = map(value, (enc_q, enc_k, enc_v, e_enc, o_enc, inv_enc))
+        unit1, dev1, sq_a = map(value, (unit1, dev1, sq_a))
+        enc_out, unit2, dev2, slope_e, wa_e, ads_e, sq_b = map(
+            value, (enc_out, unit2, dev2, slope_e, wa_e, ads_e, sq_b)
+        )
+        sqkv, e_self, o_self, inv_self = map(value, (sqkv, e_self, o_self, inv_self))
+        unit3, dev3, sq_c, cross_q = map(value, (unit3, dev3, sq_c, cross_q))
+        kv, e_cross, o_cross, inv_cross = map(value, (kv, e_cross, o_cross, inv_cross))
+        recorder = Recorder("encoder_grad", 2, {}, fsdp)
     unit4, dev4, sq_d = out_norm(
-        "cross_out_norm", dec_limit, o_cross, unit3, gain[3], w["dec_cross_out"],
-        residual_gain=gain[2], **at(1, 4.6),
+        "cross_out_norm", dec_limit, o_cross, unit3, gain[3], w["dec_cross_out"], residual_gain=gain[2]
     )
     dec_out, unit5, dev5, slope_d, wa_d, ads_d, sq_e = branch(
         "dec_branch", dec_limit, unit4, gain[3], gain[4], w["dec_ffn_in"], w["dec_ffn_out"],
-        dec_down, dec_up, **at(2, 8.0),
-    )
-    dec_sums = recorder.reduce("dec", True) if hosting else []
+        dec_down, dec_up,
+    )
     grad_cross, do_cross, *dec_grads = dec_branch_grad(
         "dec_branch_grad", (enc_limit, dec_limit), dec_cot, (unit5, dev5), gain[4], (unit4, dev4), gain[3],
         slope_d, wa_d, ads_d, w["dec_ffn_out"], w["dec_ffn_in"], w["dec_cross_out"], dec_down, dec_up,
-        (sq_a, sq_b, sq_c, sq_d, sq_e), **at(1, 11.0, "dec"),
+        (sq_a, sq_b, sq_c, sq_d, sq_e),
     )
     dcq, dck, dcv = attend_grad(
-        "cross_attend_grad", (cross_q, 0), (kv, 0), (kv, 8), e_cross, o_cross, inv_cross, do_cross,
-        **at(1, 13.0),
-    )
-    enc_sums = recorder.reduce("enc", False) if hosting else []
+        "cross_attend_grad", (cross_q, 0), (kv, 0), (kv, 8), e_cross, o_cross, inv_cross, do_cross
+    )
+    if hosting:
+        dec_sums = recorder.reduce("dec", True)
+        recorder.load("dec", dec_grads)
+        enc_sums = recorder.reduce("enc", False)
     dz, part, *enc_grads = enc_adapter_grad(
         "enc_adapter_grad", enc_limit, enc_cot, (dck, dcv), w["dec_cross_kv"], (unit2, dev2), gain[1],
         (unit1, dev1), gain[0], wa_e, ads_e, enc_down, enc_up, **at(1, 20.0, "enc"),
@@ -1294,21 +1340,11 @@
         w["enc_ffn_out"], w["enc_ffn_in"], w["enc_attn_out"], **at(2, 28.0),
     )
     deq, dek, dev = attend_grad(
-        "enc_attend_grad", (enc_q, 0), (enc_k, 0), (enc_v, 0), e_enc, o_enc, inv_enc, do_enc, **at(1, 39.0)
-    )
-    grad_self, do_self = middle_grad(
-        "dec_middle_grad", dec_limit, grad_cross, dcq, (unit3, dev3), gain[2], w["dec_cross_q"],
-        w["dec_self_out"], **at(1, 6.0),
-    )
-    dsq, dsk, dsv = attend_grad(
-        "dec_attend_grad", (sqkv, 0), (sqkv, 8), (sqkv, 16), e_self, o_self, inv_self, do_self,
-        **at(1, 8.0),
+        "enc_attend_grad", (enc_q, 0), (enc_k, 0), (enc_v, 0), e_enc, o_enc, inv_enc, do_enc, **at(1, 37.0)
     )
     if hosting:
         value = recorder.run()
-        w = {name: value(mat) for name, mat in w.items()}
-        enc_out, dec_out, grad_one, grad_self = map(value, (enc_out, dec_out, grad_one, grad_self))
-        deq, dek, dev, dsq, dsk, dsv = map(value, (deq, dek, dev, dsq, dsk, dsv))
+        grad_one, deq, dek, dev = map(value, (grad_one, deq, dek, dev))
         *dec_grads, tally = map(value, dec_sums)
         enc_grads = [value(a) for a in enc_sums]
     else:
@@ -1316,6 +1352,13 @@
         down, up = lax.psum(dec_grads, everyone)
         dec_grads, tally = [down, up[: dec_up.shape[0]]], up[dec_up.shape[0] :]
         enc_grads = lax.psum(enc_grads, everyone)
+    grad_self, do_self = middle_grad(
+        "dec_middle_grad", dec_limit, grad_cross, dcq, (unit3, dev3), gain[2], w["dec_cross_q"],
+        w["dec_self_out"],
+    )
+    dsq, dsk, dsv = attend_grad(
+        "dec_attend_grad", (sqkv, 0), (sqkv, 8), (sqkv, 16), e_self, o_self, inv_self, do_self
+    )
     dec_grad, *dec_grads = input_grad(
         "dec_input_grad", dec_limit, grad_self, [dsq, dsk, dsv], w["dec_self_qkv"], dec_grads
     )

time: 450 us -> 431 us (0.958)
  Pallas kernels: 434 us -> 417 us
    pallas_call x1 -> x2, Pallas kernels: 411 us -> 336 us  [run(): pl.pallas_call(kernel, in_specs=[ANY] * len(self.owns) + [spec for _, spe...]
    pallas_call x2 -> x8, Pallas kernels: 22.8 us -> 81 us  [launch(): pl.pallas_call(kernel, grid=grid, in_specs=[spec for _, spec in ins], out...]
where the time goes in v5:
time: 431 us; the launch traced here: 423 us
  Pallas kernels  417 us (97%)
    pallas_call x2, Pallas kernels, run(): pl.pallas_call(kernel, in_specs=[ANY] * len(self.owns) + [spec for _, spe...  336 us
    pallas_call x8, Pallas kernels, launch(): pl.pallas_call(kernel, grid=grid, in_specs=[spec for _, spec in ins], out...  81 us

profile of v5, /device:TPU:0, one launch (start us, length us, event | category | flops | bytes accessed | tf_op | source)
XLA Modules:
  0.0 423.2 jit_solution(17502035135477919441)
XLA Ops:
  1.9 1.6 fusion
  3.5 232.1 %forward.1 = (bf16[1024,3072]{1,0:T(8,128)(2,1)}, bf16[1024,1024]{1,0:T(8,128)(2,1)}, bf16[1024,4096]{1,0:T(8,128)(2,1)}, bf16[4096,1024]{1,0:T(8,128)(2,1)}, bf...) custom-call(bf16[128,3072]{1,0:T(8,128)(2,1)} %refs_0_.8, ...), custom_call_target="tpu_custom_call" | custom-call | tf_op jit(solution)/shard_map/forward/pallas_call | solution.py:521
  235.6 4.6 %cross_out_norm.1 = (bf16[256,1024]{1,0:T(8,128)(2,1)}, f32[256,128]{1,0:T(8,128)}, f32[8,1024]{1,0:T(8,128)}) custom-call(s32[1]{0:T(128)S(6)} %copy.33.refs_17_.refs_0_.refs_4_, bf16[1024,1024]{1,0:T(8,128)(2,1)} %get-tuple-element.89.refs_1_.refs_3_, bf16[256,1024]{1,0:T(8,128)(2,1)} %get-tuple-element.90.refs_2_.refs_4_, ...), custom_call_target="tpu_custom_call" | custom-call | flops 536870912 | bytes 3842048 | tf_op jit(solution)/shard_map/cross_out_norm/pallas_call | solution.py:593
  240.2 12.1 %dec_branch.1 = (bf16[256,1024]{1,0:T(8,128)(2,1)}, bf16[256,1024]{1,0:T(8,128)(2,1)}, f32[256,128]{1,0:T(8,128)}, bf16[256,4096]{1,0:T(8,128)(2,1)}, bf16[256,5...) custom-call(s32[1]{0:T(128)S(6)} %copy.33.refs_17_.refs_0_.refs_4_, ...), custom_call_target="tpu_custom_call" | custom-call | flops 4831838208 | bytes 25337856 | tf_op jit(solution)/shard_map/dec_branch/pallas_call | solution.py:593
  252.3 14.8 %dec_branch_grad.1 = (f32[256,1024]{1,0:T(8,128)}, bf16[256,1024]{1,0:T(8,128)(2,1)}, f32[1024,512]{1,0:T(8,128)}, f32[520,1024]{1,0:T(8,128)}) custom-call(s32[1]{0:T(128)S(6)} %copy.32.refs_11_.refs_0_, bf16[4096,1024]{1,0:T(8,128)(2,1)} %get-tuple-element.88.refs_2_.refs_1_, bf16[1024,4096]{1,0:T(8,128)(2,1)} %get-tuple-element.87.refs_1_.refs_2_, ...), custom_call_target="tpu_custom_call" | custom-call | flops 5368709120 | bytes 33497092 | tf_op jit(solution)/shard_map/dec_branch_grad/pallas_call | solution.py:593
  267.2 13.0 %cross_attend_grad.1 = (bf16[256,1024]{1,0:T(8,128)(2,1)}, bf16[1024,1024]{1,0:T(8,128)(2,1)}, bf16[1024,1024]{1,0:T(8,128)(2,1)}) custom-call(bf16[256,1024]{1,0:T(8,128)(2,1)} %get-tuple-element.96.refs_0_, bf16[1024,2048]{1,0:T(8,128)(2,1)} %get-tuple-element.97.refs_1_.refs_2_, bf16[1024,2048]{1,0:T(8,128)(2,1)} %get-tuple-element.97.refs_1_.refs_2_, ...), custom_call_target="tpu_custom_call" | custom-call | flops 8589934592 | bytes 8388608 | tf_op jit(solution)/shard_map/cross_attend_grad/pallas_call | solution.py:593
  280.2 5.7 %dec_middle_grad.1 = (f32[256,1024]{1,0:T(8,128)}, bf16[256,1024]{1,0:T(8,128)(2,1)}) custom-call(s32[1]{0:T(128)S(6)} %copy.33.refs_17_.refs_0_.refs_4_, bf16[1024,1024]{1,0:T(8,128)(2,1)} %get-tuple-element.141.refs_1_, bf16[1024,1024]{1,0:T(8,128)(2,1)} %get-tuple-element.142.refs_2_, f32[256,1024]{1,0:T(8,128)} %get-tuple-element.143.refs_3_, ...), custom_call_target="tpu_custom_call" | custom-call | flops 1073741824 | bytes 7999488 | tf_op jit(solution)/shard_map/dec_middle_grad/pallas_call | solution.py:593
  285.9 8.0 %dec_attend_grad.1 = (bf16[256,1024]{1,0:T(8,128)(2,1)}, bf16[256,1024]{1,0:T(8,128)(2,1)}, bf16[256,1024]{1,0:T(8,128)(2,1)}) custom-call(bf16[256,3072]{1,0:T(8,128)(2,1)} %get-tuple-element.147.refs_0_.refs_1_.refs_2_, bf16[256,3072]{1,0:T(8,128)(2,1)} %get-tuple-element.147.refs_0_.refs_1_.refs_2_, ...), custom_call_target="tpu_custom_call" | custom-call | flops 2147483648 | bytes 2097152 | tf_op jit(solution)/shard_map/dec_attend_grad/pallas_call | solution.py:593
  293.9 103.7 %encoder_grad.1 = (bf16[1024,1024]{1,0:T(8,128)(2,1)}, f32[1024,1024]{1,0:T(8,128)}, f32[1024,1024]{1,0:T(8,128)}, bf16[1024,1024]{1,0:T(8,128)(2,1)}, bf16[1024...) custom-call(s32[1]{0:T(128)S(6)} %copy.32.refs_11_.refs_0_, ...), custom_call_target="tpu_custom_call" | custom-call | tf_op jit(solution)/shard_map/encoder_grad/pallas_call | solution.py:521
  397.6 8.4 %dec_input_grad.1 = (f32[256,1024]{1,0:T(8,128)}, f32[1024,512]{1,0:T(8,128)}, f32[512,1024]{1,0:T(8,128)}) custom-call(s32[1]{0:T(128)S(6)} %copy.33.refs_17_.refs_0_.refs_4_, bf16[1024,3072]{1,0:T(8,128)(2,1)} %get-tuple-element.140.refs_1_, f32[256,1024]{1,0:T(8,128)} %get-tuple-element.146.refs_2_, bf16[256,1024]{1,0:T(8,128)(2,1)} %get-tuple-element.152.refs_3_, ...), custom_call_target="tpu_custom_call" | custom-call | flops 1610612736 | bytes 16252928 | tf_op jit(solution)/shard_map/dec_input_grad/pallas_call | solution.py:593
  406.0 0.0 copy-start
  406.1 14.4 %enc_input_grad.1 = (f32[1024,1024]{1,0:T(8,128)}, f32[1024,512]{1,0:T(8,128)}, f32[512,1024]{1,0:T(8,128)}, f32[8,128]{1,0:T(8,128)}) custom-call(s32[1]{0:T(128)S(6)} %copy.32.refs_11_.refs_0_, bf16[1024,3072]{1,0:T(8,128)(2,1)} %get-tuple-element.94.refs_1_, f32[1024,1024]{1,0:T(8,128)} %get-tuple-element.132.refs_2_, ...), custom_call_target="tpu_custom_call" | custom-call | flops 6442450944 | bytes 27299840 | tf_op jit(solution)/shard_map/enc_input_grad/pallas_call | solution.py:593
  420.4 1.3 slice_reduce_fusion
  421.7 0.0 copy-done
  421.7 1.3 copy.34
Async XLA Ops:
  406.0 15.7 %copy-start = (bf16[1024,1024]{1,0:T(8,128)(2,1)S(1)}, bf16[1024,1024]{1,0:T(8,128)(2,1)}, u32[]{:S(2)}) copy-start(bf16[1024,1024]{1,0:T(8,128)(2,1)} %get-tuple-element.177) | copy-start | bytes 6291460

commit v6 on v5

--- a/solution.py
+++ b/solution.py
@@ -1,5 +1,6 @@
 import functools
 import math
+import types
 
 import jax
 import jax.numpy as jnp
@@ -322,9 +323,10 @@
         return found[0] if found else None
 
     def add(self, **stage):
-        stage["results"] = [Later(shape, dtype) for shape, dtype, _ in stage["outs"]]
+        stage = types.SimpleNamespace(**stage)
+        stage.results = [Later(shape, dtype) for shape, dtype, _ in stage.outs]
         self.stages.append(stage)
-        return stage["results"]
+        return stage.results
 
     def schedule(self):
         acts, unit, due = [], 0, LEAD_US
@@ -341,9 +343,9 @@
         acts.sort(key=lambda act: act[0])
         clock, plans, started = 0.0, [], []
         for slot in HELD:
-            users = [stage for stage in self.stages if slot in stage["held"]]
+            users = [stage for stage in self.stages if slot in stage.held]
             if users:
-                mat = users[0]["held"][slot]
+                mat = users[0].held[slot]
                 acts.append((come.get(self.number(mat), 0.0), "fetch", (slot, mat)))
         for name in self.loads:
             started += [("load", name), ("step", (name, 0))]
@@ -361,28 +363,28 @@
                 while any(act[1] in ("pass_on", "share") and act[2] <= max(needed) for act in acts):
                     clock = max(clock, acts[0][0])
                     before.append(acts.pop(0)[1:])
-            while any(act[1] == "fetch" and act[2][1] is stage["held"].get(act[2][0]) for act in acts):
+            while any(act[1] == "fetch" and act[2][1] is stage.held.get(act[2][0]) for act in acts):
                 clock = max(clock, acts[0][0])
                 before.append(acts.pop(0)[1:])
-            pace = stage["time"] / stage["grid"][0] / stage["slots"]
-            for tick in range(stage["grid"][0] * stage["slots"]):
+            pace = stage.time / stage.grid[0] / stage.slots
+            for tick in range(stage.grid[0] * stage.slots):
                 while acts and acts[0][0] <= clock:
-                    ticks.setdefault(divmod(tick, stage["slots"]), []).append(acts.pop(0)[1:])
+                    ticks.setdefault(divmod(tick, stage.slots), []).append(acts.pop(0)[1:])
                 clock += pace
             plans.append((before, ticks))
-            for slot in stage["held"]:
-                after = [at for at in range(index + 1, len(self.stages)) if slot in self.stages[at]["held"]]
-                if after and self.stages[after[0]]["held"][slot] is not stage["held"][slot]:
-                    mat = self.stages[after[0]]["held"][slot]
+            for slot in stage.held:
+                after = [at for at in range(index + 1, len(self.stages)) if slot in self.stages[at].held]
+                if after and self.stages[after[0]].held[slot] is not stage.held[slot]:
+                    mat = self.stages[after[0]].held[slot]
                     acts.append((max(clock, come.get(self.number(mat), 0.0)), "fetch", (slot, mat)))
                     acts.sort(key=lambda act: act[0])
-            if stage["sums"]:
-                started = [("step", (stage["sums"], 0))]
+            if stage.sums:
+                started = [("step", (stage.sums, 0))]
                 due = clock
                 for at, time in enumerate(REDUCE_US):
                     due += time
                     if at:
-                        acts.append((due, "step", (stage["sums"], at)))
+                        acts.append((due, "step", (stage.sums, at)))
                 acts.sort(key=lambda act: act[0])
         return self.completed(plans, [act[1:] for act in acts])
 
@@ -415,7 +417,7 @@
 
     def parts_of(self, stage):
         found = []
-        for mat, part in stage["needs"]:
+        for mat, part in stage.needs:
             m = self.number(mat)
             if m is not None:
                 found += [(m, part)] if part is not None else [(m, each) for each in range(self.splits[m])]
@@ -424,11 +426,11 @@
     def run(self):
         given = []
         for stage in self.stages:
-            for array, spec in stage["ins"] + [(mat, ANY) for mat in stage["held"].values()]:
+            for array, spec in stage.ins + [(mat, ANY) for mat in stage.held.values()]:
                 if not isinstance(array, Later) and not any(array is g for g, _ in given):
                     given.append((array, SCALAR if spec is SCALAR else ANY))
         given += [(array, ANY) for arrays in self.loads.values() for array in arrays]
-        results = self.wholes + [r for stage in self.stages for r in stage["results"]]
+        results = self.wholes + [r for stage in self.stages for r in stage.results]
         results += [r for sums in self.sums.values() for r in sums]
         plans, left = self.schedule()
         units = sum(self.splits)
@@ -489,7 +491,7 @@
             for stage, (before, ticks) in zip(self.stages, plans):
                 for kind, unit in before:
                     act(kind, unit)
-                for slot, mat in stage["held"].items():
+                for slot, mat in stage.held.items():
                     if present.get(slot) is not mat:
                         Fetch(of[id(mat)], *held[slot], 1).copy(0).wait()
                         present[slot] = mat
@@ -533,7 +535,7 @@
         return lambda later: arrays[id(later)]
 
     def run_stage(self, stage, ticks, act, of, sums, held):
-        ins, outs = stage["ins"], stage["outs"]
+        ins, outs = stage.ins, stage.outs
         piped = [at for at, (_, spec) in enumerate(ins) if spec is not ANY and spec is not SCALAR]
         fixed = {at: of[id(a)] for at, (a, _) in enumerate(ins) if at not in piped}
 
@@ -546,27 +548,27 @@
                         for kind, unit in todo:
                             act(kind, unit)
 
-        poll.sums = sums.get(stage["sums"])
+        poll.sums = sums.get(stage.sums)
         poll.held = held
 
         def scoped(*scratch):
-            if stage["prepare"]:
-                stage["prepare"]([fixed.get(at) for at in range(len(ins))], scratch)
+            if stage.prepare:
+                stage.prepare([fixed.get(at) for at in range(len(ins))], scratch)
 
             def body(*blocks):
                 in_refs = [fixed.get(at) for at in range(len(ins))]
                 for at, ref in zip(piped, blocks):
                     in_refs[at] = ref
-                stage["body"](in_refs, list(blocks[len(piped) :]), scratch, poll)
+                stage.body(in_refs, list(blocks[len(piped) :]), scratch, poll)
 
             pltpu.emit_pipeline(
                 body,
-                grid=stage["grid"],
+                grid=stage.grid,
                 in_specs=[ins[at][1] for at in piped],
                 out_specs=[spec for _, _, spec in outs],
-            )(*[of[id(ins[at][0])] for at in piped], *[of[id(r)] for r in stage["results"]])
-
-        pl.run_scoped(scoped, *stage["scratch"])
+            )(*[of[id(ins[at][0])] for at in piped], *[of[id(r)] for r in stage.results])
+
+        pl.run_scoped(scoped, *stage.scratch)
 
 
 def launch(
@@ -1264,10 +1266,12 @@
     enc_down, enc_up, dec_down, dec_up = adapters
     if hosting:
         recorder = Recorder("forward", 1, blocks, fsdp)
-        w = dict(zip(recorder.names, recorder.wholes))
+        w = types.SimpleNamespace(**dict(zip(recorder.names, recorder.wholes)))
     else:
         recorder = None
-        w = {name: lax.all_gather(b, "fsdp", axis=0, tiled=True) for name, b in blocks.items()}
+        w = types.SimpleNamespace(
+            **{name: lax.all_gather(b, "fsdp", axis=0, tiled=True) for name, b in blocks.items()}
+        )
 
     def at(slots, time, sums=None):
         if not hosting:
@@ -1275,34 +1279,34 @@
         return {"recorder": recorder, "slots": slots, "time": time, "sums": sums}
 
     enc_q, enc_k, enc_v = (
-        project("enc_project", enc_limit, enc_input, w["enc_qkv"], 1, part, **at(1, 5.0))
+        project("enc_project", enc_limit, enc_input, w.enc_qkv, 1, part, **at(1, 5.0))
         for part in range(3)
     )
     e_enc, o_enc, inv_enc = attend(
         "enc_attend", enc_limit, (enc_q, 0), (enc_k, 0), (enc_v, 0), False, **at(1, 34.0)
     )
     unit1, dev1, sq_a = out_norm(
-        "enc_out_norm", enc_limit, o_enc, enc_input, gain[0], w["enc_attn_out"], **at(1, 9.0)
+        "enc_out_norm", enc_limit, o_enc, enc_input, gain[0], w.enc_attn_out, **at(1, 9.0)
     )
     enc_out, unit2, dev2, slope_e, wa_e, ads_e, sq_b = branch(
-        "enc_branch", enc_limit, unit1, gain[0], gain[1], w["enc_ffn_in"], w["enc_ffn_out"],
+        "enc_branch", enc_limit, unit1, gain[0], gain[1], w.enc_ffn_in, w.enc_ffn_out,
         enc_down, enc_up, **at(2, 33.0),
     )
-    sqkv = project("dec_project", dec_limit, dec_input, w["dec_self_qkv"], 3, **at(3, 6.0))
+    sqkv = project("dec_project", dec_limit, dec_input, w.dec_self_qkv, 3, **at(3, 6.0))
     e_self, o_self, inv_self = attend(
         "dec_attend", dec_limit, (sqkv, 0), (sqkv, 8), (sqkv, 16), True, **at(1, 8.5)
     )
     unit3, dev3, sq_c, cross_q = out_norm(
-        "dec_out_norm", dec_limit, o_self, dec_input, gain[2], w["dec_self_out"], w["dec_cross_q"],
+        "dec_out_norm", dec_limit, o_self, dec_input, gain[2], w.dec_self_out, w.dec_cross_q,
         **at(1, 5.3),
     )
-    kv = project("cross_project", enc_limit, enc_out, w["dec_cross_kv"], 2, **at(2, 9.5))
+    kv = project("cross_project", enc_limit, enc_out, w.dec_cross_kv, 2, **at(2, 9.5))
     e_cross, o_cross, inv_cross = attend(
         "cross_attend", enc_limit, (cross_q, 0), (kv, 0), (kv, 8), False, **at(1, 14.0)
     )
     if hosting:
         value = recorder.run()
-        w = {name: value(mat) for name, mat in w.items()}
+        w = types.SimpleNamespace(**{name: value(mat) for name, mat in vars(w).items()})
         enc_q, enc_k, enc_v, e_enc, o_enc, inv_enc = map(value, (enc_q, enc_k, enc_v, e_enc, o_enc, inv_enc))
         unit1, dev1, sq_a = map(value, (unit1, dev1, sq_a))
         enc_out, unit2, dev2, slope_e, wa_e, ads_e, sq_b = map(
@@ -1313,15 +1317,15 @@
         kv, e_cross, o_cross, inv_cross = map(value, (kv, e_cross, o_cross, inv_cross))
         recorder = Recorder("encoder_grad", 2, {}, fsdp)
     unit4, dev4, sq_d = out_norm(
-        "cross_out_norm", dec_limit, o_cross, unit3, gain[3], w["dec_cross_out"], residual_gain=gain[2]
+        "cross_out_norm", dec_limit, o_cross, unit3, gain[3], w.dec_cross_out, residual_gain=gain[2]
     )
     dec_out, unit5, dev5, slope_d, wa_d, ads_d, sq_e = branch(
-        "dec_branch", dec_limit, unit4, gain[3], gain[4], w["dec_ffn_in"], w["dec_ffn_out"],
+        "dec_branch", dec_limit, unit4, gain[3], gain[4], w.dec_ffn_in, w.dec_ffn_out,
         dec_down, dec_up,
     )
     grad_cross, do_cross, *dec_grads = dec_branch_grad(
         "dec_branch_grad", (enc_limit, dec_limit), dec_cot, (unit5, dev5), gain[4], (unit4, dev4), gain[3],
-        slope_d, wa_d, ads_d, w["dec_ffn_out"], w["dec_ffn_in"], w["dec_cross_out"], dec_down, dec_up,
+        slope_d, wa_d, ads_d, w.dec_ffn_out, w.dec_ffn_in, w.dec_cross_out, dec_down, dec_up,
         (sq_a, sq_b, sq_c, sq_d, sq_e),
     )
     dcq, dck, dcv = attend_grad(
@@ -1332,12 +1336,12 @@
         recorder.load("dec", dec_grads)
         enc_sums = recorder.reduce("enc", False)
     dz, part, *enc_grads = enc_adapter_grad(
-        "enc_adapter_grad", enc_limit, enc_cot, (dck, dcv), w["dec_cross_kv"], (unit2, dev2), gain[1],
+        "enc_adapter_grad", enc_limit, enc_cot, (dck, dcv), w.dec_cross_kv, (unit2, dev2), gain[1],
         (unit1, dev1), gain[0], wa_e, ads_e, enc_down, enc_up, **at(1, 20.0, "enc"),
     )
     grad_one, do_enc = enc_hidden_grad(
         "enc_hidden_grad", enc_limit, dz, part, slope_e, (unit1, dev1), gain[0],
-        w["enc_ffn_out"], w["enc_ffn_in"], w["enc_attn_out"], **at(2, 28.0),
+        w.enc_ffn_out, w.enc_ffn_in, w.enc_attn_out, **at(2, 28.0),
     )
     deq, dek, dev = attend_grad(
         "enc_attend_grad", (enc_q, 0), (enc_k, 0), (enc_v, 0), e_enc, o_enc, inv_enc, do_enc, **at(1, 37.0)
@@ -1353,17 +1357,17 @@
         dec_grads, tally = [down, up[: dec_up.shape[0]]], up[dec_up.shape[0] :]
         enc_grads = lax.psum(enc_grads, everyone)
     grad_self, do_self = middle_grad(
-        "dec_middle_grad", dec_limit, grad_cross, dcq, (unit3, dev3), gain[2], w["dec_cross_q"],
-        w["dec_self_out"],
+        "dec_middle_grad", dec_limit, grad_cross, dcq, (unit3, dev3), gain[2], w.dec_cross_q,
+        w.dec_self_out,
     )
     dsq, dsk, dsv = attend_grad(
         "dec_attend_grad", (sqkv, 0), (sqkv, 8), (sqkv, 16), e_self, o_self, inv_self, do_self
     )
     dec_grad, *dec_grads = input_grad(
-        "dec_input_grad", dec_limit, grad_self, [dsq, dsk, dsv], w["dec_self_qkv"], dec_grads
+        "dec_input_grad", dec_limit, grad_self, [dsq, dsk, dsv], w.dec_self_qkv, dec_grads
     )
     enc_grad, *enc_grads, rms = input_grad(
-        "enc_input_grad", enc_limit, grad_one, [deq, dek, dev], w["enc_qkv"], enc_grads, tally
+        "enc_input_grad", enc_limit, grad_one, [deq, dek, dev], w.enc_qkv, enc_grads, tally
     )
     return enc_out, dec_out, enc_grad, dec_grad, *enc_grads, *dec_grads, rms[:7, 0]
 

time: 431 us -> 431 us (level)
  no operation moved by 1% of the time
where the time goes in v6:
time: 431 us; the launch traced here: 423 us
  Pallas kernels  417 us (97%)
    pallas_call x2, Pallas kernels, run(): pl.pallas_call(kernel, in_specs=[ANY] * len(self.owns) + [spec for _, spe...  336 us
    pallas_call x8, Pallas kernels, launch(): pl.pallas_call(kernel, grid=grid, in_specs=[spec for _, spec in ins], out...  81 us

profile of v6, /device:TPU:0, one launch (start us, length us, event | category | flops | bytes accessed | tf_op | source)
XLA Modules:
  0.0 423.2 jit_solution(17502035135477919441)
XLA Ops:
  1.9 1.6 fusion
  3.5 232.1 %forward.1 = (bf16[1024,3072]{1,0:T(8,128)(2,1)}, bf16[1024,1024]{1,0:T(8,128)(2,1)}, bf16[1024,4096]{1,0:T(8,128)(2,1)}, bf16[4096,1024]{1,0:T(8,128)(2,1)}, bf...) custom-call(bf16[128,3072]{1,0:T(8,128)(2,1)} %refs_0_.8, ...), custom_call_target="tpu_custom_call" | custom-call | tf_op jit(solution)/shard_map/forward/pallas_call | solution.py:523
  235.6 4.6 %cross_out_norm.1 = (bf16[256,1024]{1,0:T(8,128)(2,1)}, f32[256,128]{1,0:T(8,128)}, f32[8,1024]{1,0:T(8,128)}) custom-call(s32[1]{0:T(128)S(6)} %copy.33.refs_17_.refs_0_.refs_4_, bf16[1024,1024]{1,0:T(8,128)(2,1)} %get-tuple-element.89.refs_1_.refs_3_, bf16[256,1024]{1,0:T(8,128)(2,1)} %get-tuple-element.90.refs_2_.refs_4_, ...), custom_call_target="tpu_custom_call" | custom-call | flops 536870912 | bytes 3842048 | tf_op jit(solution)/shard_map/cross_out_norm/pallas_call | solution.py:595
  240.2 12.1 %dec_branch.1 = (bf16[256,1024]{1,0:T(8,128)(2,1)}, bf16[256,1024]{1,0:T(8,128)(2,1)}, f32[256,128]{1,0:T(8,128)}, bf16[256,4096]{1,0:T(8,128)(2,1)}, bf16[256,5...) custom-call(s32[1]{0:T(128)S(6)} %copy.33.refs_17_.refs_0_.refs_4_, ...), custom_call_target="tpu_custom_call" | custom-call | flops 4831838208 | bytes 25337856 | tf_op jit(solution)/shard_map/dec_branch/pallas_call | solution.py:595
  252.3 14.8 %dec_branch_grad.1 = (f32[256,1024]{1,0:T(8,128)}, bf16[256,1024]{1,0:T(8,128)(2,1)}, f32[1024,512]{1,0:T(8,128)}, f32[520,1024]{1,0:T(8,128)}) custom-call(s32[1]{0:T(128)S(6)} %copy.32.refs_11_.refs_0_, bf16[4096,1024]{1,0:T(8,128)(2,1)} %get-tuple-element.88.refs_2_.refs_1_, bf16[1024,4096]{1,0:T(8,128)(2,1)} %get-tuple-element.87.refs_1_.refs_2_, ...), custom_call_target="tpu_custom_call" | custom-call | flops 5368709120 | bytes 33497092 | tf_op jit(solution)/shard_map/dec_branch_grad/pallas_call | solution.py:595
  267.2 13.0 %cross_attend_grad.1 = (bf16[256,1024]{1,0:T(8,128)(2,1)}, bf16[1024,1024]{1,0:T(8,128)(2,1)}, bf16[1024,1024]{1,0:T(8,128)(2,1)}) custom-call(bf16[256,1024]{1,0:T(8,128)(2,1)} %get-tuple-element.96.refs_0_, bf16[1024,2048]{1,0:T(8,128)(2,1)} %get-tuple-element.97.refs_1_.refs_2_, bf16[1024,2048]{1,0:T(8,128)(2,1)} %get-tuple-element.97.refs_1_.refs_2_, ...), custom_call_target="tpu_custom_call" | custom-call | flops 8589934592 | bytes 8388608 | tf_op jit(solution)/shard_map/cross_attend_grad/pallas_call | solution.py:595
  280.2 5.7 %dec_middle_grad.1 = (f32[256,1024]{1,0:T(8,128)}, bf16[256,1024]{1,0:T(8,128)(2,1)}) custom-call(s32[1]{0:T(128)S(6)} %copy.33.refs_17_.refs_0_.refs_4_, bf16[1024,1024]{1,0:T(8,128)(2,1)} %get-tuple-element.141.refs_1_, bf16[1024,1024]{1,0:T(8,128)(2,1)} %get-tuple-element.142.refs_2_, f32[256,1024]{1,0:T(8,128)} %get-tuple-element.143.refs_3_, ...), custom_call_target="tpu_custom_call" | custom-call | flops 1073741824 | bytes 7999488 | tf_op jit(solution)/shard_map/dec_middle_grad/pallas_call | solution.py:595
  285.9 8.0 %dec_attend_grad.1 = (bf16[256,1024]{1,0:T(8,128)(2,1)}, bf16[256,1024]{1,0:T(8,128)(2,1)}, bf16[256,1024]{1,0:T(8,128)(2,1)}) custom-call(bf16[256,3072]{1,0:T(8,128)(2,1)} %get-tuple-element.147.refs_0_.refs_1_.refs_2_, bf16[256,3072]{1,0:T(8,128)(2,1)} %get-tuple-element.147.refs_0_.refs_1_.refs_2_, ...), custom_call_target="tpu_custom_call" | custom-call | flops 2147483648 | bytes 2097152 | tf_op jit(solution)/shard_map/dec_attend_grad/pallas_call | solution.py:595
  293.9 103.7 %encoder_grad.1 = (bf16[1024,1024]{1,0:T(8,128)(2,1)}, f32[1024,1024]{1,0:T(8,128)}, f32[1024,1024]{1,0:T(8,128)}, bf16[1024,1024]{1,0:T(8,128)(2,1)}, bf16[1024...) custom-call(s32[1]{0:T(128)S(6)} %copy.32.refs_11_.refs_0_, ...), custom_call_target="tpu_custom_call" | custom-call | tf_op jit(solution)/shard_map/encoder_grad/pallas_call | solution.py:523
  397.6 8.4 %dec_input_grad.1 = (f32[256,1024]{1,0:T(8,128)}, f32[1024,512]{1,0:T(8,128)}, f32[512,1024]{1,0:T(8,128)}) custom-call(s32[1]{0:T(128)S(6)} %copy.33.refs_17_.refs_0_.refs_4_, bf16[1024,3072]{1,0:T(8,128)(2,1)} %get-tuple-element.140.refs_1_, f32[256,1024]{1,0:T(8,128)} %get-tuple-element.146.refs_2_, bf16[256,1024]{1,0:T(8,128)(2,1)} %get-tuple-element.152.refs_3_, ...), custom_call_target="tpu_custom_call" | custom-call | flops 1610612736 | bytes 16252928 | tf_op jit(solution)/shard_map/dec_input_grad/pallas_call | solution.py:595
  406.0 0.0 copy-start
  406.1 14.4 %enc_input_grad.1 = (f32[1024,1024]{1,0:T(8,128)}, f32[1024,512]{1,0:T(8,128)}, f32[512,1024]{1,0:T(8,128)}, f32[8,128]{1,0:T(8,128)}) custom-call(s32[1]{0:T(128)S(6)} %copy.32.refs_11_.refs_0_, bf16[1024,3072]{1,0:T(8,128)(2,1)} %get-tuple-element.94.refs_1_, f32[1024,1024]{1,0:T(8,128)} %get-tuple-element.132.refs_2_, ...), custom_call_target="tpu_custom_call" | custom-call | flops 6442450944 | bytes 27299840 | tf_op jit(solution)/shard_map/enc_input_grad/pallas_call | solution.py:595
  420.4 1.3 slice_reduce_fusion
  421.7 0.0 copy-done
  421.7 1.3 copy.34
Async XLA Ops:
  406.0 15.7 %copy-start = (bf16[1024,1024]{1,0:T(8,128)(2,1)S(1)}, bf16[1024,1024]{1,0:T(8,128)(2,1)}, u32[]{:S(2)}) copy-start(bf16[1024,1024]{1,0:T(8,128)(2,1)} %get-tuple-element.177) | copy-start | bytes 6291460
